TPU v7x, 128 devices: a whole 4x4x4 slice. The times are simulated.
128 devices in a mesh: row: 16 (over z_hi, y, core), col: 8 (over x, z_lo).
Axes of the slice: x: 4, y: 4, z: 4 (z_hi: 2, z_lo: 2; z = z_hi * 2 + z_lo), core: 2. Of those that a mesh axis runs over, the one named last changes fastest.
Arguments:
- traces: bfloat16 [65536, 8192], P(('row', 'col')), may hold values from -60 to 60
- seg_owner: int32 [65536, 1], P(('row', 'col')), may hold values from 0 to 127; in each aligned block of 512 rows (0 to 511, 512 to 1023, ...) at most 16 rows name the same one
- seg_slot: int32 [65536], P(('row', 'col')), may hold values from 0 to 767
- white_width: int32 [1024], replicated, may hold values from 1 to 8
- band_bins: int32 [256], replicated, may hold values from 513 to 1023, as said below
Outputs:
- cross_spectra: bfloat16 [1024, 1024, 512], P('row', 'col')
Inputs may be any that keep to these rules, and one draw needn't show every extreme that they name: `seg_owner`: among the 512 segments held by one device, no owner is named more than 16 times, a bound that some block reaches. `band_bins`: strictly increasing.
All inputs are finite; a program needn't handle non-finite values.
Results may differ from a plain program's by a relative error of at most 0.008.
Values may be sent and summed in bfloat16 or wider, within the bound.
No kernel may reach another device: no remote copies, remote signals or barrier semaphores. Data moves between devices by JAX's collectives and lax.ppermute only.
A program may use at most 192 MiB of HBM per device.

v0:
```python
import math

import jax
import jax.numpy as jnp
from jax import lax
from jax.sharding import PartitionSpec as P

L = 8192
NBAND = 256
HALF = 64
WMAX = 8
ST_DEV = 8
HOURS = 96


EPS = 1e-05
FLOOR = 0.5


def dft_table(band_bins, length):
    times = lax.broadcasted_iota(jnp.int32, (length, band_bins.shape[0]), 0)
    phase = times * band_bins[None, :] % length
    angle = phase.astype(jnp.float32) * (2.0 * math.pi / length)
    return jnp.concatenate([jnp.cos(angle), -jnp.sin(angle)], axis=1).astype(jnp.bfloat16)


def normalize(segments, half):
    values = segments.astype(jnp.float32)
    length = values.shape[1]
    running = jnp.cumsum(jnp.abs(values), axis=1)
    running = jnp.concatenate([jnp.zeros((values.shape[0], 1), jnp.float32), running], axis=1)
    upper = jnp.pad(running[:, half + 1 :], ((0, 0), (0, half)), mode="edge")
    lower = jnp.pad(running[:, : length - half], ((0, 0), (half, 0)))
    places = lax.broadcasted_iota(jnp.int32, (1, length), 1)
    counts = jnp.minimum(places + half, length - 1) - jnp.maximum(places - half, 0) + 1
    means = (upper - lower) / counts.astype(jnp.float32)
    return (values / (means + EPS)).astype(jnp.bfloat16)


def whiten(spectrum, widths, wmax):
    nband = spectrum.shape[1] // 2
    real_part = spectrum[:, :nband]
    imag_part = spectrum[:, nband:]
    amplitude = jnp.sqrt(real_part * real_part + imag_part * imag_part)
    padded_amp = jnp.pad(amplitude, ((0, 0), (wmax, wmax)))
    padded_one = jnp.pad(jnp.ones_like(amplitude), ((0, 0), (wmax, wmax)))
    total = amplitude
    number = jnp.ones_like(amplitude)
    chosen = jnp.zeros_like(amplitude)
    for width in range(1, wmax + 1):
        total = (
            total
            + padded_amp[:, wmax - width : wmax - width + nband]
            + padded_amp[:, wmax + width : wmax + width + nband]
        )
        number = (
            number
            + padded_one[:, wmax - width : wmax - width + nband]
            + padded_one[:, wmax + width : wmax + width + nband]
        )
        chosen = jnp.where(widths[:, None] == width, total / number, chosen)
    factor = 1.0 / jnp.maximum(chosen, FLOOR)
    return (spectrum * jnp.concatenate([factor, factor], axis=1)).astype(jnp.bfloat16)


def lookup(stations, table_values):
    hits = stations[:, None] == lax.broadcasted_iota(jnp.int32, (1, table_values.shape[0]), 1)
    return jnp.sum(jnp.where(hits, table_values[None, :], 0), axis=1)


def transform(segments, widths, table):
    normalized = normalize(segments, HALF)
    spectrum = jnp.dot(normalized, table, preferred_element_type=jnp.float32) * (1.0 / math.sqrt(L))
    return whiten(spectrum, widths, WMAX)


def transform_rows(segments, widths, table):
    number = segments.shape[0]
    group = math.gcd(number, 128)
    shaped = (
        segments.reshape(number // group, group, segments.shape[1]),
        widths.reshape(number // group, group),
    )
    result = lax.map(lambda pair: transform(pair[0], pair[1], table), shaped)
    return result.reshape(number, 2 * NBAND)


def on_device(traces, seg_owner, seg_slot, white_width, band_bins):
    devices = lax.axis_size(("row", "col"))
    held = traces.shape[0]
    capacity = 4 * held // devices
    table = dft_table(band_bins, L)
    owners = seg_owner[:, 0]
    owner_hits = (owners[:, None] == lax.broadcasted_iota(jnp.int32, (1, devices), 1)).astype(
        jnp.int32
    )
    position = jnp.sum((jnp.cumsum(owner_hits, axis=0) - owner_hits) * owner_hits, axis=1)
    target = owners * capacity + position
    slot_hits = target[None, :] == lax.broadcasted_iota(jnp.int32, (devices * capacity, 1), 0)
    source = jnp.sum(jnp.where(slot_hits, lax.broadcasted_iota(jnp.int32, (1, held), 1), 0), axis=1)
    filled = jnp.any(slot_hits, axis=1)
    send_slots = jnp.where(filled, jnp.take(seg_slot, source, axis=0), -1).reshape(
        devices, capacity
    )
    stations = owners * ST_DEV + seg_slot // HOURS
    widths = lookup(stations, white_width)
    local = transform_rows(traces, widths, table)
    send_spec = jnp.where(
        filled[:, None], jnp.take(local, source, axis=0), jnp.zeros((), jnp.bfloat16)
    )
    send_spec = send_spec.reshape(devices, capacity, 2 * NBAND)
    spectra, slots = (
        lax.all_to_all(send_spec, ("row", "col"), split_axis=0, concat_axis=0, tiled=True),
        lax.all_to_all(send_slots, ("row", "col"), split_axis=0, concat_axis=0, tiled=True),
    )
    flat_slots = slots.reshape(-1)
    flat_spec = spectra.reshape(flat_slots.shape[0], 2 * NBAND)
    picks = (lax.broadcasted_iota(jnp.int32, (ST_DEV * HOURS, 1), 0) == flat_slots[None, :]).astype(
        jnp.bfloat16
    )
    station_spec = jnp.dot(picks, flat_spec, preferred_element_type=jnp.float32).astype(
        jnp.bfloat16
    )
    station_spec = station_spec.reshape(ST_DEV, HOURS, 2 * NBAND)
    row_spec = lax.all_gather(station_spec, "col", axis=0, tiled=True)
    left_real = jnp.concatenate([row_spec[..., :NBAND], row_spec[..., NBAND:]], axis=1)
    left_imag = jnp.concatenate([row_spec[..., NBAND:], -row_spec[..., :NBAND]], axis=1)
    piece = lax.all_gather(station_spec, "row", axis=0, tiled=True)
    right_both = jnp.concatenate([piece[..., :NBAND], piece[..., NBAND:]], axis=1)
    real_out = jnp.einsum("akf,bkf->abf", left_real, right_both, preferred_element_type=jnp.float32)
    imag_out = jnp.einsum("akf,bkf->abf", left_imag, right_both, preferred_element_type=jnp.float32)
    return jnp.concatenate([real_out, imag_out], axis=2).astype(jnp.bfloat16)


def solution(mesh):
    return jax.shard_map(
        on_device,
        mesh=mesh,
        in_specs=(P(("row", "col"), None), P(("row", "col"), None), P(("row", "col")), P(), P()),
        out_specs=P("row", "col", None),
        check_vma=False,
    )
```

profile of v0, /device:TPU:1, one launch (start us, length us, event | category | flops | bytes accessed | tf_op | source)
XLA Modules:
  0.0 580.5 jit_solution(3112042157202501232)
XLA Ops:
  6.5 0.8 copy.31
  7.7 0.9 fusion.91
  8.6 0.7 multiply_add_fusion
  10.4 13.2 %gather_fusion = s32[2048]{0:T(1024)S(1)} fusion(s32[512]{0:T(512)S(1)} %copy-done, s32[2048]{0:T(1024)S(1)} %broadcast_clamp_fusion), kind=kCustom, calls=%fused_computation | custom fusion | bytes 24576 | tf_op jit(solution)/shard_map/jit(_take)/gather | solution.py:102
  23.8 0.7 select_select_fusion.1
  24.5 12.0 %all-to-all-start = ((s32[128,1,16]{2,1,0:T(1,128)}), s32[128,1,16]{2,1,0:T(1,128)}, u32[]{:S(2)}, u32[]{:S(2)}) async-start(s32[128,1,16]{2,1,0:T(1,128)} %bitcast.21), calls=%async_computation | async-start | bytes 131072 | tf_op jit(solution)/shard_map/all_to_all | solution.py:114
  36.5 0.7 broadcast_in_dim.168
  37.2 0.6 compare_and_fusion
  37.9 35.0 %cosine_convert_fusion = (bf16[8192,256]{1,0:T(8,128)(2,1)}, bf16[8192,256]{1,0:T(8,128)(2,1)}) fusion(s32[256]{0:T(256)S(1)} %copy-done.6), kind=kLoop, calls=%fused_computation.139 | loop fusion | flops 35651584 | bytes 8389632 | tf_op jit(solution)/shard_map/convert.5
  73.3 7.5 %pad_maximum_fusion.1 = bf16[8192,512]{1,0:T(8,128)(2,1)} fusion(bf16[8192,256]{1,0:T(8,128)(2,1)} %get-tuple-element.116, bf16[8192,256]{1,0:T(8,128)(2,1)} %get-tuple-element.115), kind=kLoop, calls=%fused_computation.128 | loop fusion | flops 16777216 | bytes 16777216 | tf_op jit(solution)/shard_map/concatenate | solution.py:24
  80.8 108.1 %while.12 = (s32[]{:T(128)}, bf16[4,128,512]{2,1,0:T(8,128)(2,1)S(1)}, bf16[4,128,8192]{2,1,0:T(8,128)(2,1)}, bf16[8192,512]{1,0:T(8,128)(2,1)}, s32[4,128]{1,0:T(4,128)S(1)}, /*index=5*/s32[]{:T(128)}, f32[]{:T(128)}, f32[]{:T(128)}) while((s32[]{:T(128)}, bf16[4,128,512]{2,1,0:T(8,128)(2,1)S(1)}, bf16[4,128,8192]{2,1,0:T(8,128)(2,1)}, ...), condition=%wide.region_9.10_spmd, body=%wide.region_6.9_spmd.sunk | while | flops 1219978112 | bytes 94181000 | solution.py:84
  80.8 3.1 constant_dynamic-slice_fusion.4
  84.0 3.2 copy.48
  87.5 2.4 fusion.115
  90.0 1.9 copy-done.1
  92.0 2.6 broadcast_add_fusion.3
  94.6 2.4 copy.49
  97.1 0.6 pad_slice_fusion.34
  97.6 8.7 %fusion.117 = f32[128,512]{1,0:T(8,128)S(1)} fusion(bf16[8192,512]{1,0:T(8,128)(2,1)} %get-tuple-element.189, bf16[1,128,8192]{1,2,0:T(8,128)(2,1)S(1)} %copy.48, f32[128,64]{0,1:T(8,128)S(1)} %reshape.320, f32[128,8128]{0,1:T(8,128)S(1)} %get-tuple-element.159, f32[128,8128]{0,1:T(8,128)S(1)} %get-tuple-element.160, f32[8192]{0:T(1024)S(1)} %fusion.116), kind=kOutput, calls=%fused_computation.30.clone.1 | convolution fusion | flops 1081147392 | bytes 19136512 | tf_op jit(solution)/shard_map/while/body/eval_jaxpr/dot_general | solution.py:73
  106.5 1.3 fusion.119
  107.9 3.1 constant_dynamic-slice_fusion.4
  111.0 3.2 copy.48
  114.5 2.4 fusion.115
  117.0 1.9 copy-done.1
  119.0 2.6 broadcast_add_fusion.3
  121.6 2.4 copy.49
  124.1 0.6 pad_slice_fusion.34
  124.7 8.8 %fusion.117 = f32[128,512]{1,0:T(8,128)S(1)} fusion(bf16[8192,512]{1,0:T(8,128)(2,1)} %get-tuple-element.189, bf16[1,128,8192]{1,2,0:T(8,128)(2,1)S(1)} %copy.48, f32[128,64]{0,1:T(8,128)S(1)} %reshape.320, f32[128,8128]{0,1:T(8,128)S(1)} %get-tuple-element.159, f32[128,8128]{0,1:T(8,128)S(1)} %get-tuple-element.160, f32[8192]{0:T(1024)S(1)} %fusion.116), kind=kOutput, calls=%fused_computation.30.clone.1 | convolution fusion | flops 1081147392 | bytes 19136512 | tf_op jit(solution)/shard_map/while/body/eval_jaxpr/dot_general | solution.py:73
  133.5 1.3 fusion.119
  134.9 3.1 constant_dynamic-slice_fusion.4
  138.0 3.2 copy.48
  141.6 2.4 fusion.115
  144.0 1.9 copy-done.1
  146.0 2.6 broadcast_add_fusion.3
  148.7 2.4 copy.49
  151.7 8.8 %fusion.117 = f32[128,512]{1,0:T(8,128)S(1)} fusion(bf16[8192,512]{1,0:T(8,128)(2,1)} %get-tuple-element.189, bf16[1,128,8192]{1,2,0:T(8,128)(2,1)S(1)} %copy.48, f32[128,64]{0,1:T(8,128)S(1)} %reshape.320, f32[128,8128]{0,1:T(8,128)S(1)} %get-tuple-element.159, f32[128,8128]{0,1:T(8,128)S(1)} %get-tuple-element.160, f32[8192]{0:T(1024)S(1)} %fusion.116), kind=kOutput, calls=%fused_computation.30.clone.1 | convolution fusion | flops 1081147392 | bytes 19136512 | tf_op jit(solution)/shard_map/while/body/eval_jaxpr/dot_general | solution.py:73
  160.5 1.3 fusion.119
  161.9 3.1 constant_dynamic-slice_fusion.4
  165.1 3.2 copy.48
  168.6 2.4 fusion.115
  171.0 1.9 copy-done.1
  173.1 2.6 broadcast_add_fusion.3
  175.7 2.4 copy.49
  178.7 8.8 %fusion.117 = f32[128,512]{1,0:T(8,128)S(1)} fusion(bf16[8192,512]{1,0:T(8,128)(2,1)} %get-tuple-element.189, bf16[1,128,8192]{1,2,0:T(8,128)(2,1)S(1)} %copy.48, f32[128,64]{0,1:T(8,128)S(1)} %reshape.320, f32[128,8128]{0,1:T(8,128)S(1)} %get-tuple-element.159, f32[128,8128]{0,1:T(8,128)S(1)} %get-tuple-element.160, f32[8192]{0:T(1024)S(1)} %fusion.116), kind=kOutput, calls=%fused_computation.30.clone.1 | convolution fusion | flops 1081147392 | bytes 19136512 | tf_op jit(solution)/shard_map/while/body/eval_jaxpr/dot_general | solution.py:73
  187.6 1.3 fusion.119
  188.9 7.5 %gather_fusion.1 = bf16[2048,512]{1,0:T(8,128)(2,1)S(1)} fusion(bf16[512,512]{1,0:T(8,128)(2,1)S(1)} %bitcast.85, s32[2048]{0:T(1024)S(1)} %broadcast_clamp_fusion), kind=kCustom, calls=%fused_computation.1 | custom fusion | bytes 4202496 | tf_op jit(solution)/shard_map/jit(_take)/gather | solution.py:109
  196.5 2.3 select_select_fusion
  198.7 9.8 %all-to-all-start.1 = ((bf16[128,16,512]{2,1,0:T(8,128)(2,1)}), bf16[128,16,512]{2,1,0:T(8,128)(2,1)S(1)}, u32[]{:S(2)}, u32[]{:S(2)}) async-start(bf16[128,16,512]{2,1,0:T(8,128)(2,1)} %select_select_fusion), calls=%async_computation.1 | async-start | bytes 4194304 | tf_op jit(solution)/shard_map/all_to_all | solution.py:113
  208.8 0.6 broadcast.360
  209.4 1.6 reduce.3
  211.1 26.1 %all-to-all-done.1 = bf16[128,16,512]{2,1,0:T(8,128)(2,1)S(1)} async-done(((bf16[128,16,512]{2,1,0:T(8,128)(2,1)}), bf16[128,16,512]{2,1,0:T(8,128)(2,1)S(1)}, u32[]{:S(2)}, u32[]{:S(2)}) %all-to-all-start.1) | async-done | bytes 2097184 | tf_op jit(solution)/shard_map/all_to_all | solution.py:113
  237.2 1.8 fusion.89
  239.0 1.4 copy.37
  240.6 0.7 all-gather.3.cloned.1.call-update
  241.2 165.6 %all-gather.5.cloned.1.call-done = bf16[64,96,512]{1,0,2:T(8,128)(2,1)} async-done(((bf16[8,96,512]{1,0,2:T(8,128)(2,1)}), bf16[64,96,512]{1,0,2:T(8,128)(2,1)}) %all-gather.5.cloned.1.call-update) | async-done | bytes 6291472 | tf_op jit(solution)/shard_map/all_gather | solution.py:125
  406.8 7.2 %fusion.100 = (bf16[64,96,256]{1,0,2:T(8,128)(2,1)}, bf16[64,96,256]{1,0,2:T(8,128)(2,1)}, bf16[64,96,256]{1,0,2:T(8,128)(2,1)}) fusion(bf16[64,96,512]{1,0,2:T(8,128)(2,1)} %all-gather.5.cloned.1.call-done), kind=kLoop, calls=%fused_computation.181 | loop fusion | flops 1572864 | bytes 15728640 | tf_op jit(solution)/shard_map/slice | solution.py:126
  414.0 89.3 %all-gather.3.cloned.1.call-done = bf16[128,96,512]{2,1,0:T(8,128)(2,1)} async-done(((bf16[8,96,512]{2,1,0:T(8,128)(2,1)}), bf16[128,96,512]{2,1,0:T(8,128)(2,1)}) %all-gather.3.cloned.1.call-update) | async-done | bytes 12582928 | tf_op jit(solution)/shard_map/all_gather | solution.py:128
  503.4 10.6 %fusion.99 = (bf16[128,96,256]{2,1,0:T(8,128)(2,1)}, bf16[128,96,256]{2,1,0:T(8,128)(2,1)}) fusion(bf16[128,96,512]{2,1,0:T(8,128)(2,1)} %all-gather.3.cloned.1.call-done), kind=kLoop, calls=%fused_computation.180 | loop fusion | bytes 25165824 | tf_op jit(solution)/shard_map/slice | solution.py:129
  513.9 9.6 %copy.40 = bf16[128,96,256]{0,1,2:T(8,128)(2,1)} copy(bf16[128,96,256]{2,1,0:T(8,128)(2,1)} %get-tuple-element.108) | data formatting | bytes 12582912
  523.5 9.7 %copy.41 = bf16[128,96,256]{0,1,2:T(8,128)(2,1)} copy(bf16[128,96,256]{2,1,0:T(8,128)(2,1)} %get-tuple-element.109) | data formatting | bytes 12582912
  533.3 10.9 %convert_bitcast_fusion.2 = bf16[64,128,256]{1,0,2:T(8,128)(2,1)} fusion(bf16[128,96,256]{0,1,2:T(8,128)(2,1)} %copy.41, bf16[128,96,256]{0,1,2:T(8,128)(2,1)} %copy.40, bf16[64,96,256]{1,0,2:T(8,128)(2,1)} %get-tuple-element.112, bf16[64,96,256]{1,0,2:T(8,128)(2,1)} %get-tuple-element.110), kind=kOutput, calls=%fused_computation.146 | convolution fusion | flops 845152256 | bytes 23068672 | tf_op jit(solution)/shard_map/akf,bkf->abf/dot_general | solution.py:130
  544.2 9.3 %convert_bitcast_fusion.1 = bf16[64,128,256]{1,0,2:T(8,128)(2,1)} fusion(bf16[128,96,256]{0,1,2:T(8,128)(2,1)} %copy.41, bf16[128,96,256]{0,1,2:T(8,128)(2,1)S(1)} %bitcast.90, bf16[64,96,256]{1,0,2:T(8,128)(2,1)} %get-tuple-element.111, bf16[64,96,256]{1,0,2:T(8,128)(2,1)} %get-tuple-element.112), kind=kOutput, calls=%fused_computation.145 | convolution fusion | flops 845152256 | bytes 23068672 | tf_op jit(solution)/shard_map/akf,bkf->abf/dot_general | solution.py:131
  553.4 7.4 %pad_maximum_fusion.2 = bf16[64,128,512]{1,0,2:T(8,128)(2,1)} fusion(bf16[64,128,256]{1,0,2:T(8,128)(2,1)} %convert_bitcast_fusion.1, bf16[64,128,256]{1,0,2:T(8,128)(2,1)} %convert_bitcast_fusion.2), kind=kLoop, calls=%fused_computation.137 | loop fusion | flops 4194304 | bytes 16777216 | tf_op jit(solution)/shard_map/concatenate | solution.py:132
  560.9 12.8 %copy.38 = bf16[64,128,512]{2,1,0:T(8,128)(2,1)} copy(bf16[64,128,512]{1,0,2:T(8,128)(2,1)} %pad_maximum_fusion.2) | data formatting | bytes 16777216 | tf_op jit(solution)/shard_map/concatenate | solution.py:132
  (93 shorter events, 5.8 us)
Async XLA Ops:
  6.5 3.9 copy-start
  10.4 27.4 %copy-start.6 = (s32[256]{0:T(256)S(1)}, s32[256]{0:T(256)}, u32[]{:S(2)}) copy-start(s32[256]{0:T(256)} %param.11) | copy-start | bytes 3076
  24.5 174.3 %all-to-all-start = ((s32[128,1,16]{2,1,0:T(1,128)}), s32[128,1,16]{2,1,0:T(1,128)}, u32[]{:S(2)}, u32[]{:S(2)}) async-start(s32[128,1,16]{2,1,0:T(1,128)} %bitcast.21), calls=%async_computation | async-start | bytes 131072 | tf_op jit(solution)/shard_map/all_to_all | solution.py:114
  37.9 35.0 %copy-start.5 = (s32[1024]{0:T(1024)S(1)}, s32[1024]{0:T(1024)}, u32[]{:S(2)}) copy-start(s32[1024]{0:T(1024)} %param.10) | copy-start | bytes 12292
  89.9 1.9 copy-start.1
  117.0 1.9 copy-start.1
  144.0 1.9 copy-start.1
  171.0 1.9 copy-start.1
  188.9 7.6 %copy-start.3 = (pred[128,16]{1,0:T(8,128)(4,1)S(1)}, pred[128,16]{1,0:T(8,128)(4,1)}, u32[]{:S(2)}) copy-start(pred[128,16]{1,0:T(8,128)(4,1)} %compare_and_fusion) | copy-start | bytes 6148
  188.9 7.6 %copy-start.4 = (pred[128,16]{1,0:T(8,128)(4,1)S(1)}, pred[128,16]{1,0:T(8,128)(4,1)}, u32[]{:S(2)}) copy-start(pred[128,16]{1,0:T(8,128)(4,1)} %broadcast_in_dim.168) | copy-start | bytes 6148
  198.7 38.5 %all-to-all-start.1 = ((bf16[128,16,512]{2,1,0:T(8,128)(2,1)}), bf16[128,16,512]{2,1,0:T(8,128)(2,1)S(1)}, u32[]{:S(2)}, u32[]{:S(2)}) async-start(bf16[128,16,512]{2,1,0:T(8,128)(2,1)} %select_select_fusion), calls=%async_computation.1 | async-start | bytes 4194304 | tf_op jit(solution)/shard_map/all_to_all | solution.py:113
  208.5 198.3 %all-gather.5.cloned.1.call-start = ((), (), s32[]{:S(2)}) async-start(), calls=%async_computation.3 | async-start | bytes 9437184 | tf_op jit(solution)/shard_map/all_gather | solution.py:125
  239.0 1.5 copy-start.2
  240.5 262.9 %all-gather.3.cloned.1.call-start = ((), (), s32[]{:S(2)}) async-start(), calls=%async_computation.2 | async-start | bytes 13369344 | tf_op jit(solution)/shard_map/all_gather | solution.py:128
  523.5 20.6 %slice-start = ((s8[6291456]{0:T(1024)(128)(4,1)}), s8[2097152]{0:T(1024)(128)(4,1)S(1)}, s32[]{:S(2)}) async-start(s8[6291456]{0:T(1024)(128)(4,1)} %bitcast.89), calls=%async_computation.4 | async-start | bytes 4194304
  533.3 10.9 %slice-start.1 = ((s8[6291456]{0:T(1024)(128)(4,1)}), s8[4194304]{0:T(1024)(128)(4,1)S(1)}, s32[]{:S(2)}) async-start(s8[6291456]{0:T(1024)(128)(4,1)} %bitcast.89), calls=%async_computation.5 | async-start | bytes 8388608
Sparse Core Ops, SparseCore 0:
  240.6 166.1 all-gather.4
  409.3 94.0 all-gather.2
where the time goes:
time: 582 us; the launch traced here: 581 us
  waiting for transfers between devices  282 us (48%)
  local copies, waits for them, and re-layouts  113 us (19%)
  other arithmetic  93.1 us (16%)
  matrix products  56.9 us (10%)
  starting transfers between devices  22 us (4%)
  between operations  13.6 us (2%)
    all_gather x1, waiting for transfers between devices, on_device(): row_spec = lax.all_gather(station_spec, 'col', axis=0, tiled=True)  166 us
    all_gather x1, waiting for transfers between devices, on_device(): piece = lax.all_gather(station_spec, 'row', axis=0, tiled=True)  89.3 us
    another operation x16, other arithmetic  55.9 us
    dot_general x4, matrix products, transform(): jnp.dot(normalized, table, preferred_element_type=jnp.float32)  35 us
    all_to_all x1, waiting for transfers between devices, on_device(): lax.all_to_all(send_spec, ('row', 'col'), split_axis=0, concat_axis=0, ti...  26.1 us
    dynamic_slice x8, local copies, waits for them, and re-layouts, transform_rows(): result = lax.map(lambda pair: transform(pair[0], pair[1], table), shaped)  25.3 us
    unnamed x19, local copies, waits for them, and re-layouts  19.4 us
    gather x2, local copies, waits for them, and re-layouts, on_device(): jnp.take(seg_slot, source, axis=0)  13.3 us
  transfers between devices with their start and end apart: 4, of which 3 were waited for; matrix products, arithmetic and copies ran while one was open for 28% of the time, Pallas kernels for 0%

commit v1 on v0

v1 whole, which is shorter than its diff:
```python
import functools
import math

import jax
import jax.numpy as jnp
from jax import lax
from jax.experimental import pallas as pl
from jax.experimental.pallas import tpu as pltpu
from jax.sharding import Mesh, PartitionSpec as P

L = 8192
NBAND = 256
HALF = 64
WMAX = 8
ST_DEV = 8
HOURS = 96
CAP = 16
EPS = 1e-05
FLOOR = 0.5

AXES = ("zh", "y", "core", "x", "zl")
DEVICES = 128
SEGS = 512
STEP = 1024
STEPS = L // STEP
ROWS = 80
PAIRS = 64
WIDE = 4 * HOURS
F32 = jnp.float32
BF16 = jnp.bfloat16


def iota(shape, axis):
    return lax.broadcasted_iota(jnp.int32, shape, axis)


def transform_kernel(
    main, before, after, owner_col, owner_row, slot_col, width_row, bins,
    send, low_cos, low_sin, high_cos, high_sin, band, magnitude, normal, table, total,
):
    step = pl.program_id(0)

    @pl.when(step == 0)
    def _():
        unit = 2.0 * math.pi / L
        phase = (iota((128, NBAND), 0) * bins[...]) & (L - 1)
        angle = phase.astype(F32) * unit
        low_cos[...] = jnp.cos(angle)
        low_sin[...] = jnp.sin(angle)
        phase = (iota((64, NBAND), 0) * 128 * bins[...]) & (L - 1)
        angle = phase.astype(F32) * unit
        high_cos[...] = jnp.cos(angle)
        high_sin[...] = jnp.sin(angle)
        offset = iota((512, 256), 0) - 128 - iota((512, 256), 1)
        band[...] = jnp.where(jnp.abs(offset) <= HALF, 1.0, 0.0).astype(BF16)
        total[...] = jnp.zeros_like(total)

    for part in range(STEP // 128):
        high = step * (STEP // 128) + part
        cos_high = high_cos[pl.ds(high, 1), :]
        sin_high = high_sin[pl.ds(high, 1), :]
        rows = slice(part * 128, part * 128 + 128)
        table[rows, :NBAND] = (cos_high * low_cos[...] - sin_high * low_sin[...]).astype(BF16)
        table[rows, NBAND:] = (-(sin_high * low_cos[...] + cos_high * low_sin[...])).astype(BF16)

    magnitude[:, 128 : 128 + STEP] = jnp.abs(main[...])
    magnitude[:, :128] = jnp.where(step > 0, jnp.abs(before[...]), jnp.zeros((), BF16))
    magnitude[:, 128 + STEP :] = jnp.where(
        step < STEPS - 1, jnp.abs(after[...]), jnp.zeros((), BF16)
    )
    for part in range(STEP // 256):
        sums = jnp.dot(
            magnitude[:, part * 256 : part * 256 + 512], band[...], preferred_element_type=F32
        )
        place = step * STEP + part * 256 + iota((1, 256), 1)
        count = jnp.minimum(place + HALF, L - 1) - jnp.maximum(place - HALF, 0) + 1
        count = count.astype(F32)
        below = sums + count * EPS
        inverse = pl.reciprocal(below, approx=True)
        inverse = inverse * (2.0 - below * inverse)
        values = main[:, part * 256 : part * 256 + 256].astype(F32)
        normal[:, part * 256 : part * 256 + 256] = (values * (count * inverse)).astype(BF16)
    total[...] += jnp.dot(normal[...], table[...], preferred_element_type=F32)

    @pl.when(step == STEPS - 1)
    def _():
        slots = slot_col[...]
        station = jnp.zeros_like(slots)
        for edge in range(1, ST_DEV):
            station += (slots >= edge * HOURS).astype(jnp.int32)
        hour = slots - station * HOURS
        whole = owner_col[...] * ST_DEV + station
        hits = whole == iota((1, DEVICES * ST_DEV), 1)
        widths = jnp.sum(jnp.where(hits, width_row[...], 0).astype(F32), axis=1, keepdims=True)
        widths = widths.astype(jnp.int32)
        real = total[:, :NBAND] * (1.0 / math.sqrt(L))
        imag = total[:, NBAND:] * (1.0 / math.sqrt(L))
        amplitude = jnp.sqrt(real * real + imag * imag)
        lane = iota((1, NBAND), 1)
        smooth = amplitude
        for width in range(1, WMAX + 1):
            up = pltpu.roll(amplitude, width, 1)
            down = pltpu.roll(amplitude, NBAND - width, 1)
            both = jnp.where(lane >= width, up, 0.0) + jnp.where(lane < NBAND - width, down, 0.0)
            smooth += jnp.where(widths >= width, both, 0.0)
        number = jnp.minimum(lane + widths, NBAND - 1) - jnp.maximum(lane - widths, 0) + 1
        factor = 1.0 / jnp.maximum(smooth / number.astype(F32), FLOOR)
        lanes = iota((SEGS, 128), 1)
        extra = jnp.where(
            lanes == 0, station, jnp.where(lanes == 1, hour, jnp.where(lanes == 2, 1, 0))
        )
        whitened = jnp.concatenate(
            [
                (real * factor).astype(BF16),
                (imag * factor).astype(BF16),
                extra.astype(F32).astype(BF16),
            ],
            axis=1,
        )
        same = (owner_col[...] == owner_row[...]) & (iota((SEGS, SEGS), 0) < iota((SEGS, SEGS), 1))
        rank = jnp.sum(same.astype(F32), axis=0, keepdims=True).astype(jnp.int32)
        target = owner_row[...] * CAP + rank
        for part in range(4):
            chosen = target == iota((512, SEGS), 0) + part * 512
            chosen = jnp.where(chosen, 1.0, 0.0).astype(BF16)
            picked = jnp.dot(chosen, whitened, preferred_element_type=F32).astype(BF16)
            for tile in range(5):
                send[part * 32 : part * 32 + 32, tile * CAP : tile * CAP + CAP, :] = picked[
                    :, tile * 128 : tile * 128 + 128
                ].reshape(32, CAP, 128)


def transform(traces, seg_owner, seg_slot, white_width, band_bins):
    return pl.pallas_call(
        transform_kernel,
        grid=(STEPS,),
        in_specs=[
            pl.BlockSpec((SEGS, STEP), lambda k: (0, k)),
            pl.BlockSpec((SEGS, 128), lambda k: (0, jnp.maximum(k * (STEP // 128) - 1, 0))),
            pl.BlockSpec(
                (SEGS, 128), lambda k: (0, jnp.minimum((k + 1) * (STEP // 128), L // 128 - 1))
            ),
            pl.BlockSpec((SEGS, 1), lambda k: (0, 0)),
            pl.BlockSpec((1, SEGS), lambda k: (0, 0)),
            pl.BlockSpec((SEGS, 1), lambda k: (0, 0)),
            pl.BlockSpec((1, DEVICES * ST_DEV), lambda k: (0, 0)),
            pl.BlockSpec((1, NBAND), lambda k: (0, 0)),
        ],
        out_specs=pl.BlockSpec((DEVICES, ROWS, 128), lambda k: (0, 0, 0)),
        out_shape=jax.ShapeDtypeStruct((DEVICES, ROWS, 128), BF16),
        scratch_shapes=[
            pltpu.VMEM((128, NBAND), F32),
            pltpu.VMEM((128, NBAND), F32),
            pltpu.VMEM((64, NBAND), F32),
            pltpu.VMEM((64, NBAND), F32),
            pltpu.VMEM((512, 256), BF16),
            pltpu.VMEM((SEGS, STEP + 256), BF16),
            pltpu.VMEM((SEGS, STEP), BF16),
            pltpu.VMEM((STEP, 2 * NBAND), BF16),
            pltpu.VMEM((SEGS, 2 * NBAND), F32),
        ],
        compiler_params=pltpu.CompilerParams(vmem_limit_bytes=48 << 20),
        cost_estimate=pl.CostEstimate(
            flops=10 * SEGS * L * 512, bytes_accessed=SEGS * L * 2, transcendentals=SEGS * L
        ),
        name="transform",
    )(
        traces, traces, traces, seg_owner, seg_owner.reshape(1, SEGS), seg_slot.reshape(SEGS, 1),
        white_width.reshape(1, -1), band_bins.reshape(1, -1),
    )


def stack_kernel(half, received, spectra, wide):
    tags = received[:, 4 * CAP : 5 * CAP, :].reshape(DEVICES * CAP, 128).astype(F32)
    column = (tags[:, 0:1] * 128.0 + tags[:, 1:2] + (tags[:, 2:3] - 1.0)).astype(jnp.int32)
    total = jnp.zeros((256, ST_DEV * 128), F32)
    block = 512
    for part in range(DEVICES * CAP // block):
        sources = slice(part * block // CAP, (part + 1) * block // CAP)
        hits = column[part * block : (part + 1) * block] == iota((1, ST_DEV * 128), 1)
        hits = jnp.where(hits, 1.0, 0.0).astype(BF16)
        real = received[sources, half * CAP : half * CAP + CAP, :].reshape(block, 128)
        imag = received[sources, (2 + half) * CAP : (3 + half) * CAP, :].reshape(block, 128)
        both = jnp.concatenate([real, imag], axis=1)
        total += lax.dot_general(both, hits, (((0,), (0,)), ((), ())), preferred_element_type=F32)
    lane = iota((PAIRS, 128), 1)
    for station in range(ST_DEV):
        lanes = slice(station * 128, station * 128 + 128)
        real_first = total[0:64, lanes]
        real_second = pltpu.roll(total[64:128, lanes], 64, 1)
        imag_first = pltpu.roll(total[128:192, lanes], 96, 1)
        imag_second = pltpu.roll(total[192:256, lanes], 32, 1)
        wide[:, station, 0:128] = jnp.where(lane < 96, real_first, imag_first)
        wide[:, station, 128:256] = jnp.where(lane < 64, imag_first, real_second)
        wide[:, station, 256:384] = jnp.where(lane < 32, real_second, imag_second)
    spectra[...] = wide[...].reshape(PAIRS * ST_DEV, WIDE).astype(BF16)


def stack_half(received, half):
    return pl.pallas_call(
        functools.partial(stack_kernel, half),
        out_shape=jax.ShapeDtypeStruct((PAIRS * ST_DEV, WIDE), BF16),
        scratch_shapes=[pltpu.VMEM((PAIRS, ST_DEV, WIDE), F32)],
        compiler_params=pltpu.CompilerParams(vmem_limit_bytes=40 << 20),
        cost_estimate=pl.CostEstimate(
            flops=2 * 2048 * 1024 * 256 * 2, bytes_accessed=3 << 20, transcendentals=0
        ),
        name="stack",
    )(received)


BLOCK = 16
BLOCKS = PAIRS // BLOCK
OUT_ROWS = 16


def cross_kernel(places, *refs):
    (row_own, row_left, row_right, row_first, row_second) = refs[0:5]
    columns = refs[5:15]
    out, left, right, swapped, swap, results = refs[-6:]
    step = pl.program_id(0)

    def place(source, target, count, base):
        for block in range(2):
            at = pl.multiple_of(places[base + block] * ST_DEV, ST_DEV)
            target[:, pl.ds(at, ST_DEV), :] = (
                source[block].astype(F32).reshape(BLOCK, ST_DEV, WIDE)
            )

    @pl.when(step == 0)
    def _():
        source = iota((WIDE, WIDE), 0)
        target = iota((WIDE, WIDE), 1)
        group = (target // HOURS) % 2
        ahead = (source == target + HOURS) & (group == 0)
        behind = (source == target - HOURS) & (group == 1)
        swap[...] = (jnp.where(ahead, 1.0, 0.0) - jnp.where(behind, 1.0, 0.0)).astype(BF16)

    @pl.when(step < BLOCKS)
    def _():
        place(row_own, left, 8, 0)
        place(row_left, left, 8, 2)
        place(row_right, left, 8, 4)
        for core in range(2):
            own, one, other = columns[core * 5 : core * 5 + 3]
            place(own, right, 16, 8 + core * 8)
            place(one, right, 16, 10 + core * 8)
            place(other, right, 16, 12 + core * 8)

    @pl.when(step < BLOCKS // 2)
    def _():
        place(row_first, left, 8, 6)
        place(columns[3], right, 16, 14)
        place(columns[8], right, 16, 22)

    @pl.when((step >= BLOCKS // 2) & (step < BLOCKS))
    def _():
        place(row_second, left, 8, 6)
        place(columns[4], right, 16, 14)
        place(columns[9], right, 16, 22)

    @pl.when(step < BLOCKS)
    def _():
        plain = left[...].astype(BF16).reshape(BLOCK * 64, WIDE)
        swapped[...] = (
            jnp.dot(plain, swap[...], preferred_element_type=F32)
            .astype(BF16)
            .reshape(BLOCK, 64, WIDE)
        )
        lane = iota((1, 256), 1)
        first_mask = jnp.where(lane < 2 * HOURS, 1.0, 0.0).astype(BF16)
        second_mask = jnp.where(lane >= 2 * HOURS - 128, 1.0, 0.0).astype(BF16)

        @pl.loop(0, BLOCK)
        def _(pair):
            for part, mask in ((0, first_mask), (1, second_mask)):
                lanes = slice(part * 128, part * 128 + 256)
                rows = jnp.concatenate(
                    [left[pair, :, lanes].astype(BF16), swapped[pair, :, lanes]], axis=0
                )
                product = lax.dot_general(
                    rows * mask,
                    right[pair, :, lanes].astype(BF16),
                    (((1,), (1,)), ((), ())),
                    preferred_element_type=F32,
                )
                at = step * BLOCK + pair + part * PAIRS
                results[pl.ds(at, 128, stride=128), :] = product

    @pl.when(step >= BLOCKS)
    def _():
        first = (step - BLOCKS) * OUT_ROWS
        for row in range(OUT_ROWS):
            at = pl.multiple_of((first + row) * 128, 128)
            out[row] = results[pl.ds(at, 128), :].T.astype(BF16)


def cross_half(places, rows, columns, half, earlier):
    def whole(step):
        return (0, jnp.minimum(step, BLOCKS - 1), 0)

    def first(step):
        return (0, jnp.minimum(step, BLOCKS // 2 - 1), 0)

    def second(step):
        return (0, jnp.clip(step - BLOCKS // 2, 0, BLOCKS // 2 - 1), 0)

    shape = (2, BLOCK * ST_DEV, WIDE)
    group = [pl.BlockSpec(shape, f) for f in (whole, whole, whole, first, second)]
    per_part = 64 // OUT_ROWS

    def out_map(step):
        at = jnp.maximum(step - BLOCKS, 0)
        return (at % per_part, 0, half + 2 * (at // per_part))

    arrays = [places] + list(rows) + list(columns)
    in_specs = [pl.BlockSpec(memory_space=pltpu.SMEM)] + group * 3
    aliases = {}
    if earlier is not None:
        aliases = {len(arrays): 0}
        arrays.append(earlier)
        in_specs.append(pl.BlockSpec(memory_space=pl.ANY))
    return pl.pallas_call(
        cross_kernel,
        grid=(BLOCKS + 2 * per_part,),
        in_specs=in_specs,
        out_specs=pl.BlockSpec((OUT_ROWS, 128, 128), out_map),
        out_shape=jax.ShapeDtypeStruct((64, 128, 2 * NBAND), BF16),
        scratch_shapes=[
            pltpu.VMEM((BLOCK, 64, WIDE), F32),
            pltpu.VMEM((BLOCK, 128, WIDE), F32),
            pltpu.VMEM((BLOCK, 64, WIDE), BF16),
            pltpu.VMEM((WIDE, WIDE), BF16),
            pltpu.VMEM((128 * 128, 128), F32),
        ],
        input_output_aliases=aliases,
        compiler_params=pltpu.CompilerParams(vmem_limit_bytes=50 << 20),
        cost_estimate=pl.CostEstimate(
            flops=2 * 128 * 128 * 256 * 128 * 3, bytes_accessed=14 << 20, transcendentals=0
        ),
        name="cross",
    )(*arrays)


def ring(size, shift):
    return [(i, (i + shift) % size) for i in range(size)]


def swap_with(array, axis):
    return lax.ppermute(array, axis, [(0, 1), (1, 0)])


def spread(pair, axis):
    left = lax.ppermute(pair, axis, ring(4, 1))
    right = lax.ppermute(pair, axis, ring(4, 3))
    middle = pair.shape[1] // 2
    first = lax.ppermute(left[:, :middle], axis, ring(4, 1))
    second = lax.ppermute(right[:, middle:], axis, ring(4, 3))
    return [pair, left, right, first, second]


def block_places():
    zh, y, core, x, zl = (lax.axis_index(name) for name in AXES)
    out = []
    for shift in (0, 3, 1, 2):
        there = (x + shift) % 4
        out += [there * 2 + zl, there * 2 + (1 - zl)]
    for own in (core, 1 - core):
        for shift in (0, 3, 1, 2):
            there = (y + shift) % 4
            out += [zh * 8 + there * 2 + own, (1 - zh) * 8 + there * 2 + own]
    return jnp.stack(out).astype(jnp.int32)


def on_device(traces, seg_owner, seg_slot, white_width, band_bins):
    send = transform(traces, seg_owner, seg_slot, white_width, band_bins)
    received = lax.all_to_all(send, AXES, split_axis=0, concat_axis=0, tiled=True)
    places = block_places()
    out = None
    for half in range(2):
        own = stack_half(received, half)
        rows = spread(jnp.stack([own, swap_with(own, "zl")]), "x")
        columns = spread(jnp.stack([own, swap_with(own, "zh")]), "y")
        columns = columns + [swap_with(array, "core") for array in columns]
        out = cross_half(places, rows, columns, half, out)
    return out


def solution(mesh):
    fine = Mesh(mesh.devices.reshape(2, 4, 2, 4, 2), AXES)
    return jax.shard_map(
        on_device,
        mesh=fine,
        in_specs=(P(AXES, None), P(AXES, None), P(AXES), P(), P()),
        out_specs=P(("zh", "y", "core"), ("x", "zl"), None),
        check_vma=False,
    )
```

time: 582 us -> 239 us (0.41)
  waiting for transfers between devices: 282 us -> 42 us
  local copies, waits for them, and re-layouts: 113 us -> 16.5 us
  other arithmetic: 93.1 us -> 0.3 us
  Pallas kernels: 0 us -> 84.5 us
  matrix products: 56.9 us -> 0 us
  blocking collectives: 0 us -> 45.8 us
  starting transfers between devices: 22 us -> 49.1 us
  between operations: 13.6 us -> 0.58 us
    all_gather x2 -> x0, waiting for transfers between devices: 255 us -> none  [the longest x1 166 us: on_device(): row_spec = lax.all_gather(station_spec, 'col', axis=0, tiled=True)]
    pallas_call x0 -> x5, Pallas kernels: none -> 84.5 us  [the longest x2 59.5 us: cross_half(): pl.pallas_call(cross_kernel, grid=(BLOCKS + 2 * per_part,), in_specs=in_s...]
    dot_general x7 -> x0, matrix products: 56.9 us -> none  [the longest x4 35 us: transform(): jnp.dot(normalized, table, preferred_element_type=jnp.float32)]
    another operation x16 -> x2, other arithmetic: 55.9 us -> 0.3 us  [on_device(): columns = spread(jnp.stack([own, swap_with(own, 'zh')]), 'y')]
    ppermute x0 -> x30, starting transfers between devices: none -> 49.1 us  [the longest x14 20.9 us: swap_with(): return lax.ppermute(array, axis, [(0, 1), (1, 0)])]
    all_to_all x0 -> x1, blocking collectives: none -> 45.8 us  [on_device(): lax.all_to_all(send, AXES, split_axis=0, concat_axis=0, tiled=True)]
    ppermute x0 -> x30, waiting for transfers between devices: none -> 42 us  [the longest x14 14.6 us: swap_with(): return lax.ppermute(array, axis, [(0, 1), (1, 0)])]
    all_to_all x2 -> x0, waiting for transfers between devices: 26.1 us -> none  [the longest x1 26.1 us: on_device(): lax.all_to_all(send_spec, ('row', 'col'), split_axis=0, concat_axis=0, ti...]
  transfers between devices with their start and end apart: 4 -> 30, of which waited for: 3 -> 13; matrix products, arithmetic and copies ran while one was open for 28% -> 1% of each run, Pallas kernels for 0% -> 13%
where the time goes in v1:
time: 239 us
  Pallas kernels  84.5 us (35%)
  starting transfers between devices  49.1 us (21%)
  blocking collectives  45.8 us (19%)
  waiting for transfers between devices  42 us (18%)
  local copies, waits for them, and re-layouts  16.5 us (7%)
    pallas_call x2, Pallas kernels, cross_half(): pl.pallas_call(cross_kernel, grid=(BLOCKS + 2 * per_part,), in_specs=in_s...  59.5 us
    all_to_all x1, blocking collectives, on_device(): lax.all_to_all(send, AXES, split_axis=0, concat_axis=0, tiled=True)  45.8 us
    ppermute x14, starting transfers between devices, swap_with(): return lax.ppermute(array, axis, [(0, 1), (1, 0)])  20.9 us
    pallas_call x1, Pallas kernels, transform(): pl.pallas_call(transform_kernel, grid=(STEPS,), in_specs=[pl.BlockSpec((S...  20.2 us
    ppermute x4, starting transfers between devices, spread(): right = lax.ppermute(pair, axis, ring(4, 3))  15.4 us
    ppermute x14, waiting for transfers between devices, swap_with(): return lax.ppermute(array, axis, [(0, 1), (1, 0)])  14.6 us
    unnamed x51, local copies, waits for them, and re-layouts  12.5 us
    ppermute x4, waiting for transfers between devices, spread(): left = lax.ppermute(pair, axis, ring(4, 1))  12.3 us
  transfers between devices with their start and end apart: 30, of which 13 were waited for; matrix products, arithmetic and copies ran while one was open for 1% of the time, Pallas kernels for 13%

profile of v1, /device:TPU:1, one launch (start us, length us, event | category | flops | bytes accessed | tf_op | source)
XLA Modules:
  0.0 238.7 jit_solution(16577938324971590285)
XLA Ops:
  0.0 0.8 copy.9.slot_col
  0.8 0.8 copy.8.owner_col
  1.7 0.0 copy-start.12
  1.7 0.7 copy-done.12
  2.4 0.7 copy-done.13
  3.0 0.7 copy-done.14
  3.7 20.2 %transform.1 = bf16[128,80,128]{2,1,0:T(8,128)(2,1)S(1)} custom-call(bf16[512,8192]{1,0:T(8,128)(2,1)} %after.1, bf16[512,8192]{1,0:T(8,128)(2,1)} %after.1, bf16[512,8192]{1,0:T(8,128)(2,1)} %after.1, s32[512,1]{1,0:T(8,128)S(1)} %copy.8.owner_col, s32[1,512]{1,0:T(1,128)S(1)} %bitcast.36, s32[512,1]{1,0:T(8,128)S(1)} %copy.9.slot_col, ...), custom_call_target="tpu_custom_call" | custom-call | flops 21474836480 | bytes 8388608 | tf_op jit(solution)/shard_map/transform/pallas_call | solution.py:134
  23.9 45.8 %all_to_all.5.received = bf16[128,80,128]{2,1,0:T(8,128)(2,1)S(1)} all-to-all(bf16[128,80,128]{2,1,0:T(8,128)(2,1)S(1)} %transform.1), channel_id=1, replica_groups=mesh['zh'=2,'y'=4,'core'=2,'x'=4,'zl'=2] {'zh','y','core','x','zl'}, dimensions={0} | all-to-all | bytes 5242880 | tf_op jit(solution)/shard_map/all_to_all | solution.py:377
  69.7 2.4 %stack.145 = bf16[512,384]{1,0:T(8,128)(2,1)S(1)} custom-call(bf16[128,80,128]{2,1,0:T(8,128)(2,1)S(1)} %all_to_all.5.received), custom_call_target="tpu_custom_call" | custom-call | flops 2147483648 | bytes 3145728 | tf_op jit(solution)/shard_map/stack/pallas_call | solution.py:200
  72.1 0.3 collective-permute-start.20
  72.4 0.8 collective-permute-start.15
  73.2 2.4 %stack.144 = bf16[512,384]{1,0:T(8,128)(2,1)S(1)} custom-call(bf16[128,80,128]{2,1,0:T(8,128)(2,1)S(1)} %all_to_all.5.received), custom_call_target="tpu_custom_call" | custom-call | flops 2147483648 | bytes 3145728 | tf_op jit(solution)/shard_map/stack/pallas_call | solution.py:200
  75.6 3.2 %collective-permute-start.5 = (bf16[512,384]{1,0:T(8,128)(2,1)S(1)}, bf16[512,384]{1,0:T(8,128)(2,1)S(1)}, u32[]{:S(2)}, u32[]{:S(2)}) collective-permute-start(bf16[512,384]{1,0:T(8,128)(2,1)S(1)} %stack.144), channel_id=1, source_target_pairs={{0,64},{64,0},{1,65},{65,1},{2,66},{66,2},{3,67},{67,3},{4,68},{68... | collective-permute-start | bytes 1179656 | tf_op jit(solution)/shard_map/ppermute | solution.py:350
  78.8 3.3 %collective-permute-done.20 = bf16[512,384]{1,0:T(8,128)(2,1)S(1)} collective-permute-done((bf16[512,384]{1,0:T(8,128)(2,1)S(1)}, bf16[512,384]{1,0:T(8,128)(2,1)S(1)}, u32[]{:S(2)}, u32[]{:S(2)}) %collective-permute-start.20) | collective-permute-done | bytes 393248 | tf_op jit(solution)/shard_map/ppermute | solution.py:350
  82.1 6.4 %collective-permute-done.15 = bf16[512,384]{1,0:T(8,128)(2,1)S(1)} collective-permute-done((bf16[512,384]{1,0:T(8,128)(2,1)S(1)}, bf16[512,384]{1,0:T(8,128)(2,1)S(1)}, u32[]{:S(2)}, u32[]{:S(2)}) %collective-permute-start.15) | collective-permute-done | bytes 393248 | tf_op jit(solution)/shard_map/ppermute | solution.py:350
  88.5 0.1 pad_maximum_fusion.2
  88.7 4.9 %collective-permute-start.17 = (bf16[2,512,384]{2,1,0:T(8,128)(2,1)S(1)}, bf16[2,512,384]{2,1,0:T(8,128)(2,1)S(1)}, u32[]{:S(2)}, u32[]{:S(2)}) collective-permute-start(bf16[2,512,384]{2,1,0:T(8,128)(2,1)S(1)} %get-tuple-element.6.refs_0_), channel_id=1, source_target_pairs={{0,6},{2,0},{4,2},{6,4},{1,7},{3,1},{5,3},{7,5},{8,14},{10,8},{12,... | collective-permute-start | bytes 2359304 | tf_op jit(solution)/shard_map/ppermute | solution.py:355
  93.6 3.2 %collective-permute-start.25 = (bf16[2,512,384]{2,1,0:T(8,128)(2,1)S(1)}, bf16[2,512,384]{2,1,0:T(8,128)(2,1)S(1)}, u32[]{:S(2)}, u32[]{:S(2)}) collective-permute-start(bf16[2,512,384]{2,1,0:T(8,128)(2,1)S(1)} %get-tuple-element.5.refs_5_), channel_id=1, source_target_pairs={{0,8},{8,0},{1,9},{9,1},{2,10},{10,2},{3,11},{11,3},{4,12},{12,4},... | collective-permute-start | bytes 2359304 | tf_op jit(solution)/shard_map/ppermute | solution.py:350
  96.8 2.2 collective-permute-done.5
  99.0 3.7 %collective-permute-start.22 = (bf16[2,512,384]{2,1,0:T(8,128)(2,1)S(1)}, bf16[2,512,384]{2,1,0:T(8,128)(2,1)S(1)}, u32[]{:S(2)}, u32[]{:S(2)}) collective-permute-start(bf16[2,512,384]{2,1,0:T(8,128)(2,1)S(1)} %get-tuple-element.5.refs_5_), channel_id=1, source_target_pairs={{0,48},{16,0},{32,16},{48,32},{1,49},{17,1},{33,17},{49,33},{2,50}... | collective-permute-start | bytes 2359304 | tf_op jit(solution)/shard_map/ppermute | solution.py:355
  102.7 2.7 %collective-permute-done = bf16[512,384]{1,0:T(8,128)(2,1)S(1)} collective-permute-done((bf16[512,384]{1,0:T(8,128)(2,1)S(1)}, bf16[512,384]{1,0:T(8,128)(2,1)S(1)}, u32[]{:S(2)}, u32[]{:S(2)}) %collective-permute-start) | collective-permute-done | bytes 393248 | tf_op jit(solution)/shard_map/ppermute | solution.py:350
  105.4 2.1 collective-permute-start.21
  107.5 0.1 pad_maximum_fusion
  107.6 1.7 collective-permute-done.17.refs_2_
  109.3 3.4 %collective-permute-start.2 = (bf16[2,512,384]{2,1,0:T(8,128)(2,1)S(1)}, bf16[2,512,384]{2,1,0:T(8,128)(2,1)S(1)}, u32[]{:S(2)}, u32[]{:S(2)}) collective-permute-start(bf16[2,512,384]{2,1,0:T(8,128)(2,1)S(1)} %get-tuple-element.8.refs_0_), channel_id=1, source_target_pairs={{0,6},{2,0},{4,2},{6,4},{1,7},{3,1},{5,3},{7,5},{8,14},{10,8},{12,... | collective-permute-start | bytes 2359304 | tf_op jit(solution)/shard_map/ppermute | solution.py:355
  112.8 2.4 collective-permute-start.10
  115.1 2.1 collective-permute-done.22.refs_7_
  117.2 3.4 %collective-permute-start.7 = (bf16[2,512,384]{2,1,0:T(8,128)(2,1)S(1)}, bf16[2,512,384]{2,1,0:T(8,128)(2,1)}, u32[]{:S(2)}, u32[]{:S(2)}) collective-permute-start(bf16[2,512,384]{2,1,0:T(8,128)(2,1)S(1)} %get-tuple-element.7.refs_5_), channel_id=1, source_target_pairs={{0,48},{16,0},{32,16},{48,32},{1,49},{17,1},{33,17},{49,33},{2,50}... | collective-permute-start | bytes 2359304 | tf_op jit(solution)/shard_map/ppermute | solution.py:355
  120.6 4.2 %collective-permute-done.21.refs_6_ = bf16[2,512,384]{2,1,0:T(8,128)(2,1)S(1)} collective-permute-done((bf16[2,512,384]{2,1,0:T(8,128)(2,1)S(1)}, bf16[2,512,384]{2,1,0:T(8,128)(2,1)S(1)}, u32[]{:S(2)}, u32[]{:S(2)}) %collective-permute-start.21) | collective-permute-done | bytes 786464 | tf_op jit(solution)/shard_map/ppermute | solution.py:354
  125.0 2.6 %collective-permute-done.2.refs_2_ = bf16[2,512,384]{2,1,0:T(8,128)(2,1)S(1)} collective-permute-done((bf16[2,512,384]{2,1,0:T(8,128)(2,1)S(1)}, bf16[2,512,384]{2,1,0:T(8,128)(2,1)S(1)}, u32[]{:S(2)}, u32[]{:S(2)}) %collective-permute-start.2) | collective-permute-done | bytes 786464 | tf_op jit(solution)/shard_map/ppermute | solution.py:355
  127.6 3.4 %collective-permute-start.19 = (bf16[2,256,384]{2,1,0:T(8,128)(2,1)S(1)}, bf16[2,256,384]{2,1,0:T(8,128)(2,1)S(1)}, u32[]{:S(2)}, u32[]{:S(2)}) collective-permute-start(bf16[2,256,384]{2,1,0:T(8,128)(2,1)S(1)} %slice.37), channel_id=1, source_target_pairs={{0,6},{2,0},{4,2},{6,4},{1,7},{3,1},{5,3},{7,5},{8,14},{10,8},{12,... | collective-permute-start | bytes 1179656 | tf_op jit(solution)/shard_map/ppermute | solution.py:358
  131.0 1.8 collective-permute-start.24
  132.8 1.4 collective-permute-done.7.refs_7_
  134.2 8.0 %collective-permute-done.6.refs_6_ = bf16[2,512,384]{2,1,0:T(8,128)(2,1)} collective-permute-done((bf16[2,512,384]{2,1,0:T(8,128)(2,1)S(1)}, bf16[2,512,384]{2,1,0:T(8,128)(2,1)}, u32[]{:S(2)}, u32[]{:S(2)}) %collective-permute-start.6) | collective-permute-done | bytes 786464 | tf_op jit(solution)/shard_map/ppermute | solution.py:354
  142.2 7.3 %collective-permute-start.27 = (bf16[2,512,384]{2,1,0:T(8,128)(2,1)S(1)}, bf16[2,512,384]{2,1,0:T(8,128)(2,1)S(1)}, u32[]{:S(2)}, u32[]{:S(2)}) collective-permute-start(bf16[2,512,384]{2,1,0:T(8,128)(2,1)S(1)} %collective-permute-done.22.refs_7_), channel_id=1, source_target_pairs={{0,8},{8,0},{1,9},{9,1},{2,10},{10,2},{3,11},{11,3},{4,12},{12,4},... | collective-permute-start | bytes 2359304 | tf_op jit(solution)/shard_map/ppermute | solution.py:350
  149.6 1.0 slice.35
  150.6 1.0 slice.34
  151.7 3.7 %collective-permute-start.4 = (bf16[2,256,384]{2,1,0:T(8,128)(2,1)S(1)}, bf16[2,256,384]{2,1,0:T(8,128)(2,1)S(1)}, u32[]{:S(2)}, u32[]{:S(2)}) collective-permute-start(bf16[2,256,384]{2,1,0:T(8,128)(2,1)S(1)} %slice.33), channel_id=1, source_target_pairs={{0,6},{2,0},{4,2},{6,4},{1,7},{3,1},{5,3},{7,5},{8,14},{10,8},{12,... | collective-permute-start | bytes 1179656 | tf_op jit(solution)/shard_map/ppermute | solution.py:358
  155.4 0.7 copy-done
  156.1 0.3 collective-permute-start.26
  156.4 1.7 collective-permute-start.8
  158.2 5.8 %collective-permute-done.4.refs_4_ = bf16[2,256,384]{2,1,0:T(8,128)(2,1)S(1)} collective-permute-done((bf16[2,256,384]{2,1,0:T(8,128)(2,1)S(1)}, bf16[2,256,384]{2,1,0:T(8,128)(2,1)S(1)}, u32[]{:S(2)}, u32[]{:S(2)}) %collective-permute-start.4) | collective-permute-done | bytes 393248 | tf_op jit(solution)/shard_map/ppermute | solution.py:358
  163.9 0.7 copy-done.2
  164.7 0.8 collective-permute-start.12
  165.4 1.2 collective-permute-done.9.refs_9_
  166.7 1.1 collective-permute-start.11
  167.8 0.5 collective-permute-done.8.refs_8_
  168.2 1.0 collective-permute-start.29
  169.3 0.8 copy-done.4
  170.0 0.0 collective-permute-start.28
  170.1 0.8 copy-done.6
  170.8 0.8 slice.32
  171.7 0.8 copy-done.8
  172.4 0.5 collective-permute-start.14
  172.9 0.7 copy-done.10
  173.7 0.0 collective-permute-start.13
  173.9 0.1 stack.133.places
  174.0 1.0 copy-done.1
  175.0 1.0 copy-done.5
  176.0 1.0 copy-done.7
  177.0 1.0 copy-done.9
  178.0 1.0 copy-done.11
  179.0 29.6 %cross.2.refs_15_ = bf16[64,128,512]{2,1,0:T(8,128)(2,1)} custom-call(s32[24]{0:T(128)S(1)} %stack.133.places, bf16[2,512,384]{2,1,0:T(8,128)(2,1)S(1)} %get-tuple-element.6.refs_0_, bf16[2,512,384]{2,1,0:T(8,128)(2,1)S(1)} %collective-permute-done.16.refs_1_, bf16[2,512,384]{2,1,0:T(8,128)(2,1)} %copy-done.17, bf16[2,256,384]{2,1,0:T(8,128)(2,1)S(1)} %copy-done.1, ...), custom_call_target="tpu_custom_call" | custom-call | flops 3221225472 | bytes 14680064 | tf_op jit(solution)/shard_map/cross/pallas_call | solution.py:323
  208.6 30.0 %cross.3 = bf16[64,128,512]{2,1,0:T(8,128)(2,1)} custom-call(s32[24]{0:T(128)S(1)} %stack.133.places, bf16[2,512,384]{2,1,0:T(8,128)(2,1)S(1)} %get-tuple-element.8.refs_0_, bf16[2,512,384]{2,1,0:T(8,128)(2,1)S(1)} %collective-permute-done.1.refs_1_, bf16[2,512,384]{2,1,0:T(8,128)(2,1)} %copy-done.18, ...), custom_call_target="tpu_custom_call", output_to_operand_aliasing={{}: (16, {})} | custom-call | flops 3221225472 | bytes 14680064 | tf_op jit(solution)/shard_map/cross/pallas_call | solution.py:323
  (65 shorter events, 0.3 us)
Async XLA Ops:
  1.7 0.7 copy-start.12
  2.3 0.7 copy-start.13
  3.0 0.7 copy-start.14
  72.1 10.0 %collective-permute-start.20 = (bf16[512,384]{1,0:T(8,128)(2,1)S(1)}, bf16[512,384]{1,0:T(8,128)(2,1)S(1)}, u32[]{:S(2)}, u32[]{:S(2)}) collective-permute-start(bf16[512,384]{1,0:T(8,128)(2,1)S(1)} %stack.145), channel_id=1, source_target_pairs={{0,64},{64,0},{1,65},{65,1},{2,66},{66,2},{3,67},{67,3},{4,68},{68... | collective-permute-start | bytes 1179656 | tf_op jit(solution)/shard_map/ppermute | solution.py:350
  72.4 16.1 %collective-permute-start.15 = (bf16[512,384]{1,0:T(8,128)(2,1)S(1)}, bf16[512,384]{1,0:T(8,128)(2,1)S(1)}, u32[]{:S(2)}, u32[]{:S(2)}) collective-permute-start(bf16[512,384]{1,0:T(8,128)(2,1)S(1)} %stack.145), channel_id=1, source_target_pairs={{0,1},{1,0},{2,3},{3,2},{4,5},{5,4},{6,7},{7,6},{8,9},{9,8},{10,11... | collective-permute-start | bytes 1179656 | tf_op jit(solution)/shard_map/ppermute | solution.py:350
  75.6 23.3 %collective-permute-start.5 = (bf16[512,384]{1,0:T(8,128)(2,1)S(1)}, bf16[512,384]{1,0:T(8,128)(2,1)S(1)}, u32[]{:S(2)}, u32[]{:S(2)}) collective-permute-start(bf16[512,384]{1,0:T(8,128)(2,1)S(1)} %stack.144), channel_id=1, source_target_pairs={{0,64},{64,0},{1,65},{65,1},{2,66},{66,2},{3,67},{67,3},{4,68},{68... | collective-permute-start | bytes 1179656 | tf_op jit(solution)/shard_map/ppermute | solution.py:350
  78.8 26.5 %collective-permute-start = (bf16[512,384]{1,0:T(8,128)(2,1)S(1)}, bf16[512,384]{1,0:T(8,128)(2,1)S(1)}, u32[]{:S(2)}, u32[]{:S(2)}) collective-permute-start(bf16[512,384]{1,0:T(8,128)(2,1)S(1)} %stack.144), channel_id=1, source_target_pairs={{0,1},{1,0},{2,3},{3,2},{4,5},{5,4},{6,7},{7,6},{8,9},{9,8},{10,11... | collective-permute-start | bytes 1179656 | tf_op jit(solution)/shard_map/ppermute | solution.py:350
  88.7 84.2 %copy-start.15 = (bf16[2,512,384]{2,1,0:T(8,128)(2,1)}, bf16[2,512,384]{2,1,0:T(8,128)(2,1)S(1)}, u32[]{:S(2)}) copy-start(bf16[2,512,384]{2,1,0:T(8,128)(2,1)S(1)} %get-tuple-element.5.refs_5_) | copy-start | bytes 2359300
  88.7 20.6 %collective-permute-start.17 = (bf16[2,512,384]{2,1,0:T(8,128)(2,1)S(1)}, bf16[2,512,384]{2,1,0:T(8,128)(2,1)S(1)}, u32[]{:S(2)}, u32[]{:S(2)}) collective-permute-start(bf16[2,512,384]{2,1,0:T(8,128)(2,1)S(1)} %get-tuple-element.6.refs_0_), channel_id=1, source_target_pairs={{0,6},{2,0},{4,2},{6,4},{1,7},{3,1},{5,3},{7,5},{8,14},{10,8},{12,... | collective-permute-start | bytes 2359304 | tf_op jit(solution)/shard_map/ppermute | solution.py:355
  93.6 19.2 %collective-permute-start.16 = (bf16[2,512,384]{2,1,0:T(8,128)(2,1)S(1)}, bf16[2,512,384]{2,1,0:T(8,128)(2,1)S(1)}, u32[]{:S(2)}, u32[]{:S(2)}) collective-permute-start(bf16[2,512,384]{2,1,0:T(8,128)(2,1)S(1)} %get-tuple-element.6.refs_0_), channel_id=1, source_target_pairs={{0,2},{2,4},{4,6},{6,0},{1,3},{3,5},{5,7},{7,1},{8,10},{10,12},{12... | collective-permute-start | bytes 2359304 | tf_op jit(solution)/shard_map/ppermute | solution.py:354
  93.6 19.2 %collective-permute-start.25 = (bf16[2,512,384]{2,1,0:T(8,128)(2,1)S(1)}, bf16[2,512,384]{2,1,0:T(8,128)(2,1)S(1)}, u32[]{:S(2)}, u32[]{:S(2)}) collective-permute-start(bf16[2,512,384]{2,1,0:T(8,128)(2,1)S(1)} %get-tuple-element.5.refs_5_), channel_id=1, source_target_pairs={{0,8},{8,0},{1,9},{9,1},{2,10},{10,2},{3,11},{11,3},{4,12},{12,4},... | collective-permute-start | bytes 2359304 | tf_op jit(solution)/shard_map/ppermute | solution.py:350
  99.0 18.2 %collective-permute-start.22 = (bf16[2,512,384]{2,1,0:T(8,128)(2,1)S(1)}, bf16[2,512,384]{2,1,0:T(8,128)(2,1)S(1)}, u32[]{:S(2)}, u32[]{:S(2)}) collective-permute-start(bf16[2,512,384]{2,1,0:T(8,128)(2,1)S(1)} %get-tuple-element.5.refs_5_), channel_id=1, source_target_pairs={{0,48},{16,0},{32,16},{48,32},{1,49},{17,1},{33,17},{49,33},{2,50}... | collective-permute-start | bytes 2359304 | tf_op jit(solution)/shard_map/ppermute | solution.py:355
  105.4 19.4 %collective-permute-start.21 = (bf16[2,512,384]{2,1,0:T(8,128)(2,1)S(1)}, bf16[2,512,384]{2,1,0:T(8,128)(2,1)S(1)}, u32[]{:S(2)}, u32[]{:S(2)}) collective-permute-start(bf16[2,512,384]{2,1,0:T(8,128)(2,1)S(1)} %get-tuple-element.5.refs_5_), channel_id=1, source_target_pairs={{0,16},{16,32},{32,48},{48,0},{1,17},{17,33},{33,49},{49,1},{2,18}... | collective-permute-start | bytes 2359304 | tf_op jit(solution)/shard_map/ppermute | solution.py:354
  107.6 66.1 %copy-start.16 = (bf16[2,512,384]{2,1,0:T(8,128)(2,1)}, bf16[2,512,384]{2,1,0:T(8,128)(2,1)S(1)}, u32[]{:S(2)}) copy-start(bf16[2,512,384]{2,1,0:T(8,128)(2,1)S(1)} %get-tuple-element.7.refs_5_) | copy-start | bytes 2359300
  109.3 64.4 %copy-start.17 = (bf16[2,512,384]{2,1,0:T(8,128)(2,1)}, bf16[2,512,384]{2,1,0:T(8,128)(2,1)S(1)}, u32[]{:S(2)}) copy-start(bf16[2,512,384]{2,1,0:T(8,128)(2,1)S(1)} %collective-permute-done.17.refs_2_) | copy-start | bytes 2359300
  109.3 18.2 %collective-permute-start.2 = (bf16[2,512,384]{2,1,0:T(8,128)(2,1)S(1)}, bf16[2,512,384]{2,1,0:T(8,128)(2,1)S(1)}, u32[]{:S(2)}, u32[]{:S(2)}) collective-permute-start(bf16[2,512,384]{2,1,0:T(8,128)(2,1)S(1)} %get-tuple-element.8.refs_0_), channel_id=1, source_target_pairs={{0,6},{2,0},{4,2},{6,4},{1,7},{3,1},{5,3},{7,5},{8,14},{10,8},{12,... | collective-permute-start | bytes 2359304 | tf_op jit(solution)/shard_map/ppermute | solution.py:355
  112.7 18.2 %collective-permute-start.1 = (bf16[2,512,384]{2,1,0:T(8,128)(2,1)S(1)}, bf16[2,512,384]{2,1,0:T(8,128)(2,1)S(1)}, u32[]{:S(2)}, u32[]{:S(2)}) collective-permute-start(bf16[2,512,384]{2,1,0:T(8,128)(2,1)S(1)} %get-tuple-element.8.refs_0_), channel_id=1, source_target_pairs={{0,2},{2,4},{4,6},{6,0},{1,3},{3,5},{5,7},{7,1},{8,10},{10,12},{12... | collective-permute-start | bytes 2359304 | tf_op jit(solution)/shard_map/ppermute | solution.py:354
  112.7 61.0 %copy-start.21 = (bf16[2,512,384]{2,1,0:T(8,128)(2,1)}, bf16[2,512,384]{2,1,0:T(8,128)(2,1)S(1)}, u32[]{:S(2)}) copy-start(bf16[2,512,384]{2,1,0:T(8,128)(2,1)S(1)} %collective-permute-done.25.refs_10_) | copy-start | bytes 2359300
  112.8 18.2 %collective-permute-start.10 = (bf16[2,512,384]{2,1,0:T(8,128)(2,1)S(1)}, bf16[2,512,384]{2,1,0:T(8,128)(2,1)S(1)}, u32[]{:S(2)}, u32[]{:S(2)}) collective-permute-start(bf16[2,512,384]{2,1,0:T(8,128)(2,1)S(1)} %get-tuple-element.7.refs_5_), channel_id=1, source_target_pairs={{0,8},{8,0},{1,9},{9,1},{2,10},{10,2},{3,11},{11,3},{4,12},{12,4},... | collective-permute-start | bytes 2359304 | tf_op jit(solution)/shard_map/ppermute | solution.py:350
  117.2 56.5 %copy-start.19 = (bf16[2,512,384]{2,1,0:T(8,128)(2,1)}, bf16[2,512,384]{2,1,0:T(8,128)(2,1)S(1)}, u32[]{:S(2)}) copy-start(bf16[2,512,384]{2,1,0:T(8,128)(2,1)S(1)} %collective-permute-done.22.refs_7_) | copy-start | bytes 2359300
  117.2 17.0 %collective-permute-start.7 = (bf16[2,512,384]{2,1,0:T(8,128)(2,1)S(1)}, bf16[2,512,384]{2,1,0:T(8,128)(2,1)}, u32[]{:S(2)}, u32[]{:S(2)}) collective-permute-start(bf16[2,512,384]{2,1,0:T(8,128)(2,1)S(1)} %get-tuple-element.7.refs_5_), channel_id=1, source_target_pairs={{0,48},{16,0},{32,16},{48,32},{1,49},{17,1},{33,17},{49,33},{2,50}... | collective-permute-start | bytes 2359304 | tf_op jit(solution)/shard_map/ppermute | solution.py:355
  124.8 48.9 %copy-start.20 = (bf16[2,512,384]{2,1,0:T(8,128)(2,1)}, bf16[2,512,384]{2,1,0:T(8,128)(2,1)S(1)}, u32[]{:S(2)}) copy-start(bf16[2,512,384]{2,1,0:T(8,128)(2,1)S(1)} %collective-permute-done.21.refs_6_) | copy-start | bytes 2359300
  124.8 17.4 %collective-permute-start.6 = (bf16[2,512,384]{2,1,0:T(8,128)(2,1)S(1)}, bf16[2,512,384]{2,1,0:T(8,128)(2,1)}, u32[]{:S(2)}, u32[]{:S(2)}) collective-permute-start(bf16[2,512,384]{2,1,0:T(8,128)(2,1)S(1)} %get-tuple-element.7.refs_5_), channel_id=1, source_target_pairs={{0,16},{16,32},{32,48},{48,0},{1,17},{17,33},{33,49},{49,1},{2,18}... | collective-permute-start | bytes 2359304 | tf_op jit(solution)/shard_map/ppermute | solution.py:354
  127.6 46.1 %copy-start.18 = (bf16[2,512,384]{2,1,0:T(8,128)(2,1)}, bf16[2,512,384]{2,1,0:T(8,128)(2,1)S(1)}, u32[]{:S(2)}) copy-start(bf16[2,512,384]{2,1,0:T(8,128)(2,1)S(1)} %collective-permute-done.2.refs_2_) | copy-start | bytes 2359300
  127.6 24.1 %collective-permute-start.19 = (bf16[2,256,384]{2,1,0:T(8,128)(2,1)S(1)}, bf16[2,256,384]{2,1,0:T(8,128)(2,1)S(1)}, u32[]{:S(2)}, u32[]{:S(2)}) collective-permute-start(bf16[2,256,384]{2,1,0:T(8,128)(2,1)S(1)} %slice.37), channel_id=1, source_target_pairs={{0,6},{2,0},{4,2},{6,4},{1,7},{3,1},{5,3},{7,5},{8,14},{10,8},{12,... | collective-permute-start | bytes 1179656 | tf_op jit(solution)/shard_map/ppermute | solution.py:358
  131.0 24.4 %collective-permute-start.18 = (bf16[2,256,384]{2,1,0:T(8,128)(2,1)S(1)}, bf16[2,256,384]{2,1,0:T(8,128)(2,1)S(1)}, u32[]{:S(2)}, u32[]{:S(2)}) collective-permute-start(bf16[2,256,384]{2,1,0:T(8,128)(2,1)S(1)} %slice.36), channel_id=1, source_target_pairs={{0,2},{2,4},{4,6},{6,0},{1,3},{3,5},{5,7},{7,1},{8,10},{10,12},{12... | collective-permute-start | bytes 1179656 | tf_op jit(solution)/shard_map/ppermute | solution.py:357
  131.0 42.7 %copy-start.22 = (bf16[2,512,384]{2,1,0:T(8,128)(2,1)}, bf16[2,512,384]{2,1,0:T(8,128)(2,1)S(1)}, u32[]{:S(2)}) copy-start(bf16[2,512,384]{2,1,0:T(8,128)(2,1)S(1)} %collective-permute-done.10.refs_10_) | copy-start | bytes 2359300
  131.0 25.1 %collective-permute-start.24 = (bf16[2,256,384]{2,1,0:T(8,128)(2,1)S(1)}, bf16[2,256,384]{2,1,0:T(8,128)(2,1)S(1)}, u32[]{:S(2)}, u32[]{:S(2)}) collective-permute-start(bf16[2,256,384]{2,1,0:T(8,128)(2,1)S(1)} %slice.39), channel_id=1, source_target_pairs={{0,48},{16,0},{32,16},{48,32},{1,49},{17,1},{33,17},{49,33},{2,50}... | collective-permute-start | bytes 1179656 | tf_op jit(solution)/shard_map/ppermute | solution.py:358
  134.2 22.2 %collective-permute-start.23 = (bf16[2,256,384]{2,1,0:T(8,128)(2,1)S(1)}, bf16[2,256,384]{2,1,0:T(8,128)(2,1)S(1)}, u32[]{:S(2)}, u32[]{:S(2)}) collective-permute-start(bf16[2,256,384]{2,1,0:T(8,128)(2,1)S(1)} %slice.38), channel_id=1, source_target_pairs={{0,16},{16,32},{32,48},{48,0},{1,17},{17,33},{33,49},{49,1},{2,18}... | collective-permute-start | bytes 1179656 | tf_op jit(solution)/shard_map/ppermute | solution.py:357
  142.2 27.8 %collective-permute-start.27 = (bf16[2,512,384]{2,1,0:T(8,128)(2,1)S(1)}, bf16[2,512,384]{2,1,0:T(8,128)(2,1)S(1)}, u32[]{:S(2)}, u32[]{:S(2)}) collective-permute-start(bf16[2,512,384]{2,1,0:T(8,128)(2,1)S(1)} %collective-permute-done.22.refs_7_), channel_id=1, source_target_pairs={{0,8},{8,0},{1,9},{9,1},{2,10},{10,2},{3,11},{11,3},{4,12},{12,4},... | collective-permute-start | bytes 2359304 | tf_op jit(solution)/shard_map/ppermute | solution.py:350
  151.7 12.2 %collective-permute-start.4 = (bf16[2,256,384]{2,1,0:T(8,128)(2,1)S(1)}, bf16[2,256,384]{2,1,0:T(8,128)(2,1)S(1)}, u32[]{:S(2)}, u32[]{:S(2)}) collective-permute-start(bf16[2,256,384]{2,1,0:T(8,128)(2,1)S(1)} %slice.33), channel_id=1, source_target_pairs={{0,6},{2,0},{4,2},{6,4},{1,7},{3,1},{5,3},{7,5},{8,14},{10,8},{12,... | collective-permute-start | bytes 1179656 | tf_op jit(solution)/shard_map/ppermute | solution.py:358
  155.4 0.7 copy-start
  156.1 10.5 %collective-permute-start.9 = (bf16[2,256,384]{2,1,0:T(8,128)(2,1)S(1)}, bf16[2,256,384]{2,1,0:T(8,128)(2,1)}, u32[]{:S(2)}, u32[]{:S(2)}) collective-permute-start(bf16[2,256,384]{2,1,0:T(8,128)(2,1)S(1)} %slice.35), channel_id=1, source_target_pairs={{0,48},{16,0},{32,16},{48,32},{1,49},{17,1},{33,17},{49,33},{2,50}... | collective-permute-start | bytes 1179656 | tf_op jit(solution)/shard_map/ppermute | solution.py:358
  156.1 15.5 %collective-permute-start.26 = (bf16[2,512,384]{2,1,0:T(8,128)(2,1)S(1)}, bf16[2,512,384]{2,1,0:T(8,128)(2,1)S(1)}, u32[]{:S(2)}, u32[]{:S(2)}) collective-permute-start(bf16[2,512,384]{2,1,0:T(8,128)(2,1)S(1)} %collective-permute-done.21.refs_6_), channel_id=1, source_target_pairs={{0,8},{8,0},{1,9},{9,1},{2,10},{10,2},{3,11},{11,3},{4,12},{12,4},... | collective-permute-start | bytes 2359304 | tf_op jit(solution)/shard_map/ppermute | solution.py:350
  156.4 11.8 %collective-permute-start.8 = (bf16[2,256,384]{2,1,0:T(8,128)(2,1)S(1)}, bf16[2,256,384]{2,1,0:T(8,128)(2,1)}, u32[]{:S(2)}, u32[]{:S(2)}) collective-permute-start(bf16[2,256,384]{2,1,0:T(8,128)(2,1)S(1)} %slice.34), channel_id=1, source_target_pairs={{0,16},{16,32},{32,48},{48,0},{1,17},{17,33},{33,49},{49,1},{2,18}... | collective-permute-start | bytes 1179656 | tf_op jit(solution)/shard_map/ppermute | solution.py:357
  163.9 0.8 copy-start.2
  164.7 43.9 %collective-permute-start.12 = (bf16[2,512,384]{2,1,0:T(8,128)(2,1)}, bf16[2,512,384]{2,1,0:T(8,128)(2,1)}, u32[]{:S(2)}, u32[]{:S(2)}) collective-permute-start(bf16[2,512,384]{2,1,0:T(8,128)(2,1)} %collective-permute-done.7.refs_7_), channel_id=1, source_target_pairs={{0,8},{8,0},{1,9},{9,1},{2,10},{10,2},{3,11},{11,3},{4,12},{12,4},... | collective-permute-start | bytes 2359304 | tf_op jit(solution)/shard_map/ppermute | solution.py:350
  166.7 41.9 %collective-permute-start.11 = (bf16[2,512,384]{2,1,0:T(8,128)(2,1)}, bf16[2,512,384]{2,1,0:T(8,128)(2,1)}, u32[]{:S(2)}, u32[]{:S(2)}) collective-permute-start(bf16[2,512,384]{2,1,0:T(8,128)(2,1)} %collective-permute-done.6.refs_6_), channel_id=1, source_target_pairs={{0,8},{8,0},{1,9},{9,1},{2,10},{10,2},{3,11},{11,3},{4,12},{12,4},... | collective-permute-start | bytes 2359304 | tf_op jit(solution)/shard_map/ppermute | solution.py:350
  168.2 3.4 %collective-permute-start.29 = (bf16[2,256,384]{2,1,0:T(8,128)(2,1)S(1)}, bf16[2,256,384]{2,1,0:T(8,128)(2,1)S(1)}, u32[]{:S(2)}, u32[]{:S(2)}) collective-permute-start(bf16[2,256,384]{2,1,0:T(8,128)(2,1)S(1)} %collective-permute-done.24.refs_9_), channel_id=1, source_target_pairs={{0,8},{8,0},{1,9},{9,1},{2,10},{10,2},{3,11},{11,3},{4,12},{12,4},... | collective-permute-start | bytes 1179656 | tf_op jit(solution)/shard_map/ppermute | solution.py:350
  169.3 0.8 copy-start.4
  170.0 3.7 %copy-start.23 = (bf16[2,512,384]{2,1,0:T(8,128)(2,1)}, bf16[2,512,384]{2,1,0:T(8,128)(2,1)S(1)}, u32[]{:S(2)}) copy-start(bf16[2,512,384]{2,1,0:T(8,128)(2,1)S(1)} %collective-permute-done.27.refs_12_) | copy-start | bytes 2359300
  170.0 2.9 %collective-permute-start.28 = (bf16[2,256,384]{2,1,0:T(8,128)(2,1)S(1)}, bf16[2,256,384]{2,1,0:T(8,128)(2,1)S(1)}, u32[]{:S(2)}, u32[]{:S(2)}) collective-permute-start(bf16[2,256,384]{2,1,0:T(8,128)(2,1)S(1)} %collective-permute-done.23.refs_8_), channel_id=1, source_target_pairs={{0,8},{8,0},{1,9},{9,1},{2,10},{10,2},{3,11},{11,3},{4,12},{12,4},... | collective-permute-start | bytes 1179656 | tf_op jit(solution)/shard_map/ppermute | solution.py:350
  170.0 0.8 copy-start.6
  171.6 2.1 copy-start.24
  171.6 36.9 %collective-permute-start.3 = (bf16[2,256,384]{2,1,0:T(8,128)(2,1)}, bf16[2,256,384]{2,1,0:T(8,128)(2,1)}, u32[]{:S(2)}, u32[]{:S(2)}) collective-permute-start(bf16[2,256,384]{2,1,0:T(8,128)(2,1)} %slice.32), channel_id=1, source_target_pairs={{0,2},{2,4},{4,6},{6,0},{1,3},{3,5},{5,7},{7,1},{8,10},{10,12},{12... | collective-permute-start | bytes 1179656 | tf_op jit(solution)/shard_map/ppermute | solution.py:357
  171.6 0.8 copy-start.8
  172.4 36.1 %collective-permute-start.14 = (bf16[2,256,384]{2,1,0:T(8,128)(2,1)}, bf16[2,256,384]{2,1,0:T(8,128)(2,1)}, u32[]{:S(2)}, u32[]{:S(2)}) collective-permute-start(bf16[2,256,384]{2,1,0:T(8,128)(2,1)} %collective-permute-done.9.refs_9_), channel_id=1, source_target_pairs={{0,8},{8,0},{1,9},{9,1},{2,10},{10,2},{3,11},{11,3},{4,12},{12,4},... | collective-permute-start | bytes 1179656 | tf_op jit(solution)/shard_map/ppermute | solution.py:350
  172.9 0.7 copy-start.10
  173.7 34.9 %collective-permute-start.13 = (bf16[2,256,384]{2,1,0:T(8,128)(2,1)}, bf16[2,256,384]{2,1,0:T(8,128)(2,1)}, u32[]{:S(2)}, u32[]{:S(2)}) collective-permute-start(bf16[2,256,384]{2,1,0:T(8,128)(2,1)} %collective-permute-done.8.refs_8_), channel_id=1, source_target_pairs={{0,8},{8,0},{1,9},{9,1},{2,10},{10,2},{3,11},{11,3},{4,12},{12,4},... | collective-permute-start | bytes 1179656 | tf_op jit(solution)/shard_map/ppermute | solution.py:350
  174.0 1.0 copy-start.1
  175.0 1.0 copy-start.5
  176.0 1.0 copy-start.7
  177.0 1.0 copy-start.9
  178.0 1.0 copy-start.11
  178.9 29.6 %copy-start.3 = (bf16[2,256,384]{2,1,0:T(8,128)(2,1)S(1)}, bf16[2,256,384]{2,1,0:T(8,128)(2,1)}, u32[]{:S(2)}) copy-start(bf16[2,256,384]{2,1,0:T(8,128)(2,1)} %copy-done.2) | copy-start | bytes 1179652

commit v2 on v1

v2 whole, which is shorter than its diff:
```python
import math

import jax
import jax.numpy as jnp
from jax import lax
from jax.experimental import pallas as pl
from jax.experimental.pallas import tpu as pltpu
from jax.sharding import Mesh, PartitionSpec as P

L = 8192
NBAND = 256
HALF = 64
WMAX = 8
ST_DEV = 8
HOURS = 96
CAP = 16
EPS = 1e-05
FLOOR = 0.5

AXES = ("zh", "y", "core", "x", "zl")
DEVICES = 128
SEGS = 512
STEP = 1024
STEPS = L // STEP
PAIRS = 64
WIDE = 4 * HOURS
TAGGED = 4 * CAP + 8
F32 = jnp.float32
BF16 = jnp.bfloat16


def iota(shape, axis):
    return lax.broadcasted_iota(jnp.int32, shape, axis)


def transform_kernel(
    main, before, after, owner_row, slot_row, width_row, bins,
    send, low_cos, low_sin, high_cos, high_sin, band, magnitude, normal, table, total,
):
    step = pl.program_id(0)

    @pl.when(step == 0)
    def _():
        unit = 2.0 * math.pi / L
        phase = (iota((128, NBAND), 0) * bins[...]) & (L - 1)
        angle = phase.astype(F32) * unit
        low_cos[...] = jnp.cos(angle)
        low_sin[...] = jnp.sin(angle)
        phase = (iota((64, NBAND), 0) * 128 * bins[...]) & (L - 1)
        angle = phase.astype(F32) * unit
        high_cos[...] = jnp.cos(angle)
        high_sin[...] = jnp.sin(angle)
        offset = iota((512, 256), 0) - 128 - iota((512, 256), 1)
        band[...] = jnp.where(jnp.abs(offset) <= HALF, 1.0, 0.0).astype(BF16)
        total[...] = jnp.zeros_like(total)

    for part in range(STEP // 128):
        high = step * (STEP // 128) + part
        cos_high = high_cos[pl.ds(high, 1), :]
        sin_high = high_sin[pl.ds(high, 1), :]
        rows = slice(part * 128, part * 128 + 128)
        table[rows, :NBAND] = (cos_high * low_cos[...] - sin_high * low_sin[...]).astype(BF16)
        table[rows, NBAND:] = (-(sin_high * low_cos[...] + cos_high * low_sin[...])).astype(BF16)

    magnitude[:, 128 : 128 + STEP] = jnp.abs(main[...])
    magnitude[:, :128] = jnp.where(step > 0, jnp.abs(before[...]), jnp.zeros((), BF16))
    magnitude[:, 128 + STEP :] = jnp.where(
        step < STEPS - 1, jnp.abs(after[...]), jnp.zeros((), BF16)
    )
    for part in range(STEP // 256):
        sums = jnp.dot(
            magnitude[:, part * 256 : part * 256 + 512], band[...], preferred_element_type=F32
        )
        place = step * STEP + part * 256 + iota((1, 256), 1)
        count = jnp.minimum(place + HALF, L - 1) - jnp.maximum(place - HALF, 0) + 1
        count = count.astype(F32)
        below = sums + count * EPS
        inverse = pl.reciprocal(below, approx=True)
        inverse = inverse * (2.0 - below * inverse)
        values = main[:, part * 256 : part * 256 + 256].astype(F32)
        normal[:, part * 256 : part * 256 + 256] = (values * (count * inverse)).astype(BF16)
    total[...] += jnp.dot(normal[...], table[...], preferred_element_type=F32)

    @pl.when(step == STEPS - 1)
    def _():
        rows = jnp.concatenate(
            [
                jnp.broadcast_to(owner_row[...].astype(F32), (64, SEGS)),
                jnp.broadcast_to(slot_row[...].astype(F32), (64, SEGS)),
            ],
            axis=0,
        )
        columns = rows.T.astype(jnp.int32)
        owner_col = columns[:, 0:1]
        slots = columns[:, 64:65]
        station = jnp.zeros_like(slots)
        for edge in range(1, ST_DEV):
            station += (slots >= edge * HOURS).astype(jnp.int32)
        hour = slots - station * HOURS
        whole = owner_col * ST_DEV + station
        hits = whole == iota((1, DEVICES * ST_DEV), 1)
        widths = jnp.sum(jnp.where(hits, width_row[...], 0).astype(F32), axis=1, keepdims=True)
        widths = widths.astype(jnp.int32)
        real = total[:, :NBAND] * (1.0 / math.sqrt(L))
        imag = total[:, NBAND:] * (1.0 / math.sqrt(L))
        amplitude = jnp.sqrt(real * real + imag * imag)
        lane = iota((1, NBAND), 1)
        smooth = amplitude
        for width in range(1, WMAX + 1):
            up = pltpu.roll(amplitude, width, 1)
            down = pltpu.roll(amplitude, NBAND - width, 1)
            both = jnp.where(lane >= width, up, 0.0) + jnp.where(lane < NBAND - width, down, 0.0)
            smooth += jnp.where(widths >= width, both, 0.0)
        number = jnp.minimum(lane + widths, NBAND - 1) - jnp.maximum(lane - widths, 0) + 1
        factor = 1.0 / jnp.maximum(smooth / number.astype(F32), FLOOR)
        lanes = iota((SEGS, 128), 1)
        extra = jnp.where(
            lanes == 0, station, jnp.where(lanes == 1, hour, jnp.where(lanes == 2, 1, 0))
        )
        whitened = jnp.concatenate(
            [
                (real * factor).astype(BF16),
                (imag * factor).astype(BF16),
                extra.astype(F32).astype(BF16),
            ],
            axis=1,
        )
        same = (owner_col == owner_row[...]) & (iota((SEGS, SEGS), 0) < iota((SEGS, SEGS), 1))
        rank = jnp.sum(same.astype(F32), axis=0, keepdims=True).astype(jnp.int32)
        target = owner_row[...] * CAP + rank
        for part in range(4):
            chosen = target == iota((512, SEGS), 0) + part * 512
            chosen = jnp.where(chosen, 1.0, 0.0).astype(BF16)
            picked = jnp.dot(chosen, whitened, preferred_element_type=F32)
            tags = picked[:, 2 * NBAND :].reshape(32, CAP, 128)
            tags = tags[:, :8] + pltpu.roll(tags[:, 8:], 64, 2)
            send[part * 32 : part * 32 + 32, 4 * CAP :, :] = tags.astype(BF16)
            picked = picked.astype(BF16)
            for tile in range(4):
                send[part * 32 : part * 32 + 32, tile * CAP : tile * CAP + CAP, :] = picked[
                    :, tile * 128 : tile * 128 + 128
                ].reshape(32, CAP, 128)


def transform(traces, seg_owner, seg_slot, white_width, band_bins):
    return pl.pallas_call(
        transform_kernel,
        grid=(STEPS,),
        in_specs=[
            pl.BlockSpec((SEGS, STEP), lambda k: (0, k)),
            pl.BlockSpec((SEGS, 128), lambda k: (0, jnp.maximum(k * (STEP // 128) - 1, 0))),
            pl.BlockSpec(
                (SEGS, 128), lambda k: (0, jnp.minimum((k + 1) * (STEP // 128), L // 128 - 1))
            ),
            pl.BlockSpec((1, SEGS), lambda k: (0, 0)),
            pl.BlockSpec((1, SEGS), lambda k: (0, 0)),
            pl.BlockSpec((1, DEVICES * ST_DEV), lambda k: (0, 0)),
            pl.BlockSpec((1, NBAND), lambda k: (0, 0)),
        ],
        out_specs=pl.BlockSpec((DEVICES, TAGGED, 128), lambda k: (0, 0, 0)),
        out_shape=jax.ShapeDtypeStruct((DEVICES, TAGGED, 128), BF16),
        scratch_shapes=[
            pltpu.VMEM((128, NBAND), F32),
            pltpu.VMEM((128, NBAND), F32),
            pltpu.VMEM((64, NBAND), F32),
            pltpu.VMEM((64, NBAND), F32),
            pltpu.VMEM((512, 256), BF16),
            pltpu.VMEM((SEGS, STEP + 256), BF16),
            pltpu.VMEM((SEGS, STEP), BF16),
            pltpu.VMEM((STEP, 2 * NBAND), BF16),
            pltpu.VMEM((SEGS, 2 * NBAND), F32),
        ],
        compiler_params=pltpu.CompilerParams(vmem_limit_bytes=58 << 20),
        cost_estimate=pl.CostEstimate(
            flops=10 * SEGS * L * 512, bytes_accessed=SEGS * L * 2, transcendentals=SEGS * L
        ),
        name="transform",
    )(
        traces, traces, traces, seg_owner.reshape(1, SEGS), seg_slot.reshape(1, SEGS),
        white_width.reshape(1, -1), band_bins.reshape(1, -1),
    )


def stack_kernel(received, spectra, wide):
    half = pl.program_id(0)
    tags = received[:, 4 * CAP :, :].astype(F32)
    tags = jnp.concatenate([tags, pltpu.roll(tags, 64, 2)], axis=1).reshape(DEVICES * CAP, 128)
    column = (tags[:, 0:1] * 128.0 + tags[:, 1:2] + (tags[:, 2:3] - 1.0)).astype(jnp.int32)
    total = jnp.zeros((256, ST_DEV * 128), F32)
    block = 512
    at = pl.multiple_of(half * CAP, CAP)
    for part in range(DEVICES * CAP // block):
        sources = slice(part * block // CAP, (part + 1) * block // CAP)
        hits = column[part * block : (part + 1) * block] == iota((1, ST_DEV * 128), 1)
        hits = jnp.where(hits, 1.0, 0.0).astype(BF16)
        real = received[sources, pl.ds(at, CAP), :].reshape(block, 128)
        imag = received[sources, pl.ds(at + 2 * CAP, CAP), :].reshape(block, 128)
        both = jnp.concatenate([real, imag], axis=1)
        total += lax.dot_general(both, hits, (((0,), (0,)), ((), ())), preferred_element_type=F32)
    lane = iota((PAIRS, 128), 1)
    for station in range(ST_DEV):
        lanes = slice(station * 128, station * 128 + 128)
        real_first = total[0:64, lanes]
        real_second = pltpu.roll(total[64:128, lanes], 64, 1)
        imag_first = pltpu.roll(total[128:192, lanes], 96, 1)
        imag_second = pltpu.roll(total[192:256, lanes], 32, 1)
        wide[:, station, 0:128] = jnp.where(lane < 96, real_first, imag_first)
        wide[:, station, 128:256] = jnp.where(lane < 64, imag_first, real_second)
        wide[:, station, 256:384] = jnp.where(lane < 32, real_second, imag_second)
    spectra[...] = wide[...].reshape(PAIRS * ST_DEV, WIDE).astype(BF16)


def stack(received):
    return pl.pallas_call(
        stack_kernel,
        grid=(2,),
        in_specs=[pl.BlockSpec((DEVICES, TAGGED, 128), lambda k: (0, 0, 0))],
        out_specs=pl.BlockSpec((PAIRS * ST_DEV, WIDE), lambda k: (k, 0)),
        out_shape=jax.ShapeDtypeStruct((2 * PAIRS * ST_DEV, WIDE), BF16),
        scratch_shapes=[pltpu.VMEM((PAIRS, ST_DEV, WIDE), F32)],
        compiler_params=pltpu.CompilerParams(vmem_limit_bytes=20 << 20),
        cost_estimate=pl.CostEstimate(
            flops=2 * 2048 * 1024 * 256 * 2, bytes_accessed=3 << 20, transcendentals=0
        ),
        name="stack",
    )(received)


BLOCK = 32
BLOCKS = PAIRS // BLOCK
OUT_ROWS = 16
STRIDE = 2 * 2 * PAIRS + 8


def cross_kernel(places, *refs):
    rows, columns = refs[0:8], list(refs[8:16])
    early, late, beside_left, beside_far = refs[16:20]
    out, row_blocks, column_blocks, left, right, swapped, swap, results, arrived = refs[20:]
    columns += [early.at[0], early.at[1], early.at[2], beside_left]
    columns += [early.at[3], late.at[1], late.at[0], beside_far]
    step = pl.program_id(0)

    def copies(block):
        size = BLOCK * ST_DEV
        at = pl.ds(pl.multiple_of(block * size, size), size)
        out = []
        for index in range(24):
            if index < 8:
                source, target = rows[index], row_blocks
            else:
                source, target = columns[index - 8], column_blocks
            out.append(
                pltpu.make_async_copy(
                    source.at[at], target.at[places[index], at], arrived.at[block, index]
                )
            )
        return out

    @pl.when(step == 0)
    def _():
        @pl.loop(0, 2 * BLOCKS)
        def _(block):
            for copy in copies(block):
                copy.start()

    @pl.when(step < 2 * BLOCKS)
    def _():
        for copy in copies(step):
            copy.wait()

    @pl.when(step == 0)
    def _():
        source = iota((WIDE, WIDE), 0)
        target = iota((WIDE, WIDE), 1)
        group = (target // HOURS) % 2
        ahead = (source == target + HOURS) & (group == 0)
        behind = (source == target - HOURS) & (group == 1)
        swap[...] = (jnp.where(ahead, 1.0, 0.0) - jnp.where(behind, 1.0, 0.0)).astype(BF16)

    @pl.when(step < 2 * BLOCKS)
    def _():
        size = BLOCK * ST_DEV
        whole = pl.ds(pl.multiple_of(step * size, size), size)
        for blocks, target, count in ((row_blocks, left, 8), (column_blocks, right, 16)):
            for index in range(0, count, 2):
                both = [
                    blocks[index + k, whole, :].astype(F32).reshape(BLOCK, ST_DEV, WIDE)
                    for k in range(2)
                ]
                target[:, index * ST_DEV : (index + 2) * ST_DEV, :] = jnp.concatenate(
                    both, axis=1
                ).astype(BF16)
        plain = left[...].reshape(BLOCK * 64, WIDE)
        swapped[...] = (
            jnp.dot(plain, swap[...], preferred_element_type=F32)
            .astype(BF16)
            .reshape(BLOCK, 64, WIDE)
        )
        lane = iota((1, 256), 1)
        first_mask = jnp.where(lane < 2 * HOURS, 1.0, 0.0).astype(BF16)
        second_mask = jnp.where(lane >= 2 * HOURS - 128, 1.0, 0.0).astype(BF16)

        @pl.loop(0, BLOCK, unroll=32)
        def _(pair):
            for part, mask in ((0, first_mask), (1, second_mask)):
                lanes = slice(part * 128, part * 128 + 256)
                rows = jnp.concatenate(
                    [left[pair, :, lanes], swapped[pair, :, lanes]], axis=0
                )
                product = lax.dot_general(
                    rows * mask,
                    right[pair, :, lanes],
                    (((1,), (1,)), ((), ())),
                    preferred_element_type=F32,
                )
                at = step * BLOCK + (step // BLOCKS) * PAIRS + pair + part * PAIRS
                results[pl.ds(at, 128, stride=STRIDE), :] = product

    @pl.when(step >= 2 * BLOCKS)
    def _():
        first = (step - 2 * BLOCKS) * OUT_ROWS
        for row in range(OUT_ROWS):
            for part in range(2):
                for half in range(2):
                    at = (first + row + part * 64) * STRIDE + half * 128
                    lanes = slice(part * NBAND + half * 128, part * NBAND + half * 128 + 128)
                    product = results[pl.ds(pl.multiple_of(at, 8), 128), :]
                    out[row, :, lanes] = product.T.astype(BF16)


def cross(places, rows, columns):
    return pl.pallas_call(
        cross_kernel,
        grid=(2 * BLOCKS + 64 // OUT_ROWS,),
        in_specs=[pl.BlockSpec(memory_space=pltpu.SMEM)] + [pl.BlockSpec(memory_space=pltpu.HBM)] * 20,
        out_specs=pl.BlockSpec(
            (OUT_ROWS, 128, 2 * NBAND), lambda step: (jnp.maximum(step - 2 * BLOCKS, 0), 0, 0)
        ),
        out_shape=jax.ShapeDtypeStruct((64, 128, 2 * NBAND), BF16),
        scratch_shapes=[
            pltpu.VMEM((8, 2 * PAIRS * ST_DEV, WIDE), BF16),
            pltpu.VMEM((16, 2 * PAIRS * ST_DEV, WIDE), BF16),
            pltpu.VMEM((BLOCK, 64, WIDE), BF16),
            pltpu.VMEM((BLOCK, 128, WIDE), BF16),
            pltpu.VMEM((BLOCK, 64, WIDE), BF16),
            pltpu.VMEM((WIDE, WIDE), BF16),
            pltpu.VMEM((128 * STRIDE, 128), F32),
            pltpu.SemaphoreType.DMA((2 * BLOCKS, 24)),
        ],
        compiler_params=pltpu.CompilerParams(vmem_limit_bytes=58 << 20),
        cost_estimate=pl.CostEstimate(
            flops=2 * 128 * 128 * 256 * 128 * 3, bytes_accessed=14 << 20, transcendentals=0
        ),
        name="cross",
    )(places, *rows, *columns)


def ring(size, shift):
    return [(i, (i + shift) % size) for i in range(size)]


def turn(moves, *others):
    arrays = [move[0] for move in moves]
    arrays = lax.optimization_barrier(tuple(arrays) + others)[: len(moves)]
    return [lax.ppermute(array, axis, pairs) for array, (_, axis, pairs) in zip(arrays, moves)]


UP, DOWN, SWAP = ring(4, 1), ring(4, 3), [(0, 1), (1, 0)]


def gather(own):
    lx, rx, ly, ry, q = turn(
        [(own, "x", UP), (own, "x", DOWN), (own, "y", UP), (own, "y", DOWN), (own, "zh", SWAP)]
    )
    early = jnp.stack([own, q, ly, ry])
    fx, fy, rq, p, s_early = turn(
        [(lx, "x", UP), (ly, "y", UP), (q, "y", DOWN), (own, "zl", SWAP), (early, "core", SWAP)],
        rx,
    )
    late = jnp.stack([fy, rq])
    lp, rp, lq, gq, gp = turn(
        [(p, "x", UP), (p, "x", DOWN), (q, "y", UP), (rq, "y", DOWN), (fx, "zl", SWAP)],
        fy, s_early,
    )
    s_late, s_lq, s_gq = turn(
        [(late, "core", SWAP), (lq, "core", SWAP), (gq, "core", SWAP)], lp, rp, gp
    )
    rows = [own, p, lx, lp, rx, rp, fx, gp]
    columns = [own, q, ly, lq, ry, rq, fy, gq, s_early, s_late, s_lq, s_gq]
    return rows, columns


def block_places():
    zh, y, core, x, zl = (lax.axis_index(name) for name in AXES)
    out = []
    for shift in (0, 3, 1, 2):
        there = (x + shift) % 4
        out += [there * 2 + zl, there * 2 + (1 - zl)]
    for own in (core, 1 - core):
        for shift in (0, 3, 1, 2):
            there = (y + shift) % 4
            out += [zh * 8 + there * 2 + own, (1 - zh) * 8 + there * 2 + own]
    return jnp.stack(out).astype(jnp.int32)


def on_device(traces, seg_owner, seg_slot, white_width, band_bins):
    send = transform(traces, seg_owner, seg_slot, white_width, band_bins)
    places = block_places()
    received = lax.all_to_all(send, AXES, split_axis=0, concat_axis=0, tiled=True)
    own = stack(received)
    rows, columns = gather(own)
    return cross(places, rows, columns)


def solution(mesh):
    fine = Mesh(mesh.devices.reshape(2, 4, 2, 4, 2), AXES)
    return jax.shard_map(
        on_device,
        mesh=fine,
        in_specs=(P(AXES, None), P(AXES, None), P(AXES), P(), P()),
        out_specs=P(("zh", "y", "core"), ("x", "zl"), None),
        check_vma=False,
    )
```

time: 239 us -> 168 us (0.70)
  Pallas kernels: 84.5 us -> 46.2 us
  starting transfers between devices: 49.1 us -> 22.5 us
  local copies, waits for them, and re-layouts: 16.5 us -> 2.23 us
  waiting for transfers between devices: 42 us -> 51.7 us
  blocking collectives: 45.8 us -> 43 us
    pallas_call x4 -> x2, Pallas kernels: 64.4 us -> 24.2 us  [the longest x1 19.2 us: cross(): pl.pallas_call(cross_kernel, grid=(2 * BLOCKS + 64 // OUT_ROWS,), in_spec...]
    ppermute x30 -> x18, starting transfers between devices: 49.1 us -> 22.5 us  [turn(): lax.ppermute(array, axis, pairs)]
    unnamed x51 -> x30, local copies, waits for them, and re-layouts: 12.5 us -> 1.6 us
    ppermute x30 -> x18, waiting for transfers between devices: 42 us -> 51.7 us  [turn(): lax.ppermute(array, axis, pairs)]
    slice x8 -> x0, local copies, waits for them, and re-layouts: 3.08 us -> none  [the longest x4 1.91 us: spread(): first = lax.ppermute(left[:, :middle], axis, ring(4, 1))]
    all_to_all x1, blocking collectives: 45.8 us -> 43 us  [on_device(): lax.all_to_all(send, AXES, split_axis=0, concat_axis=0, tiled=True)]
  transfers between devices with their start and end apart: 30 -> 18, of which waited for: 13 -> 13; matrix products, arithmetic and copies ran while one was open for 1% -> 1% of each run, Pallas kernels for 13% -> 0%
where the time goes in v2:
time: 168 us
  waiting for transfers between devices  51.7 us (31%)
  Pallas kernels  46.2 us (28%)
  blocking collectives  43 us (26%)
  starting transfers between devices  22.5 us (13%)
  local copies, waits for them, and re-layouts  2.23 us (1%)
  other arithmetic  1.85 us (1%)
    ppermute x18, waiting for transfers between devices, turn(): lax.ppermute(array, axis, pairs)  51.7 us
    all_to_all x1, blocking collectives, on_device(): lax.all_to_all(send, AXES, split_axis=0, concat_axis=0, tiled=True)  43 us
    ppermute x18, starting transfers between devices, turn(): lax.ppermute(array, axis, pairs)  22.5 us
    pallas_call x1, Pallas kernels, transform(): pl.pallas_call(transform_kernel, grid=(STEPS,), in_specs=[pl.BlockSpec((S...  22 us
    pallas_call x1, Pallas kernels, cross(): pl.pallas_call(cross_kernel, grid=(2 * BLOCKS + 64 // OUT_ROWS,), in_spec...  19.2 us
    pallas_call x1, Pallas kernels, stack(): pl.pallas_call(stack_kernel, grid=(2,), in_specs=[pl.BlockSpec((DEVICES,...  5.02 us
  transfers between devices with their start and end apart: 18, of which 13 were waited for; matrix products, arithmetic and copies ran while one was open for 1% of the time, Pallas kernels for 0%

profile of v2, /device:TPU:1, one launch (start us, length us, event | category | flops | bytes accessed | tf_op | source)
XLA Modules:
  0.0 167.8 jit_solution(16576737620365320095)
XLA Ops:
  0.0 22.0 %transform.1 = bf16[128,72,128]{2,1,0:T(8,128)(2,1)} custom-call(bf16[512,8192]{1,0:T(8,128)(2,1)} %after.1, bf16[512,8192]{1,0:T(8,128)(2,1)} %after.1, bf16[512,8192]{1,0:T(8,128)(2,1)} %after.1, s32[1,512]{1,0:T(1,128)} %bitcast.41, s32[1,512]{1,0:T(1,128)} %bitcast.42, s32[1,1024]{1,0:T(1,128)} %bitcast.40, s32[1,256]{1,0:T(1,128)} %bitcast.43), custom_call_target="tpu_custom_call" | custom-call | flops 21474836480 | bytes 8388608 | tf_op jit(solution)/shard_map/transform/pallas_call | solution.py:146
  22.0 43.0 %all_to_all.5.received = bf16[128,72,128]{2,1,0:T(8,128)(2,1)S(1)} all-to-all(bf16[128,72,128]{2,1,0:T(8,128)(2,1)} %transform.1), channel_id=1, replica_groups=mesh['zh'=2,'y'=4,'core'=2,'x'=4,'zl'=2] {'zh','y','core','x','zl'}, dimensions={0} | all-to-all | bytes 4718592 | tf_op jit(solution)/shard_map/all_to_all | solution.py:409
  65.0 5.0 %stack.133.refs_0_.refs_8_ = bf16[1024,384]{1,0:T(8,128)(2,1)S(1)} custom-call(bf16[128,72,128]{2,1,0:T(8,128)(2,1)S(1)} %all_to_all.5.received), custom_call_target="tpu_custom_call" | custom-call | flops 2147483648 | bytes 3145728 | tf_op jit(solution)/shard_map/stack/pallas_call | solution.py:214
  70.0 0.0 copy-start
  70.1 0.8 collective-permute-start.1
  70.9 0.9 collective-permute-start.2
  71.7 1.8 %collective-permute-start.3 = (bf16[1024,384]{1,0:T(8,128)(2,1)S(1)}, bf16[1024,384]{1,0:T(8,128)(2,1)S(1)}, u32[]{:S(2)}, u32[]{:S(2)}) collective-permute-start(bf16[1024,384]{1,0:T(8,128)(2,1)S(1)} %stack.133.refs_0_.refs_8_), channel_id=1, source_target_pairs={{0,48},{16,0},{32,16},{48,32},{1,49},{17,1},{33,17},{49,33},{2,50}... | collective-permute-start | bytes 2359304 | tf_op jit(solution)/shard_map/ppermute | solution.py:365
  73.5 1.1 collective-permute-start
  74.6 1.6 collective-permute-start.4
  76.2 11.9 %collective-permute-done.1.refs_10_ = bf16[1024,384]{1,0:T(8,128)(2,1)S(1)} collective-permute-done((bf16[1024,384]{1,0:T(8,128)(2,1)S(1)}, bf16[1024,384]{1,0:T(8,128)(2,1)S(1)}, u32[]{:S(2)}, u32[]{:S(2)}) %collective-permute-start.1) | collective-permute-done | bytes 786464 | tf_op jit(solution)/shard_map/ppermute | solution.py:365
  88.1 0.0 copy-start.1
  88.1 1.7 %collective-permute-done.2.refs_9_ = bf16[1024,384]{1,0:T(8,128)(2,1)S(1)} collective-permute-done((bf16[1024,384]{1,0:T(8,128)(2,1)S(1)}, bf16[1024,384]{1,0:T(8,128)(2,1)S(1)}, u32[]{:S(2)}, u32[]{:S(2)}) %collective-permute-start.2) | collective-permute-done | bytes 786464 | tf_op jit(solution)/shard_map/ppermute | solution.py:365
  89.8 0.0 copy-start.2
  89.8 0.0 collective-permute-done.3.refs_12_
  89.8 0.0 copy-start.3
  89.8 0.5 pad_maximum_fusion
  90.3 0.4 copy-done.3
  90.7 0.2 collective-permute-done.refs_2_
  90.9 0.0 copy-start.8
  90.9 0.8 collective-permute-done.4.refs_4_
  91.7 0.0 copy-start.9
  91.7 3.0 %collective-permute-start.9 = (bf16[4,1024,384]{2,1,0:T(8,128)(2,1)S(1)}, bf16[4,1024,384]{2,1,0:T(8,128)(2,1)S(1)}, u32[]{:S(2)}, u32[]{:S(2)}) collective-permute-start(bf16[4,1024,384]{2,1,0:T(8,128)(2,1)S(1)} %pad_maximum_fusion), channel_id=1, source_target_pairs={{0,8},{8,0},{1,9},{9,1},{2,10},{10,2},{3,11},{11,3},{4,12},{12,4},... | collective-permute-start | bytes 9437192 | tf_op jit(solution)/shard_map/ppermute | solution.py:365
  94.7 0.0 copy-done
  94.7 0.7 collective-permute-start.5
  95.5 0.9 collective-permute-start.6
  96.4 0.0 copy-done.9
  96.4 0.9 collective-permute-start.7
  97.3 0.0 copy-done.1
  97.3 0.4 collective-permute-start.8
  97.7 16.1 %collective-permute-done.5.refs_1_ = bf16[1024,384]{1,0:T(8,128)(2,1)S(1)} collective-permute-done((bf16[1024,384]{1,0:T(8,128)(2,1)S(1)}, bf16[1024,384]{1,0:T(8,128)(2,1)S(1)}, u32[]{:S(2)}, u32[]{:S(2)}) %collective-permute-start.5) | collective-permute-done | bytes 786464 | tf_op jit(solution)/shard_map/ppermute | solution.py:365
  113.9 0.4 collective-permute-done.6.refs_13_
  114.2 1.8 %collective-permute-done.7.refs_6_ = bf16[1024,384]{1,0:T(8,128)(2,1)S(1)} collective-permute-done((bf16[1024,384]{1,0:T(8,128)(2,1)S(1)}, bf16[1024,384]{1,0:T(8,128)(2,1)S(1)}, u32[]{:S(2)}, u32[]{:S(2)}) %collective-permute-start.7) | collective-permute-done | bytes 786464 | tf_op jit(solution)/shard_map/ppermute | solution.py:365
  116.1 0.6 collective-permute-done.8.refs_14_
  116.7 0.0 collective-permute-done.9.refs_16_
  116.7 1.2 collective-permute-start.10
  117.9 1.6 collective-permute-start.11
  119.4 0.9 collective-permute-start.12
  120.3 0.0 copy-done.2
  120.4 0.0 collective-permute-start.13
  120.4 0.0 copy-done.6
  120.4 2.7 %collective-permute-start.14 = (bf16[1024,384]{1,0:T(8,128)(2,1)S(1)}, bf16[1024,384]{1,0:T(8,128)(2,1)}, u32[]{:S(2)}, u32[]{:S(2)}) collective-permute-start(bf16[1024,384]{1,0:T(8,128)(2,1)S(1)} %collective-permute-done.6.refs_13_), channel_id=1, source_target_pairs={{0,48},{16,0},{32,16},{48,32},{1,49},{17,1},{33,17},{49,33},{2,50}... | collective-permute-start | bytes 2359304 | tf_op jit(solution)/shard_map/ppermute | solution.py:365
  123.0 1.3 pad_maximum_fusion.1
  124.4 10.9 %collective-permute-done.10.refs_3_ = bf16[1024,384]{1,0:T(8,128)(2,1)S(1)} collective-permute-done((bf16[1024,384]{1,0:T(8,128)(2,1)S(1)}, bf16[1024,384]{1,0:T(8,128)(2,1)S(1)}, u32[]{:S(2)}, u32[]{:S(2)}) %collective-permute-start.10) | collective-permute-done | bytes 786464 | tf_op jit(solution)/shard_map/ppermute | solution.py:365
  135.3 0.0 collective-permute-done.11.refs_5_
  135.3 0.9 collective-permute-done.12.refs_7_
  136.2 1.8 %collective-permute-done.13.refs_11_ = bf16[1024,384]{1,0:T(8,128)(2,1)} collective-permute-done((bf16[1024,384]{1,0:T(8,128)(2,1)S(1)}, bf16[1024,384]{1,0:T(8,128)(2,1)}, u32[]{:S(2)}, u32[]{:S(2)}) %collective-permute-start.13) | collective-permute-done | bytes 786464 | tf_op jit(solution)/shard_map/ppermute | solution.py:365
  138.0 0.0 collective-permute-done.14.refs_15_
  138.0 0.0 copy-done.5
  138.0 3.6 %collective-permute-start.15 = (bf16[2,1024,384]{2,1,0:T(8,128)(2,1)}, bf16[2,1024,384]{2,1,0:T(8,128)(2,1)S(1)}, u32[]{:S(2)}, u32[]{:S(2)}) collective-permute-start(bf16[2,1024,384]{2,1,0:T(8,128)(2,1)} %pad_maximum_fusion.1), channel_id=1, source_target_pairs={{0,8},{8,0},{1,9},{9,1},{2,10},{10,2},{3,11},{11,3},{4,12},{12,4},... | collective-permute-start | bytes 4718600 | tf_op jit(solution)/shard_map/ppermute | solution.py:365
  141.6 0.0 copy-done.10
  141.6 0.1 collective-permute-start.16
  141.7 0.0 copy-done.11
  141.7 0.4 collective-permute-start.17
  142.1 0.0 copy-done.12
  142.2 0.0 copy-done.13
  142.2 0.0 copy-done.14
  142.2 0.6 stack.124.places
  142.8 3.2 %collective-permute-done.16.refs_18_ = bf16[1024,384]{1,0:T(8,128)(2,1)} collective-permute-done((bf16[1024,384]{1,0:T(8,128)(2,1)}, bf16[1024,384]{1,0:T(8,128)(2,1)}, u32[]{:S(2)}, u32[]{:S(2)}) %collective-permute-start.16) | collective-permute-done | bytes 786464 | tf_op jit(solution)/shard_map/ppermute | solution.py:365
  146.0 1.3 collective-permute-done.17.refs_19_
  147.3 0.0 collective-permute-done.15.refs_17_
  147.3 0.0 copy-done.8
  147.3 0.0 copy-done.4
  147.3 1.2 copy-done.7
  148.4 19.2 %cross.1 = bf16[64,128,512]{2,1,0:T(8,128)(2,1)} custom-call(s32[24]{0:T(128)} %stack.124.places, bf16[1024,384]{1,0:T(8,128)(2,1)} %copy-done, bf16[1024,384]{1,0:T(8,128)(2,1)} %copy-done.10, bf16[1024,384]{1,0:T(8,128)(2,1)} %copy-done.8, bf16[1024,384]{1,0:T(8,128)(2,1)} %copy-done.12, bf16[1024,384]{1,0:T(8,128)(2,1)} %copy-done.9, ...), custom_call_target="tpu_custom_call" | custom-call | flops 3221225472 | bytes 14680064 | tf_op jit(solution)/shard_map/cross/pallas_call | solution.py:332
  (9 shorter events, 0.0 us)
Async XLA Ops:
  70.0 24.7 %copy-start = (bf16[1024,384]{1,0:T(8,128)(2,1)}, bf16[1024,384]{1,0:T(8,128)(2,1)S(1)}, u32[]{:S(2)}) copy-start(bf16[1024,384]{1,0:T(8,128)(2,1)S(1)} %stack.133.refs_0_.refs_8_) | copy-start | bytes 2359300
  70.1 18.0 %collective-permute-start.1 = (bf16[1024,384]{1,0:T(8,128)(2,1)S(1)}, bf16[1024,384]{1,0:T(8,128)(2,1)S(1)}, u32[]{:S(2)}, u32[]{:S(2)}) collective-permute-start(bf16[1024,384]{1,0:T(8,128)(2,1)S(1)} %stack.133.refs_0_.refs_8_), channel_id=1, source_target_pairs={{0,16},{16,32},{32,48},{48,0},{1,17},{17,33},{33,49},{49,1},{2,18}... | collective-permute-start | bytes 2359304 | tf_op jit(solution)/shard_map/ppermute | solution.py:365
  70.9 18.9 %collective-permute-start.2 = (bf16[1024,384]{1,0:T(8,128)(2,1)S(1)}, bf16[1024,384]{1,0:T(8,128)(2,1)S(1)}, u32[]{:S(2)}, u32[]{:S(2)}) collective-permute-start(bf16[1024,384]{1,0:T(8,128)(2,1)S(1)} %stack.133.refs_0_.refs_8_), channel_id=1, source_target_pairs={{0,64},{64,0},{1,65},{65,1},{2,66},{66,2},{3,67},{67,3},{4,68},{68... | collective-permute-start | bytes 2359304 | tf_op jit(solution)/shard_map/ppermute | solution.py:365
  71.7 18.0 %collective-permute-start.3 = (bf16[1024,384]{1,0:T(8,128)(2,1)S(1)}, bf16[1024,384]{1,0:T(8,128)(2,1)S(1)}, u32[]{:S(2)}, u32[]{:S(2)}) collective-permute-start(bf16[1024,384]{1,0:T(8,128)(2,1)S(1)} %stack.133.refs_0_.refs_8_), channel_id=1, source_target_pairs={{0,48},{16,0},{32,16},{48,32},{1,49},{17,1},{33,17},{49,33},{2,50}... | collective-permute-start | bytes 2359304 | tf_op jit(solution)/shard_map/ppermute | solution.py:365
  73.5 17.4 %collective-permute-start = (bf16[1024,384]{1,0:T(8,128)(2,1)S(1)}, bf16[1024,384]{1,0:T(8,128)(2,1)S(1)}, u32[]{:S(2)}, u32[]{:S(2)}) collective-permute-start(bf16[1024,384]{1,0:T(8,128)(2,1)S(1)} %stack.133.refs_0_.refs_8_), channel_id=1, source_target_pairs={{0,2},{2,4},{4,6},{6,0},{1,3},{3,5},{5,7},{7,1},{8,10},{10,12},{12... | collective-permute-start | bytes 2359304 | tf_op jit(solution)/shard_map/ppermute | solution.py:365
  74.6 17.1 %collective-permute-start.4 = (bf16[1024,384]{1,0:T(8,128)(2,1)S(1)}, bf16[1024,384]{1,0:T(8,128)(2,1)S(1)}, u32[]{:S(2)}, u32[]{:S(2)}) collective-permute-start(bf16[1024,384]{1,0:T(8,128)(2,1)S(1)} %stack.133.refs_0_.refs_8_), channel_id=1, source_target_pairs={{0,6},{2,0},{4,2},{6,4},{1,7},{3,1},{5,3},{7,5},{8,14},{10,8},{12,... | collective-permute-start | bytes 2359304 | tf_op jit(solution)/shard_map/ppermute | solution.py:365
  88.1 9.3 %copy-start.1 = (bf16[1024,384]{1,0:T(8,128)(2,1)}, bf16[1024,384]{1,0:T(8,128)(2,1)S(1)}, u32[]{:S(2)}) copy-start(bf16[1024,384]{1,0:T(8,128)(2,1)S(1)} %collective-permute-done.1.refs_10_) | copy-start | bytes 2359300
  89.8 30.6 %copy-start.2 = (bf16[1024,384]{1,0:T(8,128)(2,1)}, bf16[1024,384]{1,0:T(8,128)(2,1)S(1)}, u32[]{:S(2)}) copy-start(bf16[1024,384]{1,0:T(8,128)(2,1)S(1)} %collective-permute-done.2.refs_9_) | copy-start | bytes 2359300
  89.8 0.9 copy-start.3
  90.9 56.4 %copy-start.8 = (bf16[1024,384]{1,0:T(8,128)(2,1)}, bf16[1024,384]{1,0:T(8,128)(2,1)S(1)}, u32[]{:S(2)}) copy-start(bf16[1024,384]{1,0:T(8,128)(2,1)S(1)} %collective-permute-done.refs_2_) | copy-start | bytes 2359300
  91.7 4.7 %copy-start.9 = (bf16[1024,384]{1,0:T(8,128)(2,1)}, bf16[1024,384]{1,0:T(8,128)(2,1)S(1)}, u32[]{:S(2)}) copy-start(bf16[1024,384]{1,0:T(8,128)(2,1)S(1)} %collective-permute-done.4.refs_4_) | copy-start | bytes 2359300
  91.7 25.0 %collective-permute-start.9 = (bf16[4,1024,384]{2,1,0:T(8,128)(2,1)S(1)}, bf16[4,1024,384]{2,1,0:T(8,128)(2,1)S(1)}, u32[]{:S(2)}, u32[]{:S(2)}) collective-permute-start(bf16[4,1024,384]{2,1,0:T(8,128)(2,1)S(1)} %pad_maximum_fusion), channel_id=1, source_target_pairs={{0,8},{8,0},{1,9},{9,1},{2,10},{10,2},{3,11},{11,3},{4,12},{12,4},... | collective-permute-start | bytes 9437192 | tf_op jit(solution)/shard_map/ppermute | solution.py:365
  94.7 19.1 %collective-permute-start.5 = (bf16[1024,384]{1,0:T(8,128)(2,1)S(1)}, bf16[1024,384]{1,0:T(8,128)(2,1)S(1)}, u32[]{:S(2)}, u32[]{:S(2)}) collective-permute-start(bf16[1024,384]{1,0:T(8,128)(2,1)S(1)} %stack.133.refs_0_.refs_8_), channel_id=1, source_target_pairs={{0,1},{1,0},{2,3},{3,2},{4,5},{5,4},{6,7},{7,6},{8,9},{9,8},{10,11... | collective-permute-start | bytes 2359304 | tf_op jit(solution)/shard_map/ppermute | solution.py:365
  95.5 18.8 %collective-permute-start.6 = (bf16[1024,384]{1,0:T(8,128)(2,1)S(1)}, bf16[1024,384]{1,0:T(8,128)(2,1)S(1)}, u32[]{:S(2)}, u32[]{:S(2)}) collective-permute-start(bf16[1024,384]{1,0:T(8,128)(2,1)S(1)} %collective-permute-done.2.refs_9_), channel_id=1, source_target_pairs={{0,48},{16,0},{32,16},{48,32},{1,49},{17,1},{33,17},{49,33},{2,50}... | collective-permute-start | bytes 2359304 | tf_op jit(solution)/shard_map/ppermute | solution.py:365
  96.4 19.7 %collective-permute-start.7 = (bf16[1024,384]{1,0:T(8,128)(2,1)S(1)}, bf16[1024,384]{1,0:T(8,128)(2,1)S(1)}, u32[]{:S(2)}, u32[]{:S(2)}) collective-permute-start(bf16[1024,384]{1,0:T(8,128)(2,1)S(1)} %collective-permute-done.refs_2_), channel_id=1, source_target_pairs={{0,2},{2,4},{4,6},{6,0},{1,3},{3,5},{5,7},{7,1},{8,10},{10,12},{12... | collective-permute-start | bytes 2359304 | tf_op jit(solution)/shard_map/ppermute | solution.py:365
  97.3 19.3 %collective-permute-start.8 = (bf16[1024,384]{1,0:T(8,128)(2,1)S(1)}, bf16[1024,384]{1,0:T(8,128)(2,1)S(1)}, u32[]{:S(2)}, u32[]{:S(2)}) collective-permute-start(bf16[1024,384]{1,0:T(8,128)(2,1)S(1)} %collective-permute-done.1.refs_10_), channel_id=1, source_target_pairs={{0,16},{16,32},{32,48},{48,0},{1,17},{17,33},{33,49},{49,1},{2,18}... | collective-permute-start | bytes 2359304 | tf_op jit(solution)/shard_map/ppermute | solution.py:365
  113.8 27.8 %copy-start.10 = (bf16[1024,384]{1,0:T(8,128)(2,1)}, bf16[1024,384]{1,0:T(8,128)(2,1)S(1)}, u32[]{:S(2)}) copy-start(bf16[1024,384]{1,0:T(8,128)(2,1)S(1)} %collective-permute-done.5.refs_1_) | copy-start | bytes 2359300
  114.2 33.0 %copy-start.4 = (bf16[1024,384]{1,0:T(8,128)(2,1)}, bf16[1024,384]{1,0:T(8,128)(2,1)S(1)}, u32[]{:S(2)}) copy-start(bf16[1024,384]{1,0:T(8,128)(2,1)S(1)} %collective-permute-done.6.refs_13_) | copy-start | bytes 2359300
  116.1 25.7 %copy-start.11 = (bf16[1024,384]{1,0:T(8,128)(2,1)}, bf16[1024,384]{1,0:T(8,128)(2,1)S(1)}, u32[]{:S(2)}) copy-start(bf16[1024,384]{1,0:T(8,128)(2,1)S(1)} %collective-permute-done.7.refs_6_) | copy-start | bytes 2359300
  116.7 21.4 %copy-start.5 = (bf16[1024,384]{1,0:T(8,128)(2,1)}, bf16[1024,384]{1,0:T(8,128)(2,1)S(1)}, u32[]{:S(2)}) copy-start(bf16[1024,384]{1,0:T(8,128)(2,1)S(1)} %collective-permute-done.8.refs_14_) | copy-start | bytes 2359300
  116.7 3.7 %copy-start.6 = (bf16[4,1024,384]{2,1,0:T(8,128)(2,1)}, bf16[4,1024,384]{2,1,0:T(8,128)(2,1)S(1)}, u32[]{:S(2)}) copy-start(bf16[4,1024,384]{2,1,0:T(8,128)(2,1)S(1)} %collective-permute-done.9.refs_16_) | copy-start | bytes 9437188
  116.7 18.6 %collective-permute-start.10 = (bf16[1024,384]{1,0:T(8,128)(2,1)S(1)}, bf16[1024,384]{1,0:T(8,128)(2,1)S(1)}, u32[]{:S(2)}, u32[]{:S(2)}) collective-permute-start(bf16[1024,384]{1,0:T(8,128)(2,1)S(1)} %collective-permute-done.5.refs_1_), channel_id=1, source_target_pairs={{0,2},{2,4},{4,6},{6,0},{1,3},{3,5},{5,7},{7,1},{8,10},{10,12},{12... | collective-permute-start | bytes 2359304 | tf_op jit(solution)/shard_map/ppermute | solution.py:365
  117.9 17.4 %collective-permute-start.11 = (bf16[1024,384]{1,0:T(8,128)(2,1)S(1)}, bf16[1024,384]{1,0:T(8,128)(2,1)S(1)}, u32[]{:S(2)}, u32[]{:S(2)}) collective-permute-start(bf16[1024,384]{1,0:T(8,128)(2,1)S(1)} %collective-permute-done.5.refs_1_), channel_id=1, source_target_pairs={{0,6},{2,0},{4,2},{6,4},{1,7},{3,1},{5,3},{7,5},{8,14},{10,8},{12,... | collective-permute-start | bytes 2359304 | tf_op jit(solution)/shard_map/ppermute | solution.py:365
  119.4 16.8 %collective-permute-start.12 = (bf16[1024,384]{1,0:T(8,128)(2,1)S(1)}, bf16[1024,384]{1,0:T(8,128)(2,1)S(1)}, u32[]{:S(2)}, u32[]{:S(2)}) collective-permute-start(bf16[1024,384]{1,0:T(8,128)(2,1)S(1)} %collective-permute-done.7.refs_6_), channel_id=1, source_target_pairs={{0,1},{1,0},{2,3},{3,2},{4,5},{5,4},{6,7},{7,6},{8,9},{9,8},{10,11... | collective-permute-start | bytes 2359304 | tf_op jit(solution)/shard_map/ppermute | solution.py:365
  120.4 17.7 %collective-permute-start.13 = (bf16[1024,384]{1,0:T(8,128)(2,1)S(1)}, bf16[1024,384]{1,0:T(8,128)(2,1)}, u32[]{:S(2)}, u32[]{:S(2)}) collective-permute-start(bf16[1024,384]{1,0:T(8,128)(2,1)S(1)} %collective-permute-done.2.refs_9_), channel_id=1, source_target_pairs={{0,16},{16,32},{32,48},{48,0},{1,17},{17,33},{33,49},{49,1},{2,18}... | collective-permute-start | bytes 2359304 | tf_op jit(solution)/shard_map/ppermute | solution.py:365
  120.4 17.7 %collective-permute-start.14 = (bf16[1024,384]{1,0:T(8,128)(2,1)S(1)}, bf16[1024,384]{1,0:T(8,128)(2,1)}, u32[]{:S(2)}, u32[]{:S(2)}) collective-permute-start(bf16[1024,384]{1,0:T(8,128)(2,1)S(1)} %collective-permute-done.6.refs_13_), channel_id=1, source_target_pairs={{0,48},{16,0},{32,16},{48,32},{1,49},{17,1},{33,17},{49,33},{2,50}... | collective-permute-start | bytes 2359304 | tf_op jit(solution)/shard_map/ppermute | solution.py:365
  135.3 6.9 %copy-start.12 = (bf16[1024,384]{1,0:T(8,128)(2,1)}, bf16[1024,384]{1,0:T(8,128)(2,1)S(1)}, u32[]{:S(2)}) copy-start(bf16[1024,384]{1,0:T(8,128)(2,1)S(1)} %collective-permute-done.10.refs_3_) | copy-start | bytes 2359300
  135.3 6.9 %copy-start.13 = (bf16[1024,384]{1,0:T(8,128)(2,1)}, bf16[1024,384]{1,0:T(8,128)(2,1)S(1)}, u32[]{:S(2)}) copy-start(bf16[1024,384]{1,0:T(8,128)(2,1)S(1)} %collective-permute-done.11.refs_5_) | copy-start | bytes 2359300
  136.2 6.0 %copy-start.14 = (bf16[1024,384]{1,0:T(8,128)(2,1)}, bf16[1024,384]{1,0:T(8,128)(2,1)S(1)}, u32[]{:S(2)}) copy-start(bf16[1024,384]{1,0:T(8,128)(2,1)S(1)} %collective-permute-done.12.refs_7_) | copy-start | bytes 2359300
  138.0 9.2 %collective-permute-start.15 = (bf16[2,1024,384]{2,1,0:T(8,128)(2,1)}, bf16[2,1024,384]{2,1,0:T(8,128)(2,1)S(1)}, u32[]{:S(2)}, u32[]{:S(2)}) collective-permute-start(bf16[2,1024,384]{2,1,0:T(8,128)(2,1)} %pad_maximum_fusion.1), channel_id=1, source_target_pairs={{0,8},{8,0},{1,9},{9,1},{2,10},{10,2},{3,11},{11,3},{4,12},{12,4},... | collective-permute-start | bytes 4718600 | tf_op jit(solution)/shard_map/ppermute | solution.py:365
  141.6 4.4 %collective-permute-start.16 = (bf16[1024,384]{1,0:T(8,128)(2,1)}, bf16[1024,384]{1,0:T(8,128)(2,1)}, u32[]{:S(2)}, u32[]{:S(2)}) collective-permute-start(bf16[1024,384]{1,0:T(8,128)(2,1)} %collective-permute-done.13.refs_11_), channel_id=1, source_target_pairs={{0,8},{8,0},{1,9},{9,1},{2,10},{10,2},{3,11},{11,3},{4,12},{12,4},... | collective-permute-start | bytes 2359304 | tf_op jit(solution)/shard_map/ppermute | solution.py:365
  141.7 5.5 %collective-permute-start.17 = (bf16[1024,384]{1,0:T(8,128)(2,1)}, bf16[1024,384]{1,0:T(8,128)(2,1)}, u32[]{:S(2)}, u32[]{:S(2)}) collective-permute-start(bf16[1024,384]{1,0:T(8,128)(2,1)} %collective-permute-done.14.refs_15_), channel_id=1, source_target_pairs={{0,8},{8,0},{1,9},{9,1},{2,10},{10,2},{3,11},{11,3},{4,12},{12,4},... | collective-permute-start | bytes 2359304 | tf_op jit(solution)/shard_map/ppermute | solution.py:365
  147.3 1.2 copy-start.7

commit v3 on v2

--- a/solution.py
+++ b/solution.py
@@ -20,7 +20,7 @@
 AXES = ("zh", "y", "core", "x", "zl")
 DEVICES = 128
 SEGS = 512
-STEP = 1024
+STEP = 2048
 STEPS = L // STEP
 PAIRS = 64
 WIDE = 4 * HOURS
@@ -76,7 +76,6 @@
         count = count.astype(F32)
         below = sums + count * EPS
         inverse = pl.reciprocal(below, approx=True)
-        inverse = inverse * (2.0 - below * inverse)
         values = main[:, part * 256 : part * 256 + 256].astype(F32)
         normal[:, part * 256 : part * 256 + 256] = (values * (count * inverse)).astype(BF16)
     total[...] += jnp.dot(normal[...], table[...], preferred_element_type=F32)
@@ -99,7 +98,7 @@
         hour = slots - station * HOURS
         whole = owner_col * ST_DEV + station
         hits = whole == iota((1, DEVICES * ST_DEV), 1)
-        widths = jnp.sum(jnp.where(hits, width_row[...], 0).astype(F32), axis=1, keepdims=True)
+        widths = jnp.sum(jnp.where(hits, width_row[...].astype(F32), 0.0), axis=1, keepdims=True)
         widths = widths.astype(jnp.int32)
         real = total[:, :NBAND] * (1.0 / math.sqrt(L))
         imag = total[:, NBAND:] * (1.0 / math.sqrt(L))
@@ -182,43 +181,47 @@
 
 
 def stack_kernel(received, spectra, wide):
-    half = pl.program_id(0)
     tags = received[:, 4 * CAP :, :].astype(F32)
     tags = jnp.concatenate([tags, pltpu.roll(tags, 64, 2)], axis=1).reshape(DEVICES * CAP, 128)
     column = (tags[:, 0:1] * 128.0 + tags[:, 1:2] + (tags[:, 2:3] - 1.0)).astype(jnp.int32)
-    total = jnp.zeros((256, ST_DEV * 128), F32)
+    total = None
     block = 512
-    at = pl.multiple_of(half * CAP, CAP)
     for part in range(DEVICES * CAP // block):
         sources = slice(part * block // CAP, (part + 1) * block // CAP)
         hits = column[part * block : (part + 1) * block] == iota((1, ST_DEV * 128), 1)
         hits = jnp.where(hits, 1.0, 0.0).astype(BF16)
-        real = received[sources, pl.ds(at, CAP), :].reshape(block, 128)
-        imag = received[sources, pl.ds(at + 2 * CAP, CAP), :].reshape(block, 128)
-        both = jnp.concatenate([real, imag], axis=1)
-        total += lax.dot_general(both, hits, (((0,), (0,)), ((), ())), preferred_element_type=F32)
+        values = jnp.concatenate(
+            [
+                received[sources, tile * CAP : tile * CAP + CAP, :].reshape(block, 128)
+                for tile in range(4)
+            ],
+            axis=1,
+        )
+        term = lax.dot_general(values, hits, (((0,), (0,)), ((), ())), preferred_element_type=F32)
+        total = term if total is None else total + term
     lane = iota((PAIRS, 128), 1)
-    for station in range(ST_DEV):
-        lanes = slice(station * 128, station * 128 + 128)
-        real_first = total[0:64, lanes]
-        real_second = pltpu.roll(total[64:128, lanes], 64, 1)
-        imag_first = pltpu.roll(total[128:192, lanes], 96, 1)
-        imag_second = pltpu.roll(total[192:256, lanes], 32, 1)
-        wide[:, station, 0:128] = jnp.where(lane < 96, real_first, imag_first)
-        wide[:, station, 128:256] = jnp.where(lane < 64, imag_first, real_second)
-        wide[:, station, 256:384] = jnp.where(lane < 32, real_second, imag_second)
-    spectra[...] = wide[...].reshape(PAIRS * ST_DEV, WIDE).astype(BF16)
+    for half in range(2):
+        rows = half * 128
+        for station in range(ST_DEV):
+            lanes = slice(station * 128, station * 128 + 128)
+            real_first = total[rows : rows + 64, lanes]
+            real_second = pltpu.roll(total[rows + 64 : rows + 128, lanes], 64, 1)
+            imag_first = pltpu.roll(total[rows + 256 : rows + 320, lanes], 96, 1)
+            imag_second = pltpu.roll(total[rows + 320 : rows + 384, lanes], 32, 1)
+            wide[:, station, 0:128] = jnp.where(lane < 96, real_first, imag_first)
+            wide[:, station, 128:256] = jnp.where(lane < 64, imag_first, real_second)
+            wide[:, station, 256:384] = jnp.where(lane < 32, real_second, imag_second)
+        spectra[half * PAIRS * ST_DEV : (half + 1) * PAIRS * ST_DEV] = (
+            wide[...].reshape(PAIRS * ST_DEV, WIDE).astype(BF16)
+        )
 
 
 def stack(received):
     return pl.pallas_call(
         stack_kernel,
-        grid=(2,),
-        in_specs=[pl.BlockSpec((DEVICES, TAGGED, 128), lambda k: (0, 0, 0))],
-        out_specs=pl.BlockSpec((PAIRS * ST_DEV, WIDE), lambda k: (k, 0)),
         out_shape=jax.ShapeDtypeStruct((2 * PAIRS * ST_DEV, WIDE), BF16),
         scratch_shapes=[pltpu.VMEM((PAIRS, ST_DEV, WIDE), F32)],
-        compiler_params=pltpu.CompilerParams(vmem_limit_bytes=20 << 20),
+        compiler_params=pltpu.CompilerParams(vmem_limit_bytes=40 << 20),
         cost_estimate=pl.CostEstimate(
             flops=2 * 2048 * 1024 * 256 * 2, bytes_accessed=3 << 20, transcendentals=0
         ),
@@ -263,19 +266,19 @@
             for copy in copies(block):
                 copy.start()
 
+        for part in range(2):
+            source = iota((256, 256), 0) + part * 128
+            target = iota((256, 256), 1) + part * 128
+            mine = target // (2 * HOURS) == part
+            group = (target // HOURS) % 2
+            ahead = mine & (source == target + HOURS) & (group == 0)
+            behind = mine & (source == target - HOURS) & (group == 1)
+            swap[part] = (jnp.where(ahead, 1.0, 0.0) - jnp.where(behind, 1.0, 0.0)).astype(BF16)
+
     @pl.when(step < 2 * BLOCKS)
     def _():
         for copy in copies(step):
             copy.wait()
-
-    @pl.when(step == 0)
-    def _():
-        source = iota((WIDE, WIDE), 0)
-        target = iota((WIDE, WIDE), 1)
-        group = (target // HOURS) % 2
-        ahead = (source == target + HOURS) & (group == 0)
-        behind = (source == target - HOURS) & (group == 1)
-        swap[...] = (jnp.where(ahead, 1.0, 0.0) - jnp.where(behind, 1.0, 0.0)).astype(BF16)
 
     @pl.when(step < 2 * BLOCKS)
     def _():
@@ -291,11 +294,13 @@
                     both, axis=1
                 ).astype(BF16)
         plain = left[...].reshape(BLOCK * 64, WIDE)
-        swapped[...] = (
-            jnp.dot(plain, swap[...], preferred_element_type=F32)
-            .astype(BF16)
-            .reshape(BLOCK, 64, WIDE)
-        )
+        for part in range(2):
+            lanes = slice(part * 128, part * 128 + 256)
+            swapped[part] = (
+                jnp.dot(plain[:, lanes], swap[part], preferred_element_type=F32)
+                .astype(BF16)
+                .reshape(BLOCK, 64, 256)
+            )
         lane = iota((1, 256), 1)
         first_mask = jnp.where(lane < 2 * HOURS, 1.0, 0.0).astype(BF16)
         second_mask = jnp.where(lane >= 2 * HOURS - 128, 1.0, 0.0).astype(BF16)
@@ -304,11 +309,9 @@
         def _(pair):
             for part, mask in ((0, first_mask), (1, second_mask)):
                 lanes = slice(part * 128, part * 128 + 256)
-                rows = jnp.concatenate(
-                    [left[pair, :, lanes], swapped[pair, :, lanes]], axis=0
-                )
+                rows = jnp.concatenate([left[pair, :, lanes] * mask, swapped[part, pair]], axis=0)
                 product = lax.dot_general(
-                    rows * mask,
+                    rows,
                     right[pair, :, lanes],
                     (((1,), (1,)), ((), ())),
                     preferred_element_type=F32,
@@ -342,8 +345,8 @@
             pltpu.VMEM((16, 2 * PAIRS * ST_DEV, WIDE), BF16),
             pltpu.VMEM((BLOCK, 64, WIDE), BF16),
             pltpu.VMEM((BLOCK, 128, WIDE), BF16),
-            pltpu.VMEM((BLOCK, 64, WIDE), BF16),
-            pltpu.VMEM((WIDE, WIDE), BF16),
+            pltpu.VMEM((2, BLOCK, 64, 256), BF16),
+            pltpu.VMEM((2, 256, 256), BF16),
             pltpu.VMEM((128 * STRIDE, 128), F32),
             pltpu.SemaphoreType.DMA((2 * BLOCKS, 24)),
         ],
@@ -359,32 +362,27 @@
     return [(i, (i + shift) % size) for i in range(size)]
 
 
-def turn(moves, *others):
-    arrays = [move[0] for move in moves]
-    arrays = lax.optimization_barrier(tuple(arrays) + others)[: len(moves)]
-    return [lax.ppermute(array, axis, pairs) for array, (_, axis, pairs) in zip(arrays, moves)]
+def move(array, axis, pairs, *others):
+    return lax.ppermute(lax.optimization_barrier((array,) + others)[0], axis, pairs)
 
 
 UP, DOWN, SWAP = ring(4, 1), ring(4, 3), [(0, 1), (1, 0)]
 
 
 def gather(own):
-    lx, rx, ly, ry, q = turn(
-        [(own, "x", UP), (own, "x", DOWN), (own, "y", UP), (own, "y", DOWN), (own, "zh", SWAP)]
-    )
-    early = jnp.stack([own, q, ly, ry])
-    fx, fy, rq, p, s_early = turn(
-        [(lx, "x", UP), (ly, "y", UP), (q, "y", DOWN), (own, "zl", SWAP), (early, "core", SWAP)],
-        rx,
-    )
-    late = jnp.stack([fy, rq])
-    lp, rp, lq, gq, gp = turn(
-        [(p, "x", UP), (p, "x", DOWN), (q, "y", UP), (rq, "y", DOWN), (fx, "zl", SWAP)],
-        fy, s_early,
-    )
-    s_late, s_lq, s_gq = turn(
-        [(late, "core", SWAP), (lq, "core", SWAP), (gq, "core", SWAP)], lp, rp, gp
-    )
+    q = move(own, "zh", SWAP)
+    lx, rx = move(own, "x", UP), move(own, "x", DOWN)
+    ly, ry = move(own, "y", UP), move(own, "y", DOWN)
+    p = move(own, "zl", SWAP, ly, ry)
+    fx = move(lx, "x", UP, rx)
+    fy, rq = move(ly, "y", UP, ry), move(q, "y", DOWN, ry)
+    s_early = move(jnp.stack([own, q, ly, ry]), "core", SWAP, lx, rx)
+    lp, rp = move(p, "x", UP, fx), move(p, "x", DOWN, fx)
+    lq, gq = move(q, "y", UP, fy, rq), move(rq, "y", DOWN, fy)
+    gp = move(fx, "zl", SWAP, p, s_early)
+    s_late = move(jnp.stack([fy, rq]), "core", SWAP, s_early, lp, rp)
+    s_lq = move(lq, "core", SWAP, gp)
+    s_gq = move(gq, "core", SWAP, gp)
     rows = [own, p, lx, lp, rx, rp, fx, gp]
     columns = [own, q, ly, lq, ry, rq, fy, gq, s_early, s_late, s_lq, s_gq]
     return rows, columns

time: 168 us -> 160 us (0.952)
  Pallas kernels: 46.2 us -> 41.1 us
  starting transfers between devices: 22.5 us -> 18.3 us
    ppermute x18, starting transfers between devices: 22.5 us -> 18.3 us  [move(): lax.ppermute(lax.optimization_barrier((array,) + others)[0], axis, pairs)]
    pallas_call x1, Pallas kernels: 22 us -> 19.3 us  [transform(): pl.pallas_call(transform_kernel, grid=(STEPS,), in_specs=[pl.BlockSpec((S...]
  transfers between devices with their start and end apart: 18 -> 18, of which waited for: 13 -> 9; matrix products, arithmetic and copies ran while one was open for 1% -> 2% of each run, Pallas kernels for 0% -> 0%
where the time goes in v3:
time: 160 us
  waiting for transfers between devices  53 us (33%)
  blocking collectives  43 us (27%)
  Pallas kernels  41.1 us (26%)
  starting transfers between devices  18.3 us (11%)
  local copies, waits for them, and re-layouts  1.93 us (1%)
  other arithmetic  1.83 us (1%)
    ppermute x18, waiting for transfers between devices, move(): lax.ppermute(lax.optimization_barrier((array,) + others)[0], axis, pairs)  53 us
    all_to_all x1, blocking collectives, on_device(): lax.all_to_all(send, AXES, split_axis=0, concat_axis=0, tiled=True)  43 us
    pallas_call x1, Pallas kernels, transform(): pl.pallas_call(transform_kernel, grid=(STEPS,), in_specs=[pl.BlockSpec((S...  19.3 us
    ppermute x18, starting transfers between devices, move(): lax.ppermute(lax.optimization_barrier((array,) + others)[0], axis, pairs)  18.3 us
    pallas_call x1, Pallas kernels, cross(): pl.pallas_call(cross_kernel, grid=(2 * BLOCKS + 64 // OUT_ROWS,), in_spec...  17.7 us
    pallas_call x1, Pallas kernels, stack(): pl.pallas_call(stack_kernel, out_shape=jax.ShapeDtypeStruct((2 * PAIRS *...  4.07 us
  transfers between devices with their start and end apart: 18, of which 9 were waited for; matrix products, arithmetic and copies ran while one was open for 2% of the time, Pallas kernels for 0%

profile of v3, /device:TPU:1, one launch (start us, length us, event | category | flops | bytes accessed | tf_op | source)
XLA Modules:
  0.0 159.7 jit_solution(4813823602745355694)
XLA Ops:
  0.0 19.3 %transform.1 = bf16[128,72,128]{2,1,0:T(8,128)(2,1)} custom-call(bf16[512,8192]{1,0:T(8,128)(2,1)} %after.1, bf16[512,8192]{1,0:T(8,128)(2,1)} %after.1, bf16[512,8192]{1,0:T(8,128)(2,1)} %after.1, s32[1,512]{1,0:T(1,128)} %bitcast.41, s32[1,512]{1,0:T(1,128)} %bitcast.42, s32[1,1024]{1,0:T(1,128)} %bitcast.40, s32[1,256]{1,0:T(1,128)} %bitcast.43), custom_call_target="tpu_custom_call" | custom-call | flops 21474836480 | bytes 8388608 | tf_op jit(solution)/shard_map/transform/pallas_call | solution.py:145
  19.3 43.0 %all_to_all.5.received = bf16[128,72,128]{2,1,0:T(8,128)(2,1)S(1)} all-to-all(bf16[128,72,128]{2,1,0:T(8,128)(2,1)} %transform.1), channel_id=1, replica_groups=mesh['zh'=2,'y'=4,'core'=2,'x'=4,'zl'=2] {'zh','y','core','x','zl'}, dimensions={0} | all-to-all | bytes 4718592 | tf_op jit(solution)/shard_map/all_to_all | solution.py:407
  62.3 4.1 %stack.133.refs_0_.refs_8_ = bf16[1024,384]{1,0:T(8,128)(2,1)S(1)} custom-call(bf16[128,72,128]{2,1,0:T(8,128)(2,1)S(1)} %all_to_all.5.received), custom_call_target="tpu_custom_call" | custom-call | flops 2147483648 | bytes 3145728 | tf_op jit(solution)/shard_map/stack/pallas_call | solution.py:220
  66.4 0.0 copy-start
  66.4 0.8 collective-permute-start.8
  67.2 2.0 %collective-permute-start.1 = (bf16[1024,384]{1,0:T(8,128)(2,1)S(1)}, bf16[1024,384]{1,0:T(8,128)(2,1)S(1)}, u32[]{:S(2)}, u32[]{:S(2)}) collective-permute-start(bf16[1024,384]{1,0:T(8,128)(2,1)S(1)} %stack.133.refs_0_.refs_8_), channel_id=1, source_target_pairs={{0,48},{16,0},{32,16},{48,32},{1,49},{17,1},{33,17},{49,33},{2,50}... | collective-permute-start | bytes 2359304 | tf_op jit(solution)/shard_map/ppermute | solution.py:366
  69.2 0.0 collective-permute-start
  69.2 1.8 %collective-permute-start.4 = (bf16[1024,384]{1,0:T(8,128)(2,1)S(1)}, bf16[1024,384]{1,0:T(8,128)(2,1)S(1)}, u32[]{:S(2)}, u32[]{:S(2)}) collective-permute-start(bf16[1024,384]{1,0:T(8,128)(2,1)S(1)} %stack.133.refs_0_.refs_8_), channel_id=1, source_target_pairs={{0,6},{2,0},{4,2},{6,4},{1,7},{3,1},{5,3},{7,5},{8,14},{10,8},{12,... | collective-permute-start | bytes 2359304 | tf_op jit(solution)/shard_map/ppermute | solution.py:366
  71.0 0.0 collective-permute-start.3
  71.0 13.7 %collective-permute-done.8.refs_9_ = bf16[1024,384]{1,0:T(8,128)(2,1)S(1)} collective-permute-done((bf16[1024,384]{1,0:T(8,128)(2,1)S(1)}, bf16[1024,384]{1,0:T(8,128)(2,1)S(1)}, u32[]{:S(2)}, u32[]{:S(2)}) %collective-permute-start.8) | collective-permute-done | bytes 786464 | tf_op jit(solution)/shard_map/ppermute | solution.py:366
  84.7 0.0 copy-start.1
  84.7 0.2 collective-permute-done.1.refs_12_
  84.9 0.0 copy-start.2
  84.9 3.1 %collective-permute-done.refs_10_ = bf16[1024,384]{1,0:T(8,128)(2,1)S(1)} collective-permute-done((bf16[1024,384]{1,0:T(8,128)(2,1)S(1)}, bf16[1024,384]{1,0:T(8,128)(2,1)S(1)}, u32[]{:S(2)}, u32[]{:S(2)}) %collective-permute-start) | collective-permute-done | bytes 786464 | tf_op jit(solution)/shard_map/ppermute | solution.py:366
  88.1 0.0 copy-start.3
  88.1 0.5 pad_maximum_fusion
  88.6 0.0 copy-done.2
  88.6 0.0 collective-permute-done.4.refs_4_
  88.6 0.0 copy-start.7
  88.6 1.8 %collective-permute-done.3.refs_2_ = bf16[1024,384]{1,0:T(8,128)(2,1)S(1)} collective-permute-done((bf16[1024,384]{1,0:T(8,128)(2,1)S(1)}, bf16[1024,384]{1,0:T(8,128)(2,1)S(1)}, u32[]{:S(2)}, u32[]{:S(2)}) %collective-permute-start.3) | collective-permute-done | bytes 786464 | tf_op jit(solution)/shard_map/ppermute | solution.py:366
  90.4 0.0 copy-start.8
  90.4 1.8 %collective-permute-start.9 = (bf16[4,1024,384]{2,1,0:T(8,128)(2,1)S(1)}, bf16[4,1024,384]{2,1,0:T(8,128)(2,1)}, u32[]{:S(2)}, u32[]{:S(2)}) collective-permute-start(bf16[4,1024,384]{2,1,0:T(8,128)(2,1)S(1)} %pad_maximum_fusion), channel_id=1, source_target_pairs={{0,8},{8,0},{1,9},{9,1},{2,10},{10,2},{3,11},{11,3},{4,12},{12,4},... | collective-permute-start | bytes 9437192 | tf_op jit(solution)/shard_map/ppermute | solution.py:366
  92.2 0.0 collective-permute-start.5
  92.2 0.0 copy-done
  92.2 0.6 collective-permute-start.2
  92.8 1.7 %collective-permute-start.12 = (bf16[1024,384]{1,0:T(8,128)(2,1)S(1)}, bf16[1024,384]{1,0:T(8,128)(2,1)S(1)}, u32[]{:S(2)}, u32[]{:S(2)}) collective-permute-start(bf16[1024,384]{1,0:T(8,128)(2,1)S(1)} %collective-permute-done.8.refs_9_), channel_id=1, source_target_pairs={{0,48},{16,0},{32,16},{48,32},{1,49},{17,1},{33,17},{49,33},{2,50}... | collective-permute-start | bytes 2359304 | tf_op jit(solution)/shard_map/ppermute | solution.py:366
  94.5 0.0 copy-done.3
  94.5 0.0 collective-permute-start.11
  94.5 18.1 %collective-permute-done.5.refs_6_ = bf16[1024,384]{1,0:T(8,128)(2,1)S(1)} collective-permute-done((bf16[1024,384]{1,0:T(8,128)(2,1)S(1)}, bf16[1024,384]{1,0:T(8,128)(2,1)S(1)}, u32[]{:S(2)}, u32[]{:S(2)}) %collective-permute-start.5) | collective-permute-done | bytes 786464 | tf_op jit(solution)/shard_map/ppermute | solution.py:366
  112.6 0.0 collective-permute-done.2.refs_1_
  112.6 1.1 collective-permute-start.7
  113.7 0.4 collective-permute-start.6
  114.1 0.0 collective-permute-done.12.refs_13_
  114.1 0.0 collective-permute-done.11.refs_14_
  114.1 0.0 copy-done.1
  114.1 0.0 copy-start.5
  114.2 0.4 collective-permute-start.13
  114.6 2.3 %collective-permute-start.14 = (bf16[1024,384]{1,0:T(8,128)(2,1)S(1)}, bf16[1024,384]{1,0:T(8,128)(2,1)}, u32[]{:S(2)}, u32[]{:S(2)}) collective-permute-start(bf16[1024,384]{1,0:T(8,128)(2,1)S(1)} %collective-permute-done.12.refs_13_), channel_id=1, source_target_pairs={{0,48},{16,0},{32,16},{48,32},{1,49},{17,1},{33,17},{49,33},{2,50}... | collective-permute-start | bytes 2359304 | tf_op jit(solution)/shard_map/ppermute | solution.py:366
  116.9 0.0 collective-permute-done.9.refs_16_
  116.9 0.8 collective-permute-start.10
  117.7 1.3 pad_maximum_fusion.1
  119.0 12.0 %collective-permute-done.7.refs_5_ = bf16[1024,384]{1,0:T(8,128)(2,1)S(1)} collective-permute-done((bf16[1024,384]{1,0:T(8,128)(2,1)S(1)}, bf16[1024,384]{1,0:T(8,128)(2,1)S(1)}, u32[]{:S(2)}, u32[]{:S(2)}) %collective-permute-start.7) | collective-permute-done | bytes 786464 | tf_op jit(solution)/shard_map/ppermute | solution.py:366
  131.1 1.7 %collective-permute-done.6.refs_3_ = bf16[1024,384]{1,0:T(8,128)(2,1)S(1)} collective-permute-done((bf16[1024,384]{1,0:T(8,128)(2,1)S(1)}, bf16[1024,384]{1,0:T(8,128)(2,1)S(1)}, u32[]{:S(2)}, u32[]{:S(2)}) %collective-permute-start.6) | collective-permute-done | bytes 786464 | tf_op jit(solution)/shard_map/ppermute | solution.py:366
  132.7 2.2 %collective-permute-start.15 = (bf16[2,1024,384]{2,1,0:T(8,128)(2,1)}, bf16[2,1024,384]{2,1,0:T(8,128)(2,1)S(1)}, u32[]{:S(2)}, u32[]{:S(2)}) collective-permute-start(bf16[2,1024,384]{2,1,0:T(8,128)(2,1)} %pad_maximum_fusion.1), channel_id=1, source_target_pairs={{0,8},{8,0},{1,9},{9,1},{2,10},{10,2},{3,11},{11,3},{4,12},{12,4},... | collective-permute-start | bytes 4718600 | tf_op jit(solution)/shard_map/ppermute | solution.py:366
  134.9 0.0 collective-permute-done.14.refs_15_
  134.9 0.0 collective-permute-done.10.refs_7_
  134.9 0.0 collective-permute-done.13.refs_11_
  134.9 0.0 copy-done.5
  134.9 2.0 %collective-permute-start.16 = (bf16[1024,384]{1,0:T(8,128)(2,1)}, bf16[1024,384]{1,0:T(8,128)(2,1)}, u32[]{:S(2)}, u32[]{:S(2)}) collective-permute-start(bf16[1024,384]{1,0:T(8,128)(2,1)} %collective-permute-done.13.refs_11_), channel_id=1, source_target_pairs={{0,8},{8,0},{1,9},{9,1},{2,10},{10,2},{3,11},{11,3},{4,12},{12,4},... | collective-permute-start | bytes 2359304 | tf_op jit(solution)/shard_map/ppermute | solution.py:366
  137.0 0.0 copy-done.8
  137.0 0.3 collective-permute-start.17
  137.3 0.0 copy-done.9
  137.3 0.0 copy-done.10
  137.3 0.0 copy-done.11
  137.3 0.0 copy-done.12
  137.3 0.0 copy-done.13
  137.4 0.7 stack.124.places
  138.1 1.3 collective-permute-done.16.refs_18_
  139.4 1.1 collective-permute-done.17.refs_19_
  140.5 0.0 collective-permute-done.15.refs_17_
  140.5 0.0 copy-done.7
  140.5 0.0 copy-done.4
  140.6 1.2 copy-done.6
  141.7 17.7 %cross.1 = bf16[64,128,512]{2,1,0:T(8,128)(2,1)} custom-call(s32[24]{0:T(128)} %stack.124.places, bf16[1024,384]{1,0:T(8,128)(2,1)} %copy-done, bf16[1024,384]{1,0:T(8,128)(2,1)} %copy-done.10, bf16[1024,384]{1,0:T(8,128)(2,1)} %copy-done.8, bf16[1024,384]{1,0:T(8,128)(2,1)} %copy-done.12, bf16[1024,384]{1,0:T(8,128)(2,1)} %copy-done.7, ...), custom_call_target="tpu_custom_call" | custom-call | flops 3221225472 | bytes 14680064 | tf_op jit(solution)/shard_map/cross/pallas_call | solution.py:335
  (7 shorter events, 0.0 us)
Async XLA Ops:
  66.4 25.8 %copy-start = (bf16[1024,384]{1,0:T(8,128)(2,1)}, bf16[1024,384]{1,0:T(8,128)(2,1)S(1)}, u32[]{:S(2)}) copy-start(bf16[1024,384]{1,0:T(8,128)(2,1)S(1)} %stack.133.refs_0_.refs_8_) | copy-start | bytes 2359300
  66.4 18.3 %collective-permute-start.8 = (bf16[1024,384]{1,0:T(8,128)(2,1)S(1)}, bf16[1024,384]{1,0:T(8,128)(2,1)S(1)}, u32[]{:S(2)}, u32[]{:S(2)}) collective-permute-start(bf16[1024,384]{1,0:T(8,128)(2,1)S(1)} %stack.133.refs_0_.refs_8_), channel_id=1, source_target_pairs={{0,64},{64,0},{1,65},{65,1},{2,66},{66,2},{3,67},{67,3},{4,68},{68... | collective-permute-start | bytes 2359304 | tf_op jit(solution)/shard_map/ppermute | solution.py:366
  67.2 17.7 %collective-permute-start.1 = (bf16[1024,384]{1,0:T(8,128)(2,1)S(1)}, bf16[1024,384]{1,0:T(8,128)(2,1)S(1)}, u32[]{:S(2)}, u32[]{:S(2)}) collective-permute-start(bf16[1024,384]{1,0:T(8,128)(2,1)S(1)} %stack.133.refs_0_.refs_8_), channel_id=1, source_target_pairs={{0,48},{16,0},{32,16},{48,32},{1,49},{17,1},{33,17},{49,33},{2,50}... | collective-permute-start | bytes 2359304 | tf_op jit(solution)/shard_map/ppermute | solution.py:366
  69.2 18.9 %collective-permute-start = (bf16[1024,384]{1,0:T(8,128)(2,1)S(1)}, bf16[1024,384]{1,0:T(8,128)(2,1)S(1)}, u32[]{:S(2)}, u32[]{:S(2)}) collective-permute-start(bf16[1024,384]{1,0:T(8,128)(2,1)S(1)} %stack.133.refs_0_.refs_8_), channel_id=1, source_target_pairs={{0,16},{16,32},{32,48},{48,0},{1,17},{17,33},{33,49},{49,1},{2,18}... | collective-permute-start | bytes 2359304 | tf_op jit(solution)/shard_map/ppermute | solution.py:366
  69.2 19.4 %collective-permute-start.4 = (bf16[1024,384]{1,0:T(8,128)(2,1)S(1)}, bf16[1024,384]{1,0:T(8,128)(2,1)S(1)}, u32[]{:S(2)}, u32[]{:S(2)}) collective-permute-start(bf16[1024,384]{1,0:T(8,128)(2,1)S(1)} %stack.133.refs_0_.refs_8_), channel_id=1, source_target_pairs={{0,6},{2,0},{4,2},{6,4},{1,7},{3,1},{5,3},{7,5},{8,14},{10,8},{12,... | collective-permute-start | bytes 2359304 | tf_op jit(solution)/shard_map/ppermute | solution.py:366
  71.0 19.4 %collective-permute-start.3 = (bf16[1024,384]{1,0:T(8,128)(2,1)S(1)}, bf16[1024,384]{1,0:T(8,128)(2,1)S(1)}, u32[]{:S(2)}, u32[]{:S(2)}) collective-permute-start(bf16[1024,384]{1,0:T(8,128)(2,1)S(1)} %stack.133.refs_0_.refs_8_), channel_id=1, source_target_pairs={{0,2},{2,4},{4,6},{6,0},{1,3},{3,5},{5,7},{7,1},{8,10},{10,12},{12... | collective-permute-start | bytes 2359304 | tf_op jit(solution)/shard_map/ppermute | solution.py:366
  84.7 29.4 %copy-start.1 = (bf16[1024,384]{1,0:T(8,128)(2,1)}, bf16[1024,384]{1,0:T(8,128)(2,1)S(1)}, u32[]{:S(2)}) copy-start(bf16[1024,384]{1,0:T(8,128)(2,1)S(1)} %collective-permute-done.8.refs_9_) | copy-start | bytes 2359300
  84.9 3.7 %copy-start.2 = (bf16[1024,384]{1,0:T(8,128)(2,1)}, bf16[1024,384]{1,0:T(8,128)(2,1)S(1)}, u32[]{:S(2)}) copy-start(bf16[1024,384]{1,0:T(8,128)(2,1)S(1)} %collective-permute-done.1.refs_12_) | copy-start | bytes 2359300
  88.1 6.4 %copy-start.3 = (bf16[1024,384]{1,0:T(8,128)(2,1)}, bf16[1024,384]{1,0:T(8,128)(2,1)S(1)}, u32[]{:S(2)}) copy-start(bf16[1024,384]{1,0:T(8,128)(2,1)S(1)} %collective-permute-done.refs_10_) | copy-start | bytes 2359300
  88.6 51.9 %copy-start.7 = (bf16[1024,384]{1,0:T(8,128)(2,1)}, bf16[1024,384]{1,0:T(8,128)(2,1)S(1)}, u32[]{:S(2)}) copy-start(bf16[1024,384]{1,0:T(8,128)(2,1)S(1)} %collective-permute-done.4.refs_4_) | copy-start | bytes 2359300
  90.4 46.6 %copy-start.8 = (bf16[1024,384]{1,0:T(8,128)(2,1)}, bf16[1024,384]{1,0:T(8,128)(2,1)S(1)}, u32[]{:S(2)}) copy-start(bf16[1024,384]{1,0:T(8,128)(2,1)S(1)} %collective-permute-done.3.refs_2_) | copy-start | bytes 2359300
  90.4 26.5 %collective-permute-start.9 = (bf16[4,1024,384]{2,1,0:T(8,128)(2,1)S(1)}, bf16[4,1024,384]{2,1,0:T(8,128)(2,1)}, u32[]{:S(2)}, u32[]{:S(2)}) collective-permute-start(bf16[4,1024,384]{2,1,0:T(8,128)(2,1)S(1)} %pad_maximum_fusion), channel_id=1, source_target_pairs={{0,8},{8,0},{1,9},{9,1},{2,10},{10,2},{3,11},{11,3},{4,12},{12,4},... | collective-permute-start | bytes 9437192 | tf_op jit(solution)/shard_map/ppermute | solution.py:366
  92.2 20.4 %collective-permute-start.5 = (bf16[1024,384]{1,0:T(8,128)(2,1)S(1)}, bf16[1024,384]{1,0:T(8,128)(2,1)S(1)}, u32[]{:S(2)}, u32[]{:S(2)}) collective-permute-start(bf16[1024,384]{1,0:T(8,128)(2,1)S(1)} %collective-permute-done.3.refs_2_), channel_id=1, source_target_pairs={{0,2},{2,4},{4,6},{6,0},{1,3},{3,5},{5,7},{7,1},{8,10},{10,12},{12... | collective-permute-start | bytes 2359304 | tf_op jit(solution)/shard_map/ppermute | solution.py:366
  92.2 20.4 %collective-permute-start.2 = (bf16[1024,384]{1,0:T(8,128)(2,1)S(1)}, bf16[1024,384]{1,0:T(8,128)(2,1)S(1)}, u32[]{:S(2)}, u32[]{:S(2)}) collective-permute-start(bf16[1024,384]{1,0:T(8,128)(2,1)S(1)} %stack.133.refs_0_.refs_8_), channel_id=1, source_target_pairs={{0,1},{1,0},{2,3},{3,2},{4,5},{5,4},{6,7},{7,6},{8,9},{9,8},{10,11... | collective-permute-start | bytes 2359304 | tf_op jit(solution)/shard_map/ppermute | solution.py:366
  92.8 21.4 %collective-permute-start.12 = (bf16[1024,384]{1,0:T(8,128)(2,1)S(1)}, bf16[1024,384]{1,0:T(8,128)(2,1)S(1)}, u32[]{:S(2)}, u32[]{:S(2)}) collective-permute-start(bf16[1024,384]{1,0:T(8,128)(2,1)S(1)} %collective-permute-done.8.refs_9_), channel_id=1, source_target_pairs={{0,48},{16,0},{32,16},{48,32},{1,49},{17,1},{33,17},{49,33},{2,50}... | collective-permute-start | bytes 2359304 | tf_op jit(solution)/shard_map/ppermute | solution.py:366
  94.5 19.7 %collective-permute-start.11 = (bf16[1024,384]{1,0:T(8,128)(2,1)S(1)}, bf16[1024,384]{1,0:T(8,128)(2,1)S(1)}, u32[]{:S(2)}, u32[]{:S(2)}) collective-permute-start(bf16[1024,384]{1,0:T(8,128)(2,1)S(1)} %collective-permute-done.refs_10_), channel_id=1, source_target_pairs={{0,16},{16,32},{32,48},{48,0},{1,17},{17,33},{33,49},{49,1},{2,18}... | collective-permute-start | bytes 2359304 | tf_op jit(solution)/shard_map/ppermute | solution.py:366
  112.6 24.7 %copy-start.9 = (bf16[1024,384]{1,0:T(8,128)(2,1)}, bf16[1024,384]{1,0:T(8,128)(2,1)S(1)}, u32[]{:S(2)}) copy-start(bf16[1024,384]{1,0:T(8,128)(2,1)S(1)} %collective-permute-done.5.refs_6_) | copy-start | bytes 2359300
  112.6 24.7 %copy-start.10 = (bf16[1024,384]{1,0:T(8,128)(2,1)}, bf16[1024,384]{1,0:T(8,128)(2,1)S(1)}, u32[]{:S(2)}) copy-start(bf16[1024,384]{1,0:T(8,128)(2,1)S(1)} %collective-permute-done.2.refs_1_) | copy-start | bytes 2359300
  112.6 18.5 %collective-permute-start.7 = (bf16[1024,384]{1,0:T(8,128)(2,1)S(1)}, bf16[1024,384]{1,0:T(8,128)(2,1)S(1)}, u32[]{:S(2)}, u32[]{:S(2)}) collective-permute-start(bf16[1024,384]{1,0:T(8,128)(2,1)S(1)} %collective-permute-done.2.refs_1_), channel_id=1, source_target_pairs={{0,6},{2,0},{4,2},{6,4},{1,7},{3,1},{5,3},{7,5},{8,14},{10,8},{12,... | collective-permute-start | bytes 2359304 | tf_op jit(solution)/shard_map/ppermute | solution.py:366
  113.7 19.0 %collective-permute-start.6 = (bf16[1024,384]{1,0:T(8,128)(2,1)S(1)}, bf16[1024,384]{1,0:T(8,128)(2,1)S(1)}, u32[]{:S(2)}, u32[]{:S(2)}) collective-permute-start(bf16[1024,384]{1,0:T(8,128)(2,1)S(1)} %collective-permute-done.2.refs_1_), channel_id=1, source_target_pairs={{0,2},{2,4},{4,6},{6,0},{1,3},{3,5},{5,7},{7,1},{8,10},{10,12},{12... | collective-permute-start | bytes 2359304 | tf_op jit(solution)/shard_map/ppermute | solution.py:366
  114.1 26.4 %copy-start.4 = (bf16[1024,384]{1,0:T(8,128)(2,1)}, bf16[1024,384]{1,0:T(8,128)(2,1)S(1)}, u32[]{:S(2)}) copy-start(bf16[1024,384]{1,0:T(8,128)(2,1)S(1)} %collective-permute-done.12.refs_13_) | copy-start | bytes 2359300
  114.1 20.8 %copy-start.5 = (bf16[1024,384]{1,0:T(8,128)(2,1)}, bf16[1024,384]{1,0:T(8,128)(2,1)S(1)}, u32[]{:S(2)}) copy-start(bf16[1024,384]{1,0:T(8,128)(2,1)S(1)} %collective-permute-done.11.refs_14_) | copy-start | bytes 2359300
  114.2 20.8 %collective-permute-start.13 = (bf16[1024,384]{1,0:T(8,128)(2,1)S(1)}, bf16[1024,384]{1,0:T(8,128)(2,1)}, u32[]{:S(2)}, u32[]{:S(2)}) collective-permute-start(bf16[1024,384]{1,0:T(8,128)(2,1)S(1)} %collective-permute-done.8.refs_9_), channel_id=1, source_target_pairs={{0,16},{16,32},{32,48},{48,0},{1,17},{17,33},{33,49},{49,1},{2,18}... | collective-permute-start | bytes 2359304 | tf_op jit(solution)/shard_map/ppermute | solution.py:366
  114.6 20.3 %collective-permute-start.14 = (bf16[1024,384]{1,0:T(8,128)(2,1)S(1)}, bf16[1024,384]{1,0:T(8,128)(2,1)}, u32[]{:S(2)}, u32[]{:S(2)}) collective-permute-start(bf16[1024,384]{1,0:T(8,128)(2,1)S(1)} %collective-permute-done.12.refs_13_), channel_id=1, source_target_pairs={{0,48},{16,0},{32,16},{48,32},{1,49},{17,1},{33,17},{49,33},{2,50}... | collective-permute-start | bytes 2359304 | tf_op jit(solution)/shard_map/ppermute | solution.py:366
  116.9 18.0 %collective-permute-start.10 = (bf16[1024,384]{1,0:T(8,128)(2,1)S(1)}, bf16[1024,384]{1,0:T(8,128)(2,1)S(1)}, u32[]{:S(2)}, u32[]{:S(2)}) collective-permute-start(bf16[1024,384]{1,0:T(8,128)(2,1)S(1)} %collective-permute-done.5.refs_6_), channel_id=1, source_target_pairs={{0,1},{1,0},{2,3},{3,2},{4,5},{5,4},{6,7},{7,6},{8,9},{9,8},{10,11... | collective-permute-start | bytes 2359304 | tf_op jit(solution)/shard_map/ppermute | solution.py:366
  131.0 6.2 %copy-start.11 = (bf16[1024,384]{1,0:T(8,128)(2,1)}, bf16[1024,384]{1,0:T(8,128)(2,1)S(1)}, u32[]{:S(2)}) copy-start(bf16[1024,384]{1,0:T(8,128)(2,1)S(1)} %collective-permute-done.7.refs_5_) | copy-start | bytes 2359300
  132.7 4.6 %copy-start.12 = (bf16[1024,384]{1,0:T(8,128)(2,1)}, bf16[1024,384]{1,0:T(8,128)(2,1)S(1)}, u32[]{:S(2)}) copy-start(bf16[1024,384]{1,0:T(8,128)(2,1)S(1)} %collective-permute-done.6.refs_3_) | copy-start | bytes 2359300
  132.7 7.8 %collective-permute-start.15 = (bf16[2,1024,384]{2,1,0:T(8,128)(2,1)}, bf16[2,1024,384]{2,1,0:T(8,128)(2,1)S(1)}, u32[]{:S(2)}, u32[]{:S(2)}) collective-permute-start(bf16[2,1024,384]{2,1,0:T(8,128)(2,1)} %pad_maximum_fusion.1), channel_id=1, source_target_pairs={{0,8},{8,0},{1,9},{9,1},{2,10},{10,2},{3,11},{11,3},{4,12},{12,4},... | collective-permute-start | bytes 4718600 | tf_op jit(solution)/shard_map/ppermute | solution.py:366
  134.9 2.4 %copy-start.13 = (bf16[1024,384]{1,0:T(8,128)(2,1)}, bf16[1024,384]{1,0:T(8,128)(2,1)S(1)}, u32[]{:S(2)}) copy-start(bf16[1024,384]{1,0:T(8,128)(2,1)S(1)} %collective-permute-done.10.refs_7_) | copy-start | bytes 2359300
  134.9 4.5 %collective-permute-start.16 = (bf16[1024,384]{1,0:T(8,128)(2,1)}, bf16[1024,384]{1,0:T(8,128)(2,1)}, u32[]{:S(2)}, u32[]{:S(2)}) collective-permute-start(bf16[1024,384]{1,0:T(8,128)(2,1)} %collective-permute-done.13.refs_11_), channel_id=1, source_target_pairs={{0,8},{8,0},{1,9},{9,1},{2,10},{10,2},{3,11},{11,3},{4,12},{12,4},... | collective-permute-start | bytes 2359304 | tf_op jit(solution)/shard_map/ppermute | solution.py:366
  137.0 3.6 %collective-permute-start.17 = (bf16[1024,384]{1,0:T(8,128)(2,1)}, bf16[1024,384]{1,0:T(8,128)(2,1)}, u32[]{:S(2)}, u32[]{:S(2)}) collective-permute-start(bf16[1024,384]{1,0:T(8,128)(2,1)} %collective-permute-done.14.refs_15_), channel_id=1, source_target_pairs={{0,8},{8,0},{1,9},{9,1},{2,10},{10,2},{3,11},{11,3},{4,12},{12,4},... | collective-permute-start | bytes 2359304 | tf_op jit(solution)/shard_map/ppermute | solution.py:366
  140.5 1.2 copy-start.6

commit v4 on v3

--- a/solution.py
+++ b/solution.py
@@ -125,7 +125,9 @@
             axis=1,
         )
         same = (owner_col == owner_row[...]) & (iota((SEGS, SEGS), 0) < iota((SEGS, SEGS), 1))
-        rank = jnp.sum(same.astype(F32), axis=0, keepdims=True).astype(jnp.int32)
+        ones = jnp.ones((8, SEGS), BF16)
+        rank = jnp.dot(ones, same.astype(F32).astype(BF16), preferred_element_type=F32)
+        rank = rank[0:1].astype(jnp.int32)
         target = owner_row[...] * CAP + rank
         for part in range(4):
             chosen = target == iota((512, SEGS), 0) + part * 512
@@ -347,7 +349,7 @@
             pltpu.VMEM((BLOCK, 128, WIDE), BF16),
             pltpu.VMEM((2, BLOCK, 64, 256), BF16),
             pltpu.VMEM((2, 256, 256), BF16),
-            pltpu.VMEM((128 * STRIDE, 128), F32),
+            pltpu.VMEM((129 * STRIDE, 128), F32),
             pltpu.SemaphoreType.DMA((2 * BLOCKS, 24)),
         ],
         compiler_params=pltpu.CompilerParams(vmem_limit_bytes=58 << 20),

time: 160 us -> 160 us (level)
  no operation moved by 1% of the time
where the time goes in v4:
time: 160 us
  waiting for transfers between devices  53 us (33%)
  blocking collectives  43 us (27%)
  Pallas kernels  41 us (26%)
  starting transfers between devices  18.3 us (11%)
  local copies, waits for them, and re-layouts  1.93 us (1%)
  other arithmetic  1.83 us (1%)
    ppermute x18, waiting for transfers between devices, move(): lax.ppermute(lax.optimization_barrier((array,) + others)[0], axis, pairs)  53 us
    all_to_all x1, blocking collectives, on_device(): lax.all_to_all(send, AXES, split_axis=0, concat_axis=0, tiled=True)  43 us
    pallas_call x1, Pallas kernels, transform(): pl.pallas_call(transform_kernel, grid=(STEPS,), in_specs=[pl.BlockSpec((S...  19.2 us
    ppermute x18, starting transfers between devices, move(): lax.ppermute(lax.optimization_barrier((array,) + others)[0], axis, pairs)  18.3 us
    pallas_call x1, Pallas kernels, cross(): pl.pallas_call(cross_kernel, grid=(2 * BLOCKS + 64 // OUT_ROWS,), in_spec...  17.7 us
    pallas_call x1, Pallas kernels, stack(): pl.pallas_call(stack_kernel, out_shape=jax.ShapeDtypeStruct((2 * PAIRS *...  4.07 us
  transfers between devices with their start and end apart: 18, of which 9 were waited for; matrix products, arithmetic and copies ran while one was open for 2% of the time, Pallas kernels for 0%

profile of v4, /device:TPU:1, one launch (start us, length us, event | category | flops | bytes accessed | tf_op | source)
XLA Modules:
  0.0 159.5 jit_solution(2723689494012567929)
XLA Ops:
  0.0 19.2 %transform.1 = bf16[128,72,128]{2,1,0:T(8,128)(2,1)} custom-call(bf16[512,8192]{1,0:T(8,128)(2,1)} %after.1, bf16[512,8192]{1,0:T(8,128)(2,1)} %after.1, bf16[512,8192]{1,0:T(8,128)(2,1)} %after.1, s32[1,512]{1,0:T(1,128)} %bitcast.41, s32[1,512]{1,0:T(1,128)} %bitcast.42, s32[1,1024]{1,0:T(1,128)} %bitcast.40, s32[1,256]{1,0:T(1,128)} %bitcast.43), custom_call_target="tpu_custom_call" | custom-call | flops 21474836480 | bytes 8388608 | tf_op jit(solution)/shard_map/transform/pallas_call | solution.py:147
  19.2 43.0 %all_to_all.5.received = bf16[128,72,128]{2,1,0:T(8,128)(2,1)S(1)} all-to-all(bf16[128,72,128]{2,1,0:T(8,128)(2,1)} %transform.1), channel_id=1, replica_groups=mesh['zh'=2,'y'=4,'core'=2,'x'=4,'zl'=2] {'zh','y','core','x','zl'}, dimensions={0} | all-to-all | bytes 4718592 | tf_op jit(solution)/shard_map/all_to_all | solution.py:409
  62.2 4.1 %stack.133.refs_0_.refs_8_ = bf16[1024,384]{1,0:T(8,128)(2,1)S(1)} custom-call(bf16[128,72,128]{2,1,0:T(8,128)(2,1)S(1)} %all_to_all.5.received), custom_call_target="tpu_custom_call" | custom-call | flops 2147483648 | bytes 3145728 | tf_op jit(solution)/shard_map/stack/pallas_call | solution.py:222
  66.3 0.0 copy-start
  66.3 0.8 collective-permute-start.8
  67.1 2.0 %collective-permute-start.1 = (bf16[1024,384]{1,0:T(8,128)(2,1)S(1)}, bf16[1024,384]{1,0:T(8,128)(2,1)S(1)}, u32[]{:S(2)}, u32[]{:S(2)}) collective-permute-start(bf16[1024,384]{1,0:T(8,128)(2,1)S(1)} %stack.133.refs_0_.refs_8_), channel_id=1, source_target_pairs={{0,48},{16,0},{32,16},{48,32},{1,49},{17,1},{33,17},{49,33},{2,50}... | collective-permute-start | bytes 2359304 | tf_op jit(solution)/shard_map/ppermute | solution.py:368
  69.1 0.0 collective-permute-start
  69.1 1.8 %collective-permute-start.4 = (bf16[1024,384]{1,0:T(8,128)(2,1)S(1)}, bf16[1024,384]{1,0:T(8,128)(2,1)S(1)}, u32[]{:S(2)}, u32[]{:S(2)}) collective-permute-start(bf16[1024,384]{1,0:T(8,128)(2,1)S(1)} %stack.133.refs_0_.refs_8_), channel_id=1, source_target_pairs={{0,6},{2,0},{4,2},{6,4},{1,7},{3,1},{5,3},{7,5},{8,14},{10,8},{12,... | collective-permute-start | bytes 2359304 | tf_op jit(solution)/shard_map/ppermute | solution.py:368
  70.9 0.0 collective-permute-start.3
  70.9 13.7 %collective-permute-done.8.refs_9_ = bf16[1024,384]{1,0:T(8,128)(2,1)S(1)} collective-permute-done((bf16[1024,384]{1,0:T(8,128)(2,1)S(1)}, bf16[1024,384]{1,0:T(8,128)(2,1)S(1)}, u32[]{:S(2)}, u32[]{:S(2)}) %collective-permute-start.8) | collective-permute-done | bytes 786464 | tf_op jit(solution)/shard_map/ppermute | solution.py:368
  84.6 0.0 copy-start.1
  84.7 0.2 collective-permute-done.1.refs_12_
  84.9 3.1 %collective-permute-done.refs_10_ = bf16[1024,384]{1,0:T(8,128)(2,1)S(1)} collective-permute-done((bf16[1024,384]{1,0:T(8,128)(2,1)S(1)}, bf16[1024,384]{1,0:T(8,128)(2,1)S(1)}, u32[]{:S(2)}, u32[]{:S(2)}) %collective-permute-start) | collective-permute-done | bytes 786464 | tf_op jit(solution)/shard_map/ppermute | solution.py:368
  88.0 0.0 copy-start.3
  88.0 0.5 pad_maximum_fusion
  88.5 0.0 copy-done.2
  88.5 0.0 collective-permute-done.4.refs_4_
  88.5 0.0 copy-start.7
  88.5 1.7 %collective-permute-done.3.refs_2_ = bf16[1024,384]{1,0:T(8,128)(2,1)S(1)} collective-permute-done((bf16[1024,384]{1,0:T(8,128)(2,1)S(1)}, bf16[1024,384]{1,0:T(8,128)(2,1)S(1)}, u32[]{:S(2)}, u32[]{:S(2)}) %collective-permute-start.3) | collective-permute-done | bytes 786464 | tf_op jit(solution)/shard_map/ppermute | solution.py:368
  90.3 0.0 copy-start.8
  90.3 1.8 %collective-permute-start.9 = (bf16[4,1024,384]{2,1,0:T(8,128)(2,1)S(1)}, bf16[4,1024,384]{2,1,0:T(8,128)(2,1)}, u32[]{:S(2)}, u32[]{:S(2)}) collective-permute-start(bf16[4,1024,384]{2,1,0:T(8,128)(2,1)S(1)} %pad_maximum_fusion), channel_id=1, source_target_pairs={{0,8},{8,0},{1,9},{9,1},{2,10},{10,2},{3,11},{11,3},{4,12},{12,4},... | collective-permute-start | bytes 9437192 | tf_op jit(solution)/shard_map/ppermute | solution.py:368
  92.1 0.0 collective-permute-start.5
  92.1 0.0 copy-done
  92.1 0.6 collective-permute-start.2
  92.7 1.7 %collective-permute-start.12 = (bf16[1024,384]{1,0:T(8,128)(2,1)S(1)}, bf16[1024,384]{1,0:T(8,128)(2,1)S(1)}, u32[]{:S(2)}, u32[]{:S(2)}) collective-permute-start(bf16[1024,384]{1,0:T(8,128)(2,1)S(1)} %collective-permute-done.8.refs_9_), channel_id=1, source_target_pairs={{0,48},{16,0},{32,16},{48,32},{1,49},{17,1},{33,17},{49,33},{2,50}... | collective-permute-start | bytes 2359304 | tf_op jit(solution)/shard_map/ppermute | solution.py:368
  94.4 0.0 copy-done.3
  94.4 0.0 collective-permute-start.11
  94.4 18.1 %collective-permute-done.5.refs_6_ = bf16[1024,384]{1,0:T(8,128)(2,1)S(1)} collective-permute-done((bf16[1024,384]{1,0:T(8,128)(2,1)S(1)}, bf16[1024,384]{1,0:T(8,128)(2,1)S(1)}, u32[]{:S(2)}, u32[]{:S(2)}) %collective-permute-start.5) | collective-permute-done | bytes 786464 | tf_op jit(solution)/shard_map/ppermute | solution.py:368
  112.5 0.0 collective-permute-done.2.refs_1_
  112.5 0.0 copy-start.10
  112.5 1.1 collective-permute-start.7
  113.6 0.4 collective-permute-start.6
  114.0 0.0 collective-permute-done.12.refs_13_
  114.0 0.0 collective-permute-done.11.refs_14_
  114.0 0.0 copy-done.1
  114.0 0.0 copy-start.5
  114.1 0.4 collective-permute-start.13
  114.5 2.3 %collective-permute-start.14 = (bf16[1024,384]{1,0:T(8,128)(2,1)S(1)}, bf16[1024,384]{1,0:T(8,128)(2,1)}, u32[]{:S(2)}, u32[]{:S(2)}) collective-permute-start(bf16[1024,384]{1,0:T(8,128)(2,1)S(1)} %collective-permute-done.12.refs_13_), channel_id=1, source_target_pairs={{0,48},{16,0},{32,16},{48,32},{1,49},{17,1},{33,17},{49,33},{2,50}... | collective-permute-start | bytes 2359304 | tf_op jit(solution)/shard_map/ppermute | solution.py:368
  116.8 0.0 collective-permute-done.9.refs_16_
  116.8 0.8 collective-permute-start.10
  117.6 1.3 pad_maximum_fusion.1
  118.9 12.0 %collective-permute-done.7.refs_5_ = bf16[1024,384]{1,0:T(8,128)(2,1)S(1)} collective-permute-done((bf16[1024,384]{1,0:T(8,128)(2,1)S(1)}, bf16[1024,384]{1,0:T(8,128)(2,1)S(1)}, u32[]{:S(2)}, u32[]{:S(2)}) %collective-permute-start.7) | collective-permute-done | bytes 786464 | tf_op jit(solution)/shard_map/ppermute | solution.py:368
  130.9 1.7 %collective-permute-done.6.refs_3_ = bf16[1024,384]{1,0:T(8,128)(2,1)S(1)} collective-permute-done((bf16[1024,384]{1,0:T(8,128)(2,1)S(1)}, bf16[1024,384]{1,0:T(8,128)(2,1)S(1)}, u32[]{:S(2)}, u32[]{:S(2)}) %collective-permute-start.6) | collective-permute-done | bytes 786464 | tf_op jit(solution)/shard_map/ppermute | solution.py:368
  132.6 2.2 %collective-permute-start.15 = (bf16[2,1024,384]{2,1,0:T(8,128)(2,1)}, bf16[2,1024,384]{2,1,0:T(8,128)(2,1)S(1)}, u32[]{:S(2)}, u32[]{:S(2)}) collective-permute-start(bf16[2,1024,384]{2,1,0:T(8,128)(2,1)} %pad_maximum_fusion.1), channel_id=1, source_target_pairs={{0,8},{8,0},{1,9},{9,1},{2,10},{10,2},{3,11},{11,3},{4,12},{12,4},... | collective-permute-start | bytes 4718600 | tf_op jit(solution)/shard_map/ppermute | solution.py:368
  134.8 0.0 collective-permute-done.14.refs_15_
  134.8 0.0 collective-permute-done.10.refs_7_
  134.8 0.0 collective-permute-done.13.refs_11_
  134.8 0.0 copy-done.5
  134.8 2.0 %collective-permute-start.16 = (bf16[1024,384]{1,0:T(8,128)(2,1)}, bf16[1024,384]{1,0:T(8,128)(2,1)}, u32[]{:S(2)}, u32[]{:S(2)}) collective-permute-start(bf16[1024,384]{1,0:T(8,128)(2,1)} %collective-permute-done.13.refs_11_), channel_id=1, source_target_pairs={{0,8},{8,0},{1,9},{9,1},{2,10},{10,2},{3,11},{11,3},{4,12},{12,4},... | collective-permute-start | bytes 2359304 | tf_op jit(solution)/shard_map/ppermute | solution.py:368
  136.9 0.0 copy-done.8
  136.9 0.3 collective-permute-start.17
  137.2 0.0 copy-done.9
  137.2 0.0 copy-done.10
  137.2 0.0 copy-done.11
  137.2 0.0 copy-done.12
  137.2 0.0 copy-done.13
  137.3 0.7 stack.124.places
  138.0 1.3 collective-permute-done.16.refs_18_
  139.3 1.1 collective-permute-done.17.refs_19_
  140.4 0.0 collective-permute-done.15.refs_17_
  140.4 0.0 copy-done.7
  140.4 0.0 copy-done.4
  140.5 1.2 copy-done.6
  141.6 17.7 %cross.1 = bf16[64,128,512]{2,1,0:T(8,128)(2,1)} custom-call(s32[24]{0:T(128)} %stack.124.places, bf16[1024,384]{1,0:T(8,128)(2,1)} %copy-done, bf16[1024,384]{1,0:T(8,128)(2,1)} %copy-done.10, bf16[1024,384]{1,0:T(8,128)(2,1)} %copy-done.8, bf16[1024,384]{1,0:T(8,128)(2,1)} %copy-done.12, bf16[1024,384]{1,0:T(8,128)(2,1)} %copy-done.7, ...), custom_call_target="tpu_custom_call" | custom-call | flops 3221225472 | bytes 14680064 | tf_op jit(solution)/shard_map/cross/pallas_call | solution.py:337
  (7 shorter events, 0.0 us)
Async XLA Ops:
  66.3 25.8 %copy-start = (bf16[1024,384]{1,0:T(8,128)(2,1)}, bf16[1024,384]{1,0:T(8,128)(2,1)S(1)}, u32[]{:S(2)}) copy-start(bf16[1024,384]{1,0:T(8,128)(2,1)S(1)} %stack.133.refs_0_.refs_8_) | copy-start | bytes 2359300
  66.3 18.3 %collective-permute-start.8 = (bf16[1024,384]{1,0:T(8,128)(2,1)S(1)}, bf16[1024,384]{1,0:T(8,128)(2,1)S(1)}, u32[]{:S(2)}, u32[]{:S(2)}) collective-permute-start(bf16[1024,384]{1,0:T(8,128)(2,1)S(1)} %stack.133.refs_0_.refs_8_), channel_id=1, source_target_pairs={{0,64},{64,0},{1,65},{65,1},{2,66},{66,2},{3,67},{67,3},{4,68},{68... | collective-permute-start | bytes 2359304 | tf_op jit(solution)/shard_map/ppermute | solution.py:368
  67.1 17.8 %collective-permute-start.1 = (bf16[1024,384]{1,0:T(8,128)(2,1)S(1)}, bf16[1024,384]{1,0:T(8,128)(2,1)S(1)}, u32[]{:S(2)}, u32[]{:S(2)}) collective-permute-start(bf16[1024,384]{1,0:T(8,128)(2,1)S(1)} %stack.133.refs_0_.refs_8_), channel_id=1, source_target_pairs={{0,48},{16,0},{32,16},{48,32},{1,49},{17,1},{33,17},{49,33},{2,50}... | collective-permute-start | bytes 2359304 | tf_op jit(solution)/shard_map/ppermute | solution.py:368
  69.1 18.9 %collective-permute-start = (bf16[1024,384]{1,0:T(8,128)(2,1)S(1)}, bf16[1024,384]{1,0:T(8,128)(2,1)S(1)}, u32[]{:S(2)}, u32[]{:S(2)}) collective-permute-start(bf16[1024,384]{1,0:T(8,128)(2,1)S(1)} %stack.133.refs_0_.refs_8_), channel_id=1, source_target_pairs={{0,16},{16,32},{32,48},{48,0},{1,17},{17,33},{33,49},{49,1},{2,18}... | collective-permute-start | bytes 2359304 | tf_op jit(solution)/shard_map/ppermute | solution.py:368
  69.1 19.4 %collective-permute-start.4 = (bf16[1024,384]{1,0:T(8,128)(2,1)S(1)}, bf16[1024,384]{1,0:T(8,128)(2,1)S(1)}, u32[]{:S(2)}, u32[]{:S(2)}) collective-permute-start(bf16[1024,384]{1,0:T(8,128)(2,1)S(1)} %stack.133.refs_0_.refs_8_), channel_id=1, source_target_pairs={{0,6},{2,0},{4,2},{6,4},{1,7},{3,1},{5,3},{7,5},{8,14},{10,8},{12,... | collective-permute-start | bytes 2359304 | tf_op jit(solution)/shard_map/ppermute | solution.py:368
  70.9 19.4 %collective-permute-start.3 = (bf16[1024,384]{1,0:T(8,128)(2,1)S(1)}, bf16[1024,384]{1,0:T(8,128)(2,1)S(1)}, u32[]{:S(2)}, u32[]{:S(2)}) collective-permute-start(bf16[1024,384]{1,0:T(8,128)(2,1)S(1)} %stack.133.refs_0_.refs_8_), channel_id=1, source_target_pairs={{0,2},{2,4},{4,6},{6,0},{1,3},{3,5},{5,7},{7,1},{8,10},{10,12},{12... | collective-permute-start | bytes 2359304 | tf_op jit(solution)/shard_map/ppermute | solution.py:368
  84.6 29.4 %copy-start.1 = (bf16[1024,384]{1,0:T(8,128)(2,1)}, bf16[1024,384]{1,0:T(8,128)(2,1)S(1)}, u32[]{:S(2)}) copy-start(bf16[1024,384]{1,0:T(8,128)(2,1)S(1)} %collective-permute-done.8.refs_9_) | copy-start | bytes 2359300
  84.9 3.7 %copy-start.2 = (bf16[1024,384]{1,0:T(8,128)(2,1)}, bf16[1024,384]{1,0:T(8,128)(2,1)S(1)}, u32[]{:S(2)}) copy-start(bf16[1024,384]{1,0:T(8,128)(2,1)S(1)} %collective-permute-done.1.refs_12_) | copy-start | bytes 2359300
  88.0 6.4 %copy-start.3 = (bf16[1024,384]{1,0:T(8,128)(2,1)}, bf16[1024,384]{1,0:T(8,128)(2,1)S(1)}, u32[]{:S(2)}) copy-start(bf16[1024,384]{1,0:T(8,128)(2,1)S(1)} %collective-permute-done.refs_10_) | copy-start | bytes 2359300
  88.5 51.9 %copy-start.7 = (bf16[1024,384]{1,0:T(8,128)(2,1)}, bf16[1024,384]{1,0:T(8,128)(2,1)S(1)}, u32[]{:S(2)}) copy-start(bf16[1024,384]{1,0:T(8,128)(2,1)S(1)} %collective-permute-done.4.refs_4_) | copy-start | bytes 2359300
  90.3 46.6 %copy-start.8 = (bf16[1024,384]{1,0:T(8,128)(2,1)}, bf16[1024,384]{1,0:T(8,128)(2,1)S(1)}, u32[]{:S(2)}) copy-start(bf16[1024,384]{1,0:T(8,128)(2,1)S(1)} %collective-permute-done.3.refs_2_) | copy-start | bytes 2359300
  90.3 26.5 %collective-permute-start.9 = (bf16[4,1024,384]{2,1,0:T(8,128)(2,1)S(1)}, bf16[4,1024,384]{2,1,0:T(8,128)(2,1)}, u32[]{:S(2)}, u32[]{:S(2)}) collective-permute-start(bf16[4,1024,384]{2,1,0:T(8,128)(2,1)S(1)} %pad_maximum_fusion), channel_id=1, source_target_pairs={{0,8},{8,0},{1,9},{9,1},{2,10},{10,2},{3,11},{11,3},{4,12},{12,4},... | collective-permute-start | bytes 9437192 | tf_op jit(solution)/shard_map/ppermute | solution.py:368
  92.1 20.4 %collective-permute-start.5 = (bf16[1024,384]{1,0:T(8,128)(2,1)S(1)}, bf16[1024,384]{1,0:T(8,128)(2,1)S(1)}, u32[]{:S(2)}, u32[]{:S(2)}) collective-permute-start(bf16[1024,384]{1,0:T(8,128)(2,1)S(1)} %collective-permute-done.3.refs_2_), channel_id=1, source_target_pairs={{0,2},{2,4},{4,6},{6,0},{1,3},{3,5},{5,7},{7,1},{8,10},{10,12},{12... | collective-permute-start | bytes 2359304 | tf_op jit(solution)/shard_map/ppermute | solution.py:368
  92.1 20.4 %collective-permute-start.2 = (bf16[1024,384]{1,0:T(8,128)(2,1)S(1)}, bf16[1024,384]{1,0:T(8,128)(2,1)S(1)}, u32[]{:S(2)}, u32[]{:S(2)}) collective-permute-start(bf16[1024,384]{1,0:T(8,128)(2,1)S(1)} %stack.133.refs_0_.refs_8_), channel_id=1, source_target_pairs={{0,1},{1,0},{2,3},{3,2},{4,5},{5,4},{6,7},{7,6},{8,9},{9,8},{10,11... | collective-permute-start | bytes 2359304 | tf_op jit(solution)/shard_map/ppermute | solution.py:368
  92.7 21.4 %collective-permute-start.12 = (bf16[1024,384]{1,0:T(8,128)(2,1)S(1)}, bf16[1024,384]{1,0:T(8,128)(2,1)S(1)}, u32[]{:S(2)}, u32[]{:S(2)}) collective-permute-start(bf16[1024,384]{1,0:T(8,128)(2,1)S(1)} %collective-permute-done.8.refs_9_), channel_id=1, source_target_pairs={{0,48},{16,0},{32,16},{48,32},{1,49},{17,1},{33,17},{49,33},{2,50}... | collective-permute-start | bytes 2359304 | tf_op jit(solution)/shard_map/ppermute | solution.py:368
  94.4 19.7 %collective-permute-start.11 = (bf16[1024,384]{1,0:T(8,128)(2,1)S(1)}, bf16[1024,384]{1,0:T(8,128)(2,1)S(1)}, u32[]{:S(2)}, u32[]{:S(2)}) collective-permute-start(bf16[1024,384]{1,0:T(8,128)(2,1)S(1)} %collective-permute-done.refs_10_), channel_id=1, source_target_pairs={{0,16},{16,32},{32,48},{48,0},{1,17},{17,33},{33,49},{49,1},{2,18}... | collective-permute-start | bytes 2359304 | tf_op jit(solution)/shard_map/ppermute | solution.py:368
  112.5 24.7 %copy-start.9 = (bf16[1024,384]{1,0:T(8,128)(2,1)}, bf16[1024,384]{1,0:T(8,128)(2,1)S(1)}, u32[]{:S(2)}) copy-start(bf16[1024,384]{1,0:T(8,128)(2,1)S(1)} %collective-permute-done.5.refs_6_) | copy-start | bytes 2359300
  112.5 24.7 %copy-start.10 = (bf16[1024,384]{1,0:T(8,128)(2,1)}, bf16[1024,384]{1,0:T(8,128)(2,1)S(1)}, u32[]{:S(2)}) copy-start(bf16[1024,384]{1,0:T(8,128)(2,1)S(1)} %collective-permute-done.2.refs_1_) | copy-start | bytes 2359300
  112.5 18.5 %collective-permute-start.7 = (bf16[1024,384]{1,0:T(8,128)(2,1)S(1)}, bf16[1024,384]{1,0:T(8,128)(2,1)S(1)}, u32[]{:S(2)}, u32[]{:S(2)}) collective-permute-start(bf16[1024,384]{1,0:T(8,128)(2,1)S(1)} %collective-permute-done.2.refs_1_), channel_id=1, source_target_pairs={{0,6},{2,0},{4,2},{6,4},{1,7},{3,1},{5,3},{7,5},{8,14},{10,8},{12,... | collective-permute-start | bytes 2359304 | tf_op jit(solution)/shard_map/ppermute | solution.py:368
  113.6 19.0 %collective-permute-start.6 = (bf16[1024,384]{1,0:T(8,128)(2,1)S(1)}, bf16[1024,384]{1,0:T(8,128)(2,1)S(1)}, u32[]{:S(2)}, u32[]{:S(2)}) collective-permute-start(bf16[1024,384]{1,0:T(8,128)(2,1)S(1)} %collective-permute-done.2.refs_1_), channel_id=1, source_target_pairs={{0,2},{2,4},{4,6},{6,0},{1,3},{3,5},{5,7},{7,1},{8,10},{10,12},{12... | collective-permute-start | bytes 2359304 | tf_op jit(solution)/shard_map/ppermute | solution.py:368
  114.0 26.4 %copy-start.4 = (bf16[1024,384]{1,0:T(8,128)(2,1)}, bf16[1024,384]{1,0:T(8,128)(2,1)S(1)}, u32[]{:S(2)}) copy-start(bf16[1024,384]{1,0:T(8,128)(2,1)S(1)} %collective-permute-done.12.refs_13_) | copy-start | bytes 2359300
  114.0 20.8 %copy-start.5 = (bf16[1024,384]{1,0:T(8,128)(2,1)}, bf16[1024,384]{1,0:T(8,128)(2,1)S(1)}, u32[]{:S(2)}) copy-start(bf16[1024,384]{1,0:T(8,128)(2,1)S(1)} %collective-permute-done.11.refs_14_) | copy-start | bytes 2359300
  114.1 20.8 %collective-permute-start.13 = (bf16[1024,384]{1,0:T(8,128)(2,1)S(1)}, bf16[1024,384]{1,0:T(8,128)(2,1)}, u32[]{:S(2)}, u32[]{:S(2)}) collective-permute-start(bf16[1024,384]{1,0:T(8,128)(2,1)S(1)} %collective-permute-done.8.refs_9_), channel_id=1, source_target_pairs={{0,16},{16,32},{32,48},{48,0},{1,17},{17,33},{33,49},{49,1},{2,18}... | collective-permute-start | bytes 2359304 | tf_op jit(solution)/shard_map/ppermute | solution.py:368
  114.5 20.3 %collective-permute-start.14 = (bf16[1024,384]{1,0:T(8,128)(2,1)S(1)}, bf16[1024,384]{1,0:T(8,128)(2,1)}, u32[]{:S(2)}, u32[]{:S(2)}) collective-permute-start(bf16[1024,384]{1,0:T(8,128)(2,1)S(1)} %collective-permute-done.12.refs_13_), channel_id=1, source_target_pairs={{0,48},{16,0},{32,16},{48,32},{1,49},{17,1},{33,17},{49,33},{2,50}... | collective-permute-start | bytes 2359304 | tf_op jit(solution)/shard_map/ppermute | solution.py:368
  116.8 18.0 %collective-permute-start.10 = (bf16[1024,384]{1,0:T(8,128)(2,1)S(1)}, bf16[1024,384]{1,0:T(8,128)(2,1)S(1)}, u32[]{:S(2)}, u32[]{:S(2)}) collective-permute-start(bf16[1024,384]{1,0:T(8,128)(2,1)S(1)} %collective-permute-done.5.refs_6_), channel_id=1, source_target_pairs={{0,1},{1,0},{2,3},{3,2},{4,5},{5,4},{6,7},{7,6},{8,9},{9,8},{10,11... | collective-permute-start | bytes 2359304 | tf_op jit(solution)/shard_map/ppermute | solution.py:368
  130.9 6.2 %copy-start.11 = (bf16[1024,384]{1,0:T(8,128)(2,1)}, bf16[1024,384]{1,0:T(8,128)(2,1)S(1)}, u32[]{:S(2)}) copy-start(bf16[1024,384]{1,0:T(8,128)(2,1)S(1)} %collective-permute-done.7.refs_5_) | copy-start | bytes 2359300
  132.6 4.6 %copy-start.12 = (bf16[1024,384]{1,0:T(8,128)(2,1)}, bf16[1024,384]{1,0:T(8,128)(2,1)S(1)}, u32[]{:S(2)}) copy-start(bf16[1024,384]{1,0:T(8,128)(2,1)S(1)} %collective-permute-done.6.refs_3_) | copy-start | bytes 2359300
  132.6 7.8 %collective-permute-start.15 = (bf16[2,1024,384]{2,1,0:T(8,128)(2,1)}, bf16[2,1024,384]{2,1,0:T(8,128)(2,1)S(1)}, u32[]{:S(2)}, u32[]{:S(2)}) collective-permute-start(bf16[2,1024,384]{2,1,0:T(8,128)(2,1)} %pad_maximum_fusion.1), channel_id=1, source_target_pairs={{0,8},{8,0},{1,9},{9,1},{2,10},{10,2},{3,11},{11,3},{4,12},{12,4},... | collective-permute-start | bytes 4718600 | tf_op jit(solution)/shard_map/ppermute | solution.py:368
  134.8 2.4 %copy-start.13 = (bf16[1024,384]{1,0:T(8,128)(2,1)}, bf16[1024,384]{1,0:T(8,128)(2,1)S(1)}, u32[]{:S(2)}) copy-start(bf16[1024,384]{1,0:T(8,128)(2,1)S(1)} %collective-permute-done.10.refs_7_) | copy-start | bytes 2359300
  134.8 4.5 %collective-permute-start.16 = (bf16[1024,384]{1,0:T(8,128)(2,1)}, bf16[1024,384]{1,0:T(8,128)(2,1)}, u32[]{:S(2)}, u32[]{:S(2)}) collective-permute-start(bf16[1024,384]{1,0:T(8,128)(2,1)} %collective-permute-done.13.refs_11_), channel_id=1, source_target_pairs={{0,8},{8,0},{1,9},{9,1},{2,10},{10,2},{3,11},{11,3},{4,12},{12,4},... | collective-permute-start | bytes 2359304 | tf_op jit(solution)/shard_map/ppermute | solution.py:368
  136.9 3.6 %collective-permute-start.17 = (bf16[1024,384]{1,0:T(8,128)(2,1)}, bf16[1024,384]{1,0:T(8,128)(2,1)}, u32[]{:S(2)}, u32[]{:S(2)}) collective-permute-start(bf16[1024,384]{1,0:T(8,128)(2,1)} %collective-permute-done.14.refs_15_), channel_id=1, source_target_pairs={{0,8},{8,0},{1,9},{9,1},{2,10},{10,2},{3,11},{11,3},{4,12},{12,4},... | collective-permute-start | bytes 2359304 | tf_op jit(solution)/shard_map/ppermute | solution.py:368
  140.4 1.2 copy-start.6

commit v5 on v4

--- a/solution.py
+++ b/solution.py
@@ -104,12 +104,12 @@
         imag = total[:, NBAND:] * (1.0 / math.sqrt(L))
         amplitude = jnp.sqrt(real * real + imag * imag)
         lane = iota((1, NBAND), 1)
+        padded = jnp.concatenate([amplitude, jnp.zeros((SEGS, 128), F32)], axis=1)
         smooth = amplitude
         for width in range(1, WMAX + 1):
-            up = pltpu.roll(amplitude, width, 1)
-            down = pltpu.roll(amplitude, NBAND - width, 1)
-            both = jnp.where(lane >= width, up, 0.0) + jnp.where(lane < NBAND - width, down, 0.0)
-            smooth += jnp.where(widths >= width, both, 0.0)
+            up = pltpu.roll(padded, width, 1)[:, :NBAND]
+            down = pltpu.roll(padded, NBAND + 128 - width, 1)[:, :NBAND]
+            smooth += jnp.where(widths >= width, up + down, 0.0)
         number = jnp.minimum(lane + widths, NBAND - 1) - jnp.maximum(lane - widths, 0) + 1
         factor = 1.0 / jnp.maximum(smooth / number.astype(F32), FLOOR)
         lanes = iota((SEGS, 128), 1)

time: 160 us -> 160 us (level)
  no operation moved by 1% of the time
where the time goes in v5:
time: 160 us; the launch traced here: 159 us
  waiting for transfers between devices  53 us (33%)
  blocking collectives  43 us (27%)
  Pallas kernels  41 us (26%)
  starting transfers between devices  18.3 us (11%)
  local copies, waits for them, and re-layouts  1.93 us (1%)
  other arithmetic  1.83 us (1%)
    ppermute x18, waiting for transfers between devices, move(): lax.ppermute(lax.optimization_barrier((array,) + others)[0], axis, pairs)  53 us
    all_to_all x1, blocking collectives, on_device(): lax.all_to_all(send, AXES, split_axis=0, concat_axis=0, tiled=True)  43 us
    pallas_call x1, Pallas kernels, transform(): pl.pallas_call(transform_kernel, grid=(STEPS,), in_specs=[pl.BlockSpec((S...  19.2 us
    ppermute x18, starting transfers between devices, move(): lax.ppermute(lax.optimization_barrier((array,) + others)[0], axis, pairs)  18.3 us
    pallas_call x1, Pallas kernels, cross(): pl.pallas_call(cross_kernel, grid=(2 * BLOCKS + 64 // OUT_ROWS,), in_spec...  17.7 us
    pallas_call x1, Pallas kernels, stack(): pl.pallas_call(stack_kernel, out_shape=jax.ShapeDtypeStruct((2 * PAIRS *...  4.07 us
  transfers between devices with their start and end apart: 18, of which 9 were waited for; matrix products, arithmetic and copies ran while one was open for 2% of the time, Pallas kernels for 0%

profile of v5, /device:TPU:1, one launch (start us, length us, event | category | flops | bytes accessed | tf_op | source)
XLA Modules:
  0.0 159.5 jit_solution(12372845043219621125)
XLA Ops:
  0.0 19.2 %transform.1 = bf16[128,72,128]{2,1,0:T(8,128)(2,1)} custom-call(bf16[512,8192]{1,0:T(8,128)(2,1)} %after.1, bf16[512,8192]{1,0:T(8,128)(2,1)} %after.1, bf16[512,8192]{1,0:T(8,128)(2,1)} %after.1, s32[1,512]{1,0:T(1,128)} %bitcast.41, s32[1,512]{1,0:T(1,128)} %bitcast.42, s32[1,1024]{1,0:T(1,128)} %bitcast.40, s32[1,256]{1,0:T(1,128)} %bitcast.43), custom_call_target="tpu_custom_call" | custom-call | flops 21474836480 | bytes 8388608 | tf_op jit(solution)/shard_map/transform/pallas_call | solution.py:147
  19.2 43.0 %all_to_all.5.received = bf16[128,72,128]{2,1,0:T(8,128)(2,1)S(1)} all-to-all(bf16[128,72,128]{2,1,0:T(8,128)(2,1)} %transform.1), channel_id=1, replica_groups=mesh['zh'=2,'y'=4,'core'=2,'x'=4,'zl'=2] {'zh','y','core','x','zl'}, dimensions={0} | all-to-all | bytes 4718592 | tf_op jit(solution)/shard_map/all_to_all | solution.py:409
  62.2 4.1 %stack.133.refs_0_.refs_8_ = bf16[1024,384]{1,0:T(8,128)(2,1)S(1)} custom-call(bf16[128,72,128]{2,1,0:T(8,128)(2,1)S(1)} %all_to_all.5.received), custom_call_target="tpu_custom_call" | custom-call | flops 2147483648 | bytes 3145728 | tf_op jit(solution)/shard_map/stack/pallas_call | solution.py:222
  66.3 0.0 copy-start
  66.3 0.8 collective-permute-start.8
  67.0 2.0 %collective-permute-start.1 = (bf16[1024,384]{1,0:T(8,128)(2,1)S(1)}, bf16[1024,384]{1,0:T(8,128)(2,1)S(1)}, u32[]{:S(2)}, u32[]{:S(2)}) collective-permute-start(bf16[1024,384]{1,0:T(8,128)(2,1)S(1)} %stack.133.refs_0_.refs_8_), channel_id=1, source_target_pairs={{0,48},{16,0},{32,16},{48,32},{1,49},{17,1},{33,17},{49,33},{2,50}... | collective-permute-start | bytes 2359304 | tf_op jit(solution)/shard_map/ppermute | solution.py:368
  69.0 0.0 collective-permute-start
  69.1 1.8 %collective-permute-start.4 = (bf16[1024,384]{1,0:T(8,128)(2,1)S(1)}, bf16[1024,384]{1,0:T(8,128)(2,1)S(1)}, u32[]{:S(2)}, u32[]{:S(2)}) collective-permute-start(bf16[1024,384]{1,0:T(8,128)(2,1)S(1)} %stack.133.refs_0_.refs_8_), channel_id=1, source_target_pairs={{0,6},{2,0},{4,2},{6,4},{1,7},{3,1},{5,3},{7,5},{8,14},{10,8},{12,... | collective-permute-start | bytes 2359304 | tf_op jit(solution)/shard_map/ppermute | solution.py:368
  70.9 0.0 collective-permute-start.3
  70.9 13.7 %collective-permute-done.8.refs_9_ = bf16[1024,384]{1,0:T(8,128)(2,1)S(1)} collective-permute-done((bf16[1024,384]{1,0:T(8,128)(2,1)S(1)}, bf16[1024,384]{1,0:T(8,128)(2,1)S(1)}, u32[]{:S(2)}, u32[]{:S(2)}) %collective-permute-start.8) | collective-permute-done | bytes 786464 | tf_op jit(solution)/shard_map/ppermute | solution.py:368
  84.6 0.0 copy-start.1
  84.6 0.2 collective-permute-done.1.refs_12_
  84.8 0.0 copy-start.2
  84.8 3.1 %collective-permute-done.refs_10_ = bf16[1024,384]{1,0:T(8,128)(2,1)S(1)} collective-permute-done((bf16[1024,384]{1,0:T(8,128)(2,1)S(1)}, bf16[1024,384]{1,0:T(8,128)(2,1)S(1)}, u32[]{:S(2)}, u32[]{:S(2)}) %collective-permute-start) | collective-permute-done | bytes 786464 | tf_op jit(solution)/shard_map/ppermute | solution.py:368
  87.9 0.0 copy-start.3
  87.9 0.5 pad_maximum_fusion
  88.4 0.0 copy-done.2
  88.4 0.0 collective-permute-done.4.refs_4_
  88.4 0.0 copy-start.7
  88.5 1.8 %collective-permute-done.3.refs_2_ = bf16[1024,384]{1,0:T(8,128)(2,1)S(1)} collective-permute-done((bf16[1024,384]{1,0:T(8,128)(2,1)S(1)}, bf16[1024,384]{1,0:T(8,128)(2,1)S(1)}, u32[]{:S(2)}, u32[]{:S(2)}) %collective-permute-start.3) | collective-permute-done | bytes 786464 | tf_op jit(solution)/shard_map/ppermute | solution.py:368
  90.2 0.0 copy-start.8
  90.2 1.8 %collective-permute-start.9 = (bf16[4,1024,384]{2,1,0:T(8,128)(2,1)S(1)}, bf16[4,1024,384]{2,1,0:T(8,128)(2,1)}, u32[]{:S(2)}, u32[]{:S(2)}) collective-permute-start(bf16[4,1024,384]{2,1,0:T(8,128)(2,1)S(1)} %pad_maximum_fusion), channel_id=1, source_target_pairs={{0,8},{8,0},{1,9},{9,1},{2,10},{10,2},{3,11},{11,3},{4,12},{12,4},... | collective-permute-start | bytes 9437192 | tf_op jit(solution)/shard_map/ppermute | solution.py:368
  92.0 0.0 collective-permute-start.5
  92.0 0.0 copy-done
  92.0 0.6 collective-permute-start.2
  92.6 1.7 %collective-permute-start.12 = (bf16[1024,384]{1,0:T(8,128)(2,1)S(1)}, bf16[1024,384]{1,0:T(8,128)(2,1)S(1)}, u32[]{:S(2)}, u32[]{:S(2)}) collective-permute-start(bf16[1024,384]{1,0:T(8,128)(2,1)S(1)} %collective-permute-done.8.refs_9_), channel_id=1, source_target_pairs={{0,48},{16,0},{32,16},{48,32},{1,49},{17,1},{33,17},{49,33},{2,50}... | collective-permute-start | bytes 2359304 | tf_op jit(solution)/shard_map/ppermute | solution.py:368
  94.3 0.0 copy-done.3
  94.3 0.0 collective-permute-start.11
  94.3 18.1 %collective-permute-done.5.refs_6_ = bf16[1024,384]{1,0:T(8,128)(2,1)S(1)} collective-permute-done((bf16[1024,384]{1,0:T(8,128)(2,1)S(1)}, bf16[1024,384]{1,0:T(8,128)(2,1)S(1)}, u32[]{:S(2)}, u32[]{:S(2)}) %collective-permute-start.5) | collective-permute-done | bytes 786464 | tf_op jit(solution)/shard_map/ppermute | solution.py:368
  112.4 0.0 copy-start.9
  112.4 0.0 collective-permute-done.2.refs_1_
  112.4 1.1 collective-permute-start.7
  113.6 0.4 collective-permute-start.6
  114.0 0.0 collective-permute-done.12.refs_13_
  114.0 0.0 collective-permute-done.11.refs_14_
  114.0 0.0 copy-done.1
  114.0 0.4 collective-permute-start.13
  114.4 2.3 %collective-permute-start.14 = (bf16[1024,384]{1,0:T(8,128)(2,1)S(1)}, bf16[1024,384]{1,0:T(8,128)(2,1)}, u32[]{:S(2)}, u32[]{:S(2)}) collective-permute-start(bf16[1024,384]{1,0:T(8,128)(2,1)S(1)} %collective-permute-done.12.refs_13_), channel_id=1, source_target_pairs={{0,48},{16,0},{32,16},{48,32},{1,49},{17,1},{33,17},{49,33},{2,50}... | collective-permute-start | bytes 2359304 | tf_op jit(solution)/shard_map/ppermute | solution.py:368
  116.7 0.0 collective-permute-done.9.refs_16_
  116.7 0.8 collective-permute-start.10
  117.5 1.3 pad_maximum_fusion.1
  118.9 12.0 %collective-permute-done.7.refs_5_ = bf16[1024,384]{1,0:T(8,128)(2,1)S(1)} collective-permute-done((bf16[1024,384]{1,0:T(8,128)(2,1)S(1)}, bf16[1024,384]{1,0:T(8,128)(2,1)S(1)}, u32[]{:S(2)}, u32[]{:S(2)}) %collective-permute-start.7) | collective-permute-done | bytes 786464 | tf_op jit(solution)/shard_map/ppermute | solution.py:368
  130.9 1.7 %collective-permute-done.6.refs_3_ = bf16[1024,384]{1,0:T(8,128)(2,1)S(1)} collective-permute-done((bf16[1024,384]{1,0:T(8,128)(2,1)S(1)}, bf16[1024,384]{1,0:T(8,128)(2,1)S(1)}, u32[]{:S(2)}, u32[]{:S(2)}) %collective-permute-start.6) | collective-permute-done | bytes 786464 | tf_op jit(solution)/shard_map/ppermute | solution.py:368
  132.5 2.2 %collective-permute-start.15 = (bf16[2,1024,384]{2,1,0:T(8,128)(2,1)}, bf16[2,1024,384]{2,1,0:T(8,128)(2,1)S(1)}, u32[]{:S(2)}, u32[]{:S(2)}) collective-permute-start(bf16[2,1024,384]{2,1,0:T(8,128)(2,1)} %pad_maximum_fusion.1), channel_id=1, source_target_pairs={{0,8},{8,0},{1,9},{9,1},{2,10},{10,2},{3,11},{11,3},{4,12},{12,4},... | collective-permute-start | bytes 4718600 | tf_op jit(solution)/shard_map/ppermute | solution.py:368
  134.7 0.0 collective-permute-done.14.refs_15_
  134.7 0.0 collective-permute-done.10.refs_7_
  134.8 0.0 collective-permute-done.13.refs_11_
  134.8 0.0 copy-done.5
  134.8 2.0 %collective-permute-start.16 = (bf16[1024,384]{1,0:T(8,128)(2,1)}, bf16[1024,384]{1,0:T(8,128)(2,1)}, u32[]{:S(2)}, u32[]{:S(2)}) collective-permute-start(bf16[1024,384]{1,0:T(8,128)(2,1)} %collective-permute-done.13.refs_11_), channel_id=1, source_target_pairs={{0,8},{8,0},{1,9},{9,1},{2,10},{10,2},{3,11},{11,3},{4,12},{12,4},... | collective-permute-start | bytes 2359304 | tf_op jit(solution)/shard_map/ppermute | solution.py:368
  136.8 0.0 copy-done.8
  136.8 0.3 collective-permute-start.17
  137.1 0.0 copy-done.9
  137.1 0.0 copy-done.10
  137.1 0.0 copy-done.11
  137.1 0.0 copy-done.12
  137.1 0.0 copy-done.13
  137.2 0.7 stack.124.places
  137.9 1.3 collective-permute-done.16.refs_18_
  139.2 1.1 collective-permute-done.17.refs_19_
  140.4 0.0 collective-permute-done.15.refs_17_
  140.4 0.0 copy-done.7
  140.4 0.0 copy-done.4
  140.4 1.2 copy-done.6
  141.6 17.7 %cross.1 = bf16[64,128,512]{2,1,0:T(8,128)(2,1)} custom-call(s32[24]{0:T(128)} %stack.124.places, bf16[1024,384]{1,0:T(8,128)(2,1)} %copy-done, bf16[1024,384]{1,0:T(8,128)(2,1)} %copy-done.10, bf16[1024,384]{1,0:T(8,128)(2,1)} %copy-done.8, bf16[1024,384]{1,0:T(8,128)(2,1)} %copy-done.12, bf16[1024,384]{1,0:T(8,128)(2,1)} %copy-done.7, ...), custom_call_target="tpu_custom_call" | custom-call | flops 3221225472 | bytes 14680064 | tf_op jit(solution)/shard_map/cross/pallas_call | solution.py:337
  (7 shorter events, 0.0 us)
Async XLA Ops:
  66.3 25.8 %copy-start = (bf16[1024,384]{1,0:T(8,128)(2,1)}, bf16[1024,384]{1,0:T(8,128)(2,1)S(1)}, u32[]{:S(2)}) copy-start(bf16[1024,384]{1,0:T(8,128)(2,1)S(1)} %stack.133.refs_0_.refs_8_) | copy-start | bytes 2359300
  66.3 18.3 %collective-permute-start.8 = (bf16[1024,384]{1,0:T(8,128)(2,1)S(1)}, bf16[1024,384]{1,0:T(8,128)(2,1)S(1)}, u32[]{:S(2)}, u32[]{:S(2)}) collective-permute-start(bf16[1024,384]{1,0:T(8,128)(2,1)S(1)} %stack.133.refs_0_.refs_8_), channel_id=1, source_target_pairs={{0,64},{64,0},{1,65},{65,1},{2,66},{66,2},{3,67},{67,3},{4,68},{68... | collective-permute-start | bytes 2359304 | tf_op jit(solution)/shard_map/ppermute | solution.py:368
  67.0 17.7 %collective-permute-start.1 = (bf16[1024,384]{1,0:T(8,128)(2,1)S(1)}, bf16[1024,384]{1,0:T(8,128)(2,1)S(1)}, u32[]{:S(2)}, u32[]{:S(2)}) collective-permute-start(bf16[1024,384]{1,0:T(8,128)(2,1)S(1)} %stack.133.refs_0_.refs_8_), channel_id=1, source_target_pairs={{0,48},{16,0},{32,16},{48,32},{1,49},{17,1},{33,17},{49,33},{2,50}... | collective-permute-start | bytes 2359304 | tf_op jit(solution)/shard_map/ppermute | solution.py:368
  69.0 18.9 %collective-permute-start = (bf16[1024,384]{1,0:T(8,128)(2,1)S(1)}, bf16[1024,384]{1,0:T(8,128)(2,1)S(1)}, u32[]{:S(2)}, u32[]{:S(2)}) collective-permute-start(bf16[1024,384]{1,0:T(8,128)(2,1)S(1)} %stack.133.refs_0_.refs_8_), channel_id=1, source_target_pairs={{0,16},{16,32},{32,48},{48,0},{1,17},{17,33},{33,49},{49,1},{2,18}... | collective-permute-start | bytes 2359304 | tf_op jit(solution)/shard_map/ppermute | solution.py:368
  69.1 19.4 %collective-permute-start.4 = (bf16[1024,384]{1,0:T(8,128)(2,1)S(1)}, bf16[1024,384]{1,0:T(8,128)(2,1)S(1)}, u32[]{:S(2)}, u32[]{:S(2)}) collective-permute-start(bf16[1024,384]{1,0:T(8,128)(2,1)S(1)} %stack.133.refs_0_.refs_8_), channel_id=1, source_target_pairs={{0,6},{2,0},{4,2},{6,4},{1,7},{3,1},{5,3},{7,5},{8,14},{10,8},{12,... | collective-permute-start | bytes 2359304 | tf_op jit(solution)/shard_map/ppermute | solution.py:368
  70.9 19.4 %collective-permute-start.3 = (bf16[1024,384]{1,0:T(8,128)(2,1)S(1)}, bf16[1024,384]{1,0:T(8,128)(2,1)S(1)}, u32[]{:S(2)}, u32[]{:S(2)}) collective-permute-start(bf16[1024,384]{1,0:T(8,128)(2,1)S(1)} %stack.133.refs_0_.refs_8_), channel_id=1, source_target_pairs={{0,2},{2,4},{4,6},{6,0},{1,3},{3,5},{5,7},{7,1},{8,10},{10,12},{12... | collective-permute-start | bytes 2359304 | tf_op jit(solution)/shard_map/ppermute | solution.py:368
  84.6 29.4 %copy-start.1 = (bf16[1024,384]{1,0:T(8,128)(2,1)}, bf16[1024,384]{1,0:T(8,128)(2,1)S(1)}, u32[]{:S(2)}) copy-start(bf16[1024,384]{1,0:T(8,128)(2,1)S(1)} %collective-permute-done.8.refs_9_) | copy-start | bytes 2359300
  84.8 3.7 %copy-start.2 = (bf16[1024,384]{1,0:T(8,128)(2,1)}, bf16[1024,384]{1,0:T(8,128)(2,1)S(1)}, u32[]{:S(2)}) copy-start(bf16[1024,384]{1,0:T(8,128)(2,1)S(1)} %collective-permute-done.1.refs_12_) | copy-start | bytes 2359300
  87.9 6.4 %copy-start.3 = (bf16[1024,384]{1,0:T(8,128)(2,1)}, bf16[1024,384]{1,0:T(8,128)(2,1)S(1)}, u32[]{:S(2)}) copy-start(bf16[1024,384]{1,0:T(8,128)(2,1)S(1)} %collective-permute-done.refs_10_) | copy-start | bytes 2359300
  88.4 51.9 %copy-start.7 = (bf16[1024,384]{1,0:T(8,128)(2,1)}, bf16[1024,384]{1,0:T(8,128)(2,1)S(1)}, u32[]{:S(2)}) copy-start(bf16[1024,384]{1,0:T(8,128)(2,1)S(1)} %collective-permute-done.4.refs_4_) | copy-start | bytes 2359300
  90.2 46.6 %copy-start.8 = (bf16[1024,384]{1,0:T(8,128)(2,1)}, bf16[1024,384]{1,0:T(8,128)(2,1)S(1)}, u32[]{:S(2)}) copy-start(bf16[1024,384]{1,0:T(8,128)(2,1)S(1)} %collective-permute-done.3.refs_2_) | copy-start | bytes 2359300
  90.2 26.5 %collective-permute-start.9 = (bf16[4,1024,384]{2,1,0:T(8,128)(2,1)S(1)}, bf16[4,1024,384]{2,1,0:T(8,128)(2,1)}, u32[]{:S(2)}, u32[]{:S(2)}) collective-permute-start(bf16[4,1024,384]{2,1,0:T(8,128)(2,1)S(1)} %pad_maximum_fusion), channel_id=1, source_target_pairs={{0,8},{8,0},{1,9},{9,1},{2,10},{10,2},{3,11},{11,3},{4,12},{12,4},... | collective-permute-start | bytes 9437192 | tf_op jit(solution)/shard_map/ppermute | solution.py:368
  92.0 20.4 %collective-permute-start.5 = (bf16[1024,384]{1,0:T(8,128)(2,1)S(1)}, bf16[1024,384]{1,0:T(8,128)(2,1)S(1)}, u32[]{:S(2)}, u32[]{:S(2)}) collective-permute-start(bf16[1024,384]{1,0:T(8,128)(2,1)S(1)} %collective-permute-done.3.refs_2_), channel_id=1, source_target_pairs={{0,2},{2,4},{4,6},{6,0},{1,3},{3,5},{5,7},{7,1},{8,10},{10,12},{12... | collective-permute-start | bytes 2359304 | tf_op jit(solution)/shard_map/ppermute | solution.py:368
  92.0 20.4 %collective-permute-start.2 = (bf16[1024,384]{1,0:T(8,128)(2,1)S(1)}, bf16[1024,384]{1,0:T(8,128)(2,1)S(1)}, u32[]{:S(2)}, u32[]{:S(2)}) collective-permute-start(bf16[1024,384]{1,0:T(8,128)(2,1)S(1)} %stack.133.refs_0_.refs_8_), channel_id=1, source_target_pairs={{0,1},{1,0},{2,3},{3,2},{4,5},{5,4},{6,7},{7,6},{8,9},{9,8},{10,11... | collective-permute-start | bytes 2359304 | tf_op jit(solution)/shard_map/ppermute | solution.py:368
  92.6 21.4 %collective-permute-start.12 = (bf16[1024,384]{1,0:T(8,128)(2,1)S(1)}, bf16[1024,384]{1,0:T(8,128)(2,1)S(1)}, u32[]{:S(2)}, u32[]{:S(2)}) collective-permute-start(bf16[1024,384]{1,0:T(8,128)(2,1)S(1)} %collective-permute-done.8.refs_9_), channel_id=1, source_target_pairs={{0,48},{16,0},{32,16},{48,32},{1,49},{17,1},{33,17},{49,33},{2,50}... | collective-permute-start | bytes 2359304 | tf_op jit(solution)/shard_map/ppermute | solution.py:368
  94.3 19.7 %collective-permute-start.11 = (bf16[1024,384]{1,0:T(8,128)(2,1)S(1)}, bf16[1024,384]{1,0:T(8,128)(2,1)S(1)}, u32[]{:S(2)}, u32[]{:S(2)}) collective-permute-start(bf16[1024,384]{1,0:T(8,128)(2,1)S(1)} %collective-permute-done.refs_10_), channel_id=1, source_target_pairs={{0,16},{16,32},{32,48},{48,0},{1,17},{17,33},{33,49},{49,1},{2,18}... | collective-permute-start | bytes 2359304 | tf_op jit(solution)/shard_map/ppermute | solution.py:368
  112.4 24.7 %copy-start.9 = (bf16[1024,384]{1,0:T(8,128)(2,1)}, bf16[1024,384]{1,0:T(8,128)(2,1)S(1)}, u32[]{:S(2)}) copy-start(bf16[1024,384]{1,0:T(8,128)(2,1)S(1)} %collective-permute-done.5.refs_6_) | copy-start | bytes 2359300
  112.4 24.7 %copy-start.10 = (bf16[1024,384]{1,0:T(8,128)(2,1)}, bf16[1024,384]{1,0:T(8,128)(2,1)S(1)}, u32[]{:S(2)}) copy-start(bf16[1024,384]{1,0:T(8,128)(2,1)S(1)} %collective-permute-done.2.refs_1_) | copy-start | bytes 2359300
  112.4 18.5 %collective-permute-start.7 = (bf16[1024,384]{1,0:T(8,128)(2,1)S(1)}, bf16[1024,384]{1,0:T(8,128)(2,1)S(1)}, u32[]{:S(2)}, u32[]{:S(2)}) collective-permute-start(bf16[1024,384]{1,0:T(8,128)(2,1)S(1)} %collective-permute-done.2.refs_1_), channel_id=1, source_target_pairs={{0,6},{2,0},{4,2},{6,4},{1,7},{3,1},{5,3},{7,5},{8,14},{10,8},{12,... | collective-permute-start | bytes 2359304 | tf_op jit(solution)/shard_map/ppermute | solution.py:368
  113.6 19.0 %collective-permute-start.6 = (bf16[1024,384]{1,0:T(8,128)(2,1)S(1)}, bf16[1024,384]{1,0:T(8,128)(2,1)S(1)}, u32[]{:S(2)}, u32[]{:S(2)}) collective-permute-start(bf16[1024,384]{1,0:T(8,128)(2,1)S(1)} %collective-permute-done.2.refs_1_), channel_id=1, source_target_pairs={{0,2},{2,4},{4,6},{6,0},{1,3},{3,5},{5,7},{7,1},{8,10},{10,12},{12... | collective-permute-start | bytes 2359304 | tf_op jit(solution)/shard_map/ppermute | solution.py:368
  114.0 26.4 %copy-start.4 = (bf16[1024,384]{1,0:T(8,128)(2,1)}, bf16[1024,384]{1,0:T(8,128)(2,1)S(1)}, u32[]{:S(2)}) copy-start(bf16[1024,384]{1,0:T(8,128)(2,1)S(1)} %collective-permute-done.12.refs_13_) | copy-start | bytes 2359300
  114.0 20.8 %copy-start.5 = (bf16[1024,384]{1,0:T(8,128)(2,1)}, bf16[1024,384]{1,0:T(8,128)(2,1)S(1)}, u32[]{:S(2)}) copy-start(bf16[1024,384]{1,0:T(8,128)(2,1)S(1)} %collective-permute-done.11.refs_14_) | copy-start | bytes 2359300
  114.0 20.8 %collective-permute-start.13 = (bf16[1024,384]{1,0:T(8,128)(2,1)S(1)}, bf16[1024,384]{1,0:T(8,128)(2,1)}, u32[]{:S(2)}, u32[]{:S(2)}) collective-permute-start(bf16[1024,384]{1,0:T(8,128)(2,1)S(1)} %collective-permute-done.8.refs_9_), channel_id=1, source_target_pairs={{0,16},{16,32},{32,48},{48,0},{1,17},{17,33},{33,49},{49,1},{2,18}... | collective-permute-start | bytes 2359304 | tf_op jit(solution)/shard_map/ppermute | solution.py:368
  114.4 20.3 %collective-permute-start.14 = (bf16[1024,384]{1,0:T(8,128)(2,1)S(1)}, bf16[1024,384]{1,0:T(8,128)(2,1)}, u32[]{:S(2)}, u32[]{:S(2)}) collective-permute-start(bf16[1024,384]{1,0:T(8,128)(2,1)S(1)} %collective-permute-done.12.refs_13_), channel_id=1, source_target_pairs={{0,48},{16,0},{32,16},{48,32},{1,49},{17,1},{33,17},{49,33},{2,50}... | collective-permute-start | bytes 2359304 | tf_op jit(solution)/shard_map/ppermute | solution.py:368
  116.7 18.0 %collective-permute-start.10 = (bf16[1024,384]{1,0:T(8,128)(2,1)S(1)}, bf16[1024,384]{1,0:T(8,128)(2,1)S(1)}, u32[]{:S(2)}, u32[]{:S(2)}) collective-permute-start(bf16[1024,384]{1,0:T(8,128)(2,1)S(1)} %collective-permute-done.5.refs_6_), channel_id=1, source_target_pairs={{0,1},{1,0},{2,3},{3,2},{4,5},{5,4},{6,7},{7,6},{8,9},{9,8},{10,11... | collective-permute-start | bytes 2359304 | tf_op jit(solution)/shard_map/ppermute | solution.py:368
  130.9 6.2 %copy-start.11 = (bf16[1024,384]{1,0:T(8,128)(2,1)}, bf16[1024,384]{1,0:T(8,128)(2,1)S(1)}, u32[]{:S(2)}) copy-start(bf16[1024,384]{1,0:T(8,128)(2,1)S(1)} %collective-permute-done.7.refs_5_) | copy-start | bytes 2359300
  132.5 4.6 %copy-start.12 = (bf16[1024,384]{1,0:T(8,128)(2,1)}, bf16[1024,384]{1,0:T(8,128)(2,1)S(1)}, u32[]{:S(2)}) copy-start(bf16[1024,384]{1,0:T(8,128)(2,1)S(1)} %collective-permute-done.6.refs_3_) | copy-start | bytes 2359300
  132.5 7.8 %collective-permute-start.15 = (bf16[2,1024,384]{2,1,0:T(8,128)(2,1)}, bf16[2,1024,384]{2,1,0:T(8,128)(2,1)S(1)}, u32[]{:S(2)}, u32[]{:S(2)}) collective-permute-start(bf16[2,1024,384]{2,1,0:T(8,128)(2,1)} %pad_maximum_fusion.1), channel_id=1, source_target_pairs={{0,8},{8,0},{1,9},{9,1},{2,10},{10,2},{3,11},{11,3},{4,12},{12,4},... | collective-permute-start | bytes 4718600 | tf_op jit(solution)/shard_map/ppermute | solution.py:368
  134.7 2.4 %copy-start.13 = (bf16[1024,384]{1,0:T(8,128)(2,1)}, bf16[1024,384]{1,0:T(8,128)(2,1)S(1)}, u32[]{:S(2)}) copy-start(bf16[1024,384]{1,0:T(8,128)(2,1)S(1)} %collective-permute-done.10.refs_7_) | copy-start | bytes 2359300
  134.8 4.5 %collective-permute-start.16 = (bf16[1024,384]{1,0:T(8,128)(2,1)}, bf16[1024,384]{1,0:T(8,128)(2,1)}, u32[]{:S(2)}, u32[]{:S(2)}) collective-permute-start(bf16[1024,384]{1,0:T(8,128)(2,1)} %collective-permute-done.13.refs_11_), channel_id=1, source_target_pairs={{0,8},{8,0},{1,9},{9,1},{2,10},{10,2},{3,11},{11,3},{4,12},{12,4},... | collective-permute-start | bytes 2359304 | tf_op jit(solution)/shard_map/ppermute | solution.py:368
  136.8 3.6 %collective-permute-start.17 = (bf16[1024,384]{1,0:T(8,128)(2,1)}, bf16[1024,384]{1,0:T(8,128)(2,1)}, u32[]{:S(2)}, u32[]{:S(2)}) collective-permute-start(bf16[1024,384]{1,0:T(8,128)(2,1)} %collective-permute-done.14.refs_15_), channel_id=1, source_target_pairs={{0,8},{8,0},{1,9},{9,1},{2,10},{10,2},{3,11},{11,3},{4,12},{12,4},... | collective-permute-start | bytes 2359304 | tf_op jit(solution)/shard_map/ppermute | solution.py:368
  140.4 1.2 copy-start.6
